TPU v7x, 128 devices: a whole 4x4x4 slice. The times are simulated.
128 devices in a mesh: row: 8 (over y, x_lo), col: 16 (over x_hi, z, core).
Axes of the slice: x: 4 (x_hi: 2, x_lo: 2; x = x_hi * 2 + x_lo), y: 4, z: 4, core: 2. Of those that a mesh axis runs over, the one named last changes fastest.
Arguments:
- segments: float32 [49152, 512], P(('row', 'col')), may hold values from -60 to 60
- exclusion: int32 [1], replicated, may hold values from 1 to 12
Outputs:
- profile: float32 [2, 49152], P(None, ('row', 'col'))
All inputs are finite; a program needn't handle non-finite values.
Results may differ from a plain program's by a relative error of at most 0.0005.
Values may be sent and summed in bfloat16 or wider, within the bound.
No kernel may reach another device: no remote copies, remote signals or barrier semaphores. Data moves between devices by JAX's collectives and lax.ppermute only.
A program may use at most 192 MiB of HBM per device.

v0:
```python
import math

import jax
import jax.numpy as jnp
from jax import lax
from jax.sharding import PartitionSpec as P


def statistics(segments):
    seg_len = segments.shape[1]
    average = jnp.mean(segments, axis=1)
    centered = segments - average[:, None]
    spread_inv = lax.rsqrt(jnp.mean(centered * centered, axis=1) + 1e-05) * (
        1.0 / math.sqrt(seg_len)
    )
    return (average, spread_inv)


def normalize(samples, average, spread_inv):
    return ((samples - average[:, None]) * spread_inv[:, None]).astype(jnp.bfloat16)


def tile_minima(row_data, row_pos, upper_rows, lower_rows, col_data, col_pos, exclude):
    products = lax.dot_general(
        row_data, col_data, (((1,), (1,)), ((), ())), preferred_element_type=jnp.float32
    )
    apart = 1.0 - products
    offset_by = col_pos[None, :] - row_pos[:, None]
    upper_mask = (offset_by > exclude) & upper_rows[:, None]
    lower_mask = (offset_by < -exclude) & lower_rows[:, None]
    upper_dist = jnp.where(upper_mask, apart, 4.0)
    lower_dist = jnp.where(lower_mask, apart, 4.0)
    row_part = jnp.stack([jnp.min(lower_dist, axis=1), jnp.min(upper_dist, axis=1)])
    col_part = jnp.stack([jnp.min(upper_dist, axis=0), jnp.min(lower_dist, axis=0)])
    return (row_part, col_part)


def shards(segments, exclusion):
    seg_rows = segments.shape[0]
    n_row = lax.axis_size("row")
    n_col = lax.axis_size("col")
    my_row = lax.axis_index("row")
    my_col = lax.axis_index("col")
    exclude = exclusion[0]
    average, spread_inv = statistics(segments)
    col_index = jnp.arange(n_row * seg_rows, dtype=jnp.int32)
    col_pos = (col_index // seg_rows * n_col + my_col) * seg_rows + col_index % seg_rows
    initial = (
        jnp.full((2, n_col * seg_rows), 4.0, jnp.float32),
        jnp.full((2, n_row * seg_rows), 4.0, jnp.float32),
    )
    col_raw, col_average, col_spread = (
        lax.all_gather(segments, "row", axis=0, tiled=True),
        lax.all_gather(average, "row", axis=0, tiled=True),
        lax.all_gather(spread_inv, "row", axis=0, tiled=True),
    )
    columns = normalize(col_raw, col_average, col_spread)
    totals = initial
    normed_rows = normalize(
        lax.all_gather(segments, "col", axis=0, tiled=True),
        lax.all_gather(average, "col", axis=0, tiled=True),
        lax.all_gather(spread_inv, "col", axis=0, tiled=True),
    )
    offset = jnp.int32(0)
    count = normed_rows.shape[0]
    for step_idx in range(count // seg_rows):
        row_data = normed_rows[step_idx * seg_rows : (step_idx + 1) * seg_rows]
        visit_offset = offset + step_idx * seg_rows
        visit_row_min, visit_col_min = totals
        visit_count = row_data.shape[0]
        panel_idx = visit_offset + jnp.arange(visit_count, dtype=jnp.int32)
        row_pos = my_row * n_col * seg_rows + panel_idx
        part_row, part_col = tile_minima(
            row_data, row_pos, row_pos >= 0, row_pos < 0, columns, col_pos, exclude
        )
        visit_col_min = jnp.minimum(visit_col_min, part_col)
        previous = lax.dynamic_slice_in_dim(visit_row_min, visit_offset, visit_count, 1)
        visit_row_min = lax.dynamic_update_slice_in_dim(
            visit_row_min, jnp.minimum(previous, part_row), visit_offset, 1
        )
        totals = (visit_row_min, visit_col_min)
    row_min, col_min = totals
    from_rows = lax.all_to_all(
        row_min.reshape(2, n_col, seg_rows), "col", split_axis=1, concat_axis=1, tiled=True
    )
    from_cols = lax.all_to_all(
        col_min.reshape(2, n_row, seg_rows), "row", split_axis=1, concat_axis=1, tiled=True
    )
    return jnp.minimum(jnp.min(from_rows, axis=1), jnp.min(from_cols, axis=1))


def solution(mesh):
    return jax.shard_map(
        shards,
        mesh=mesh,
        in_specs=(P(("row", "col"), None), P()),
        out_specs=P(None, ("row", "col")),
        check_vma=False,
    )
```

profile of v0, /device:TPU:1, one launch (start us, length us, event | category | flops | bytes accessed | tf_op | source)
XLA Modules:
  0.0 377.7 jit_solution(11968121700011622800)
XLA Ops:
  11.4 21.2 %all-gather.3 = f32[8,1,384]{2,1,0:T(1,128)S(1)} all-gather(f32[1,1,384]{2,1,0:T(1,128)S(1)} %reshape.274), channel_id=1, replica_groups=mesh['row'=8,'col'=16] {'row'}, dimensions={0}, use_global_device_ids=true | all-gather | bytes 13824 | tf_op jit(solution)/shard_map/all_gather | solution.py:55
  32.6 20.9 %all-gather.2 = f32[8,1,384]{2,1,0:T(1,128)S(1)} all-gather(f32[1,1,384]{2,1,0:T(1,128)S(1)} %reshape.272), channel_id=1, replica_groups=mesh['row'=8,'col'=16] {'row'}, dimensions={0}, use_global_device_ids=true | all-gather | bytes 13824 | tf_op jit(solution)/shard_map/all_gather | solution.py:54
  53.5 34.0 %all-gather.1 = f32[16,1,384]{2,1,0:T(1,128)S(1)} all-gather(f32[1,1,384]{2,1,0:T(1,128)S(1)} %reshape.274), channel_id=1, replica_groups=mesh['row'=8,'col'=16] {'col'}, dimensions={0}, use_global_device_ids=true | all-gather | bytes 26112 | tf_op jit(solution)/shard_map/all_gather | solution.py:62
  87.5 19.3 %all-gather = f32[16,1,384]{2,1,0:T(1,128)S(1)} all-gather(f32[1,1,384]{2,1,0:T(1,128)S(1)} %reshape.272), channel_id=1, replica_groups=mesh['row'=8,'col'=16] {'col'}, dimensions={0}, use_global_device_ids=true | all-gather | bytes 26112 | tf_op jit(solution)/shard_map/all_gather | solution.py:61
  107.2 34.8 %all-gather.9.cloned.1.call-done = f32[3072,512]{1,0:T(8,128)} async-done(((f32[384,512]{1,0:T(8,128)}), f32[3072,512]{1,0:T(8,128)}) %all-gather.9.cloned.1.call-update) | async-done | bytes 6291472 | tf_op jit(solution)/shard_map/all_gather | solution.py:53
  142.0 3.7 multiply_convert_fusion.1
  145.6 90.9 %all-gather.7.cloned.1.call-done = f32[6144,512]{1,0:T(8,128)} async-done(((f32[384,512]{1,0:T(8,128)}), f32[6144,512]{1,0:T(8,128)}) %all-gather.7.cloned.1.call-update) | async-done | bytes 12582928 | tf_op jit(solution)/shard_map/all_gather | solution.py:60
  236.5 6.0 %multiply_convert_fusion = bf16[6144,512]{1,0:T(8,128)(2,1)S(1)} fusion(f32[6144,512]{1,0:T(8,128)} %all-gather.7.cloned.1.call-done, f32[6144]{0:T(1024)S(1)} %bitcast.59, f32[6144]{0:T(1024)S(1)} %bitcast.60), kind=kLoop, calls=%fused_computation | loop fusion | flops 9437184 | bytes 18923520 | tf_op jit(solution)/shard_map/convert_element_type | solution.py:20
  242.5 3.7 convolution_subtract_fusion.10
  246.2 3.7 convolution_subtract_fusion.11
  249.9 3.7 convolution_subtract_fusion.9
  253.6 3.7 convolution_subtract_fusion.6
  257.3 3.6 convolution_subtract_fusion.7
  260.9 3.6 convolution_subtract_fusion.8
  266.1 3.6 convolution_subtract_fusion.4
  269.7 3.7 convolution_subtract_fusion.5
  276.3 1.7 convolution_subtract_fusion.2
  278.1 14.6 %fusion.112 = (f32[3072]{0:T(1024)S(1)}, f32[384]{0:T(512)S(1)}, f32[384]{0:T(512)S(1)}, f32[3072]{0:T(1024)S(1)}, f32[3072]{0:T(1024)S(1)}, /*index=5*/f32[384]...) fusion(s32[384]{0:T(512)S(1)} %get-tuple-element.161, ...), kind=kOutput, calls=%fused_computation.162 | convolution fusion | flops 1261016064 | bytes 17829896 | tf_op jit(solution)/shard_map/dot_general | solution.py:24
  292.7 14.6 %fusion.116 = (f32[3072]{0:T(1024)S(1)}, f32[384]{0:T(512)S(1)}, f32[384]{0:T(512)S(1)}, f32[3072]{0:T(1024)S(1)}, f32[3072]{0:T(1024)S(1)}, /*index=5*/f32[384]...) fusion(s32[384]{0:T(512)S(1)} %get-tuple-element.162, ...), kind=kOutput, calls=%fused_computation.166 | convolution fusion | flops 1261016064 | bytes 17829896 | tf_op jit(solution)/shard_map/dot_general | solution.py:24
  307.3 14.4 %fusion.120 = (f32[3072]{0:T(1024)S(1)}, f32[384]{0:T(512)S(1)}, f32[384]{0:T(512)S(1)}, f32[3072]{0:T(1024)S(1)}, f32[3072]{0:T(1024)S(1)}, /*index=5*/f32[384]...) fusion(s32[384]{0:T(512)S(1)} %get-tuple-element.163, ...), kind=kOutput, calls=%fused_computation.170 | convolution fusion | flops 1261016064 | bytes 17829896 | tf_op jit(solution)/shard_map/dot_general | solution.py:24
  321.7 12.3 %fusion.124 = (f32[3072]{0:T(1024)S(1)}, f32[384]{0:T(512)S(1)}, f32[384]{0:T(512)S(1)}, f32[3072]{0:T(1024)S(1)}, f32[3072]{0:T(1024)S(1)}, /*index=5*/f32[384]...) fusion(s32[]{:T(128)} %bitcast.56, ...), kind=kOutput, calls=%fused_computation.174 | convolution fusion | flops 1261016064 | bytes 17829896 | tf_op jit(solution)/shard_map/dot_general | solution.py:24
  334.9 4.0 %all-to-all-start.1 = ((f32[2,8,384]{2,0,1:T(2,128)}), f32[2,8,384]{2,0,1:T(2,128)S(1)}, u32[]{:S(2)}, u32[]{:S(2)}) async-start(f32[2,8,384]{2,0,1:T(2,128)} %fusion.156), calls=%async_computation.1 | async-start | bytes 49152 | tf_op jit(solution)/shard_map/all_to_all | solution.py:86
  358.3 4.7 %all-to-all-start = ((f32[2,16,384]{2,0,1:T(2,128)}), f32[2,16,384]{2,0,1:T(2,128)S(1)}, u32[]{:S(2)}, u32[]{:S(2)}) async-start(f32[2,16,384]{2,0,1:T(2,128)} %bitcast.5), calls=%async_computation | async-start | bytes 98304 | tf_op jit(solution)/shard_map/all_to_all | solution.py:83
  363.0 7.3 %all-to-all-done = f32[2,16,384]{2,0,1:T(2,128)S(1)} async-done(((f32[2,16,384]{2,0,1:T(2,128)}), f32[2,16,384]{2,0,1:T(2,128)S(1)}, u32[]{:S(2)}, u32[]{:S(2)}) %all-to-all-start) | async-done | bytes 49184 | tf_op jit(solution)/shard_map/all_to_all | solution.py:83
  (92 shorter events, 29.5 us)
Async XLA Ops:
  6.5 135.4 %all-gather.9.cloned.1.call-start = ((), (), s32[]{:S(2)}) async-start(), calls=%async_computation.3 | async-start | bytes 7077888 | tf_op jit(solution)/shard_map/all_gather | solution.py:53
  7.3 229.3 %all-gather.7.cloned.1.call-start = ((), (), s32[]{:S(2)}) async-start(), calls=%async_computation.2 | async-start | bytes 13369344 | tf_op jit(solution)/shard_map/all_gather | solution.py:60
  334.9 23.4 %all-to-all-start.1 = ((f32[2,8,384]{2,0,1:T(2,128)}), f32[2,8,384]{2,0,1:T(2,128)S(1)}, u32[]{:S(2)}, u32[]{:S(2)}) async-start(f32[2,8,384]{2,0,1:T(2,128)} %fusion.156), calls=%async_computation.1 | async-start | bytes 49152 | tf_op jit(solution)/shard_map/all_to_all | solution.py:86
  358.3 12.0 %all-to-all-start = ((f32[2,16,384]{2,0,1:T(2,128)}), f32[2,16,384]{2,0,1:T(2,128)S(1)}, u32[]{:S(2)}, u32[]{:S(2)}) async-start(f32[2,16,384]{2,0,1:T(2,128)} %bitcast.5), calls=%async_computation | async-start | bytes 98304 | tf_op jit(solution)/shard_map/all_to_all | solution.py:83
Sparse Core Ops, SparseCore 0:
  9.0 132.9 all-gather.8
  144.4 92.0 all-gather.6
where the time goes:
time: 379 us; the launch traced here: 378 us
  waiting for transfers between devices  134 us (35%)
  blocking collectives  95.5 us (25%)
  matrix products  91.4 us (24%)
  other arithmetic  32.5 us (9%)
  between operations  14.5 us (4%)
  starting transfers between devices  8.72 us (2%)
    dot_general x16, matrix products, tile_minima(): lax.dot_general(row_data, col_data, (((1,), (1,)), ((), ())), preferred_e...  91.4 us
    all_gather x1, waiting for transfers between devices, shards(): lax.all_gather(segments, 'col', axis=0, tiled=True)  90.9 us
    all_gather x1, waiting for transfers between devices, shards(): lax.all_gather(segments, 'row', axis=0, tiled=True)  34.8 us
    all_gather x1, blocking collectives, shards(): lax.all_gather(spread_inv, 'col', axis=0, tiled=True)  34 us
    all_gather x1, blocking collectives, shards(): lax.all_gather(spread_inv, 'row', axis=0, tiled=True)  21.2 us
    all_gather x1, blocking collectives, shards(): lax.all_gather(average, 'row', axis=0, tiled=True)  20.9 us
    all_gather x1, blocking collectives, shards(): lax.all_gather(average, 'col', axis=0, tiled=True)  19.3 us
    dynamic_update_slice x15, other arithmetic, shards(): lax.dynamic_update_slice_in_dim(visit_row_min, jnp.minimum(previous, part...  18.3 us
  transfers between devices with their start and end apart: 4, of which 3 were waited for; matrix products, arithmetic and copies ran while one was open for 7% of the time, Pallas kernels for 0%

commit v1 on v0

v1 whole, which is shorter than its diff:
```python
import functools
import math

import jax
import jax.numpy as jnp
import numpy as np
from jax import lax
from jax.experimental import pallas as pl
from jax.experimental.pallas import tpu as pltpu
from jax.sharding import PartitionSpec as P

AXES = ("row", "col")
SIDE = 4
OFFSETS = (
    ((3, 3, 0), (0, 1, 0)),
    ((1, 0, 3), (0, 0, 1)),
    ((0, 0, 3), (1, 1, 0)),
    ((3, 3, 3), (0, 2, 1)),
    ((2, 0, 3), (0, 3, 1)),
)
SOURCES = (None, None, None, 0, 1)
SLOTS = ((0, 0, 0),) + tuple(off for pair in OFFSETS for off in pair)
LOW = -3.0


def coords(device):
    row, col = divmod(device, 16)
    y, x_lo = divmod(row, 2)
    return (col // 8 * 2 + x_lo, y, col // 2 % SIDE, col % 2)


def device_at(x, y, z, core):
    x, y, z = x % SIDE, y % SIDE, z % SIDE
    return (y * 2 + x % 2) * 16 + x // 2 * 8 + z * 2 + core


def minus(a, b):
    return tuple((p - q) % SIDE for p, q in zip(a, b))


def moves(hops):
    out = []
    for target in range(128):
        x, y, z, core = coords(target)
        dx, dy, dz = hops[core]
        out.append((device_at(x + dx, y + dy, z + dz, core), target))
    return out


def across():
    return [(device, device ^ 1) for device in range(128)]


def pair_lists():
    chosen = {}
    for t in range(len(SLOTS)):
        for s in range(t):
            diff = minus(SLOTS[t], SLOTS[s])
            key = min(diff, minus((0, 0, 0), diff))
            if key not in chosen:
                chosen[key] = (s, t)
    assert len(chosen) == 35
    full, half = [], []
    for key, pair in chosen.items():
        (half if key == minus((0, 0, 0), key) else full).append(pair)
    return full, half


def normalize_kernel(x_ref, o_ref):
    x = x_ref[...]
    length = x.shape[1]
    average = jnp.sum(x, axis=1, keepdims=True) * (1.0 / length)
    centered = x - average
    power = jnp.sum(centered * centered, axis=1, keepdims=True) * (1.0 / length)
    spread_inv = lax.rsqrt(power + 1e-05) * (1.0 / math.sqrt(length))
    o_ref[...] = (centered * spread_inv).astype(jnp.bfloat16)


def phase_kernel(n_moved, groups, diag, has_prev, rows, *refs):
    meta, table = refs[:2]
    blocks = refs[2 : 3 + 2 * n_moved]
    rest = refs[3 + 2 * n_moved :]
    prev = rest[0] if has_prev else None
    rest = rest[1:] if has_prev else rest
    out, data, row_acc, col_acc, sems = rest
    core = meta[0]
    exclude = meta[1]

    def copies(index):
        if index == 0:
            slot, first = 0, core
        else:
            first = core if index % 2 else 1 - core
            slot = 1 + (index - 1) // 2 * 2 + first
        base = slot * 2 * rows
        near = pl.multiple_of(base + first * rows, rows)
        far = pl.multiple_of(base + (1 - first) * rows, rows)
        return (
            pltpu.make_async_copy(
                blocks[index].at[pl.ds(0, rows)], data.at[pl.ds(near, rows)], sems.at[index, 0]
            ),
            pltpu.make_async_copy(
                blocks[index].at[pl.ds(rows, rows)], data.at[pl.ds(far, rows)], sems.at[index, 1]
            ),
        )

    for index in range(len(blocks)):
        for copy in copies(index):
            copy.start()

    row_acc[...] = jnp.full(row_acc.shape, LOW, jnp.float32)
    col_acc[...] = jnp.full(col_acc.shape, LOW, jnp.float32)

    def product(a, start, width):
        b = data[pl.ds(pl.multiple_of(start, 128), width), :]
        return lax.dot_general(
            a, b, (((1,), (1,)), ((), ())), preferred_element_type=jnp.float32
        )

    def row_max(values):
        best = values[:, :128]
        for at in range(128, values.shape[1], 128):
            best = jnp.maximum(best, values[:, at : at + 128])
        return best

    def col_max(values):
        return jnp.max(values.reshape(rows // 8, 8, values.shape[1]), axis=0)

    def row_block(slot):
        return data[pl.ds(pl.multiple_of((2 * slot + core) * rows, rows), rows), :]

    def visit(index, carry):
        s = table[2 * index]
        t = table[2 * index + 1]
        order_s = meta[2 + s]
        order_t = meta[2 + t]
        later = (order_t > order_s).astype(jnp.int32)
        row_at = 2 * s + later
        col_at = 2 * t + 1 - later
        near = jnp.abs(order_t - order_s) == 1

        def run(masked):
            a = row_block(s)
            best = row_acc[row_at]
            for part in range(2 * rows // 256):
                values = product(a, 2 * t * rows + part * 256, 256)
                if masked:
                    first = (order_t - order_s) * 2 * rows + part * 256 - core * rows
                    offset = (
                        lax.broadcasted_iota(jnp.int32, values.shape, 1)
                        - lax.broadcasted_iota(jnp.int32, values.shape, 0)
                        + first
                    )
                    values = jnp.where(jnp.abs(offset) > exclude, values, LOW)
                best = jnp.maximum(best, row_max(values))
                at = pl.ds(part * 256, 256)
                col_acc[col_at, :, at] = jnp.maximum(col_acc[col_at, :, at], col_max(values))
            row_acc[row_at] = best

        pl.when(near)(functools.partial(run, True))
        pl.when(jnp.logical_not(near))(functools.partial(run, False))
        return carry

    def visit_half(index, carry):
        s = table[2 * index]
        t = table[2 * index + 1]
        later = (meta[2 + t] > meta[2 + s]).astype(jnp.int32)
        row_at = 2 * s + later
        col_at = 2 * t + 1 - later
        half = jnp.where(later == 1, core, 1 - core)
        values = product(row_block(s), (2 * t + half) * rows, rows)
        row_acc[row_at] = jnp.maximum(row_acc[row_at], row_max(values))
        at = pl.ds(pl.multiple_of(half * rows, rows), rows)
        col_acc[col_at, :, at] = jnp.maximum(col_acc[col_at, :, at], col_max(values))
        return carry

    for indices, full_range, half_range in groups:
        for index in indices:
            for copy in copies(index):
                copy.wait()
        if diag and 0 in indices:
            a = row_block(0)
            for part in range(2 * rows // 256):
                values = product(a, part * 256, 256)
                offset = (
                    lax.broadcasted_iota(jnp.int32, values.shape, 1)
                    - lax.broadcasted_iota(jnp.int32, values.shape, 0)
                    + (part * 256 - core * rows)
                )
                earlier = jnp.where(offset < -exclude, values, LOW)
                later = jnp.where(offset > exclude, values, LOW)
                row_acc[0] = jnp.maximum(row_acc[0], row_max(earlier))
                row_acc[1] = jnp.maximum(row_acc[1], row_max(later))
        if full_range[1] > full_range[0]:
            lax.fori_loop(full_range[0], full_range[1], visit, 0)
        if half_range[1] > half_range[0]:
            lax.fori_loop(half_range[0], half_range[1], visit_half, 0)

    lanes = lax.broadcasted_iota(jnp.int32, (rows, 128), 1)
    gathered = jnp.full((rows, 128), LOW, jnp.float32)
    for at in range(row_acc.shape[0]):
        gathered = jnp.where(
            lanes == at, jnp.max(row_acc[at], axis=1, keepdims=True), gathered
        )
    turned = gathered.T[: out.shape[0]]
    total = jnp.max(col_acc[...], axis=1)
    if has_prev:
        total = jnp.maximum(total, prev[...])
    out[...] = total
    at = pl.ds(pl.multiple_of(core * rows, rows), rows)
    out[:, at] = jnp.maximum(out[:, at], turned)


def merge_kernel(n_moved, meta, mine_ref, other_ref, *outs):
    core = meta[0]
    best = jnp.maximum(mine_ref[...], other_ref[...])
    outs[0][...] = best[0:2]
    for i in range(n_moved):
        at = 2 + 4 * i
        outs[1 + i][...] = jnp.where(core == 0, best[at : at + 2], best[at + 2 : at + 4])


def finish_kernel(rows, meta, mine_ref, other_ref, o_ref):
    at = pl.ds(pl.multiple_of(meta[0] * rows, rows), rows)
    o_ref[...] = 1.0 - jnp.maximum(mine_ref[:, at], other_ref[:, at])


SMEM = pl.BlockSpec(memory_space=pltpu.SMEM)
VMEM = pl.BlockSpec(memory_space=pltpu.VMEM)
ANY = pl.BlockSpec(memory_space=pl.ANY)


def shards(segments, exclusion):
    rows, length = segments.shape
    n_moved = len(OFFSETS)
    device = lax.axis_index("row") * 16 + lax.axis_index("col")
    core = device % 2
    x = device // 8 % 2 * 2 + device // 16 % 2
    y = device // 32
    z = device // 2 % SIDE
    off = np.array(SLOTS, np.int32)
    sx, sy, sz = (x + off[:, 0]) % SIDE, (y + off[:, 1]) % SIDE, (z + off[:, 2]) % SIDE
    order = ((sy * 2 + sx % 2) * 2 + sx // 2) * SIDE + sz
    meta = jnp.concatenate([core[None], exclusion, order]).astype(jnp.int32)

    own = pl.pallas_call(
        normalize_kernel, out_shape=jax.ShapeDtypeStruct((rows, length), jnp.bfloat16)
    )(segments)
    other = lax.ppermute(own, AXES, across())
    block = jnp.concatenate([own, other], axis=0)

    moved, shared = [], []
    for i, offsets in enumerate(OFFSETS):
        source = SOURCES[i]
        if source is None:
            moved.append(lax.ppermute(block, AXES, moves(offsets)))
        else:
            hops = tuple(minus(a, b) for a, b in zip(offsets, OFFSETS[source]))
            moved.append(lax.ppermute(moved[source], AXES, moves(hops)))
    for i in range(n_moved):
        shared.append(lax.ppermute(moved[i], AXES, across()))

    full, half = pair_lists()

    def phase(count, pairs, halves, groups, diag, prev):
        n_acc = 2 * len(SLOTS)
        table = np.array(pairs + halves, np.int32).reshape(-1)
        operands = [meta, jnp.asarray(table), block]
        for i in range(count):
            operands += [moved[i], shared[i]]
        specs = [SMEM, SMEM] + [ANY] * (1 + 2 * count)
        if prev is not None:
            operands.append(prev)
            specs.append(VMEM)
        n_products = len(pairs) + len(halves) / 2 + diag
        return pl.pallas_call(
            functools.partial(phase_kernel, count, groups, diag, prev is not None, rows),
            out_shape=jax.ShapeDtypeStruct((n_acc, 2 * rows), jnp.float32),
            in_specs=specs,
            out_specs=VMEM,
            scratch_shapes=[
                pltpu.VMEM(((1 + 2 * count) * 2 * rows, length), jnp.bfloat16),
                pltpu.VMEM((n_acc, rows, 128), jnp.float32),
                pltpu.VMEM((n_acc, 8, 2 * rows), jnp.float32),
                pltpu.SemaphoreType.DMA((1 + 2 * count, 2)),
            ],
            compiler_params=pltpu.CompilerParams(vmem_limit_bytes=48 * 2**20),
            cost_estimate=pl.CostEstimate(
                flops=int(4 * n_products * rows * rows * length),
                bytes_accessed=(1 + 2 * count) * 4 * rows * length,
                transcendentals=0,
            ),
        )(*operands)

    def stage(pair):
        return (max(pair) + 1) // 2

    first = 3
    pairs = sorted((p for p in full if stage(p) <= first), key=stage)
    halves = sorted((p for p in half if stage(p) <= first), key=stage)
    groups, i, j = [], 0, len(pairs)
    for step in range(first + 1):
        indices = (0,) if step == 0 else (2 * step - 1, 2 * step)
        i_end = i + sum(stage(p) == step for p in pairs)
        j_end = j + sum(stage(p) == step for p in halves)
        groups.append((indices, (i, i_end), (j, j_end)))
        i, j = i_end, j_end
    best = phase(first, pairs, halves, tuple(groups), True, None)

    pairs = [p for p in full if stage(p) > first]
    halves = [p for p in half if stage(p) > first]
    groups = (
        (tuple(range(1 + 2 * n_moved)), (0, len(pairs)), (len(pairs), len(pairs) + len(halves))),
    )
    best = phase(n_moved, pairs, halves, groups, False, best)

    shape = jax.ShapeDtypeStruct((2, 2 * rows), jnp.float32)
    parts = pl.pallas_call(
        functools.partial(merge_kernel, n_moved),
        out_shape=[shape] * (1 + n_moved),
        in_specs=[SMEM, VMEM, VMEM],
        out_specs=[VMEM] * (1 + n_moved),
    )(meta, best, lax.ppermute(best, AXES, across()))
    mine = parts[0]
    for i, offsets in enumerate(OFFSETS):
        back = tuple(minus((0, 0, 0), a) for a in offsets)
        mine = jnp.maximum(mine, lax.ppermute(parts[1 + i], AXES, moves(back)))
    return pl.pallas_call(
        functools.partial(finish_kernel, rows),
        out_shape=jax.ShapeDtypeStruct((2, rows), jnp.float32),
        in_specs=[SMEM, VMEM, VMEM],
        out_specs=VMEM,
    )(meta, mine, lax.ppermute(mine, AXES, across()))


def solution(mesh):
    return jax.shard_map(
        shards,
        mesh=mesh,
        in_specs=(P(AXES, None), P()),
        out_specs=P(None, AXES),
        check_vma=False,
    )
```

time: 379 us -> 95.9 us (0.25)
  waiting for transfers between devices: 134 us -> 22.2 us
  blocking collectives: 95.5 us -> 0 us
  matrix products: 91.4 us -> 0 us
  Pallas kernels: 0 us -> 32.9 us
  other arithmetic: 32.5 us -> 1.85 us
  starting transfers between devices: 8.72 us -> 36.6 us
  between operations: 14.5 us -> 0.82 us
    all_gather x2 -> x0, waiting for transfers between devices: 126 us -> none  [the longest x1 90.9 us: shards(): lax.all_gather(segments, 'col', axis=0, tiled=True)]
    all_gather x4 -> x0, blocking collectives: 95.5 us -> none  [the longest x1 34 us: shards(): lax.all_gather(spread_inv, 'col', axis=0, tiled=True)]
    dot_general x16 -> x0, matrix products: 91.4 us -> none  [tile_minima(): lax.dot_general(row_data, col_data, (((1,), (1,)), ((), ())), preferred_e...]
    ppermute x0 -> x18, starting transfers between devices: none -> 36.6 us  [the longest x3 9.3 us: shards(): moved.append(lax.ppermute(block, AXES, moves(offsets)))]
    pallas_call x0 -> x5, Pallas kernels: none -> 32.9 us  [the longest x2 27.9 us: phase(): pl.pallas_call(functools.partial(phase_kernel, count, groups, diag, prev...]
    ppermute x0 -> x18, waiting for transfers between devices: none -> 22.2 us  [the longest x3 13.4 us: shards(): moved.append(lax.ppermute(block, AXES, moves(offsets)))]
    dynamic_update_slice x15 -> x0, other arithmetic: 18.3 us -> none  [shards(): lax.dynamic_update_slice_in_dim(visit_row_min, jnp.minimum(previous, part...]
    convert_element_type x2 -> x0, other arithmetic: 9.65 us -> none  [normalize(): ((samples - average[:, None]) * spread_inv[:, None]).astype(jnp.bfloat16)]
  transfers between devices with their start and end apart: 4 -> 18, of which waited for: 3 -> 10; matrix products, arithmetic and copies ran while one was open for 7% -> 0% of each run, Pallas kernels for 0% -> 13%
where the time goes in v1:
time: 95.9 us; the launch traced here: 95.6 us
  starting transfers between devices  36.6 us (38%)
  Pallas kernels  32.9 us (34%)
  waiting for transfers between devices  22.2 us (23%)
  other arithmetic  1.85 us (2%)
  local copies, waits for them, and re-layouts  1.24 us (1%)
    pallas_call x2, Pallas kernels, phase(): pl.pallas_call(functools.partial(phase_kernel, count, groups, diag, prev...  27.9 us
    ppermute x3, waiting for transfers between devices, shards(): moved.append(lax.ppermute(block, AXES, moves(offsets)))  13.4 us
    ppermute x3, starting transfers between devices, shards(): moved.append(lax.ppermute(block, AXES, moves(offsets)))  9.3 us
    ppermute x5, starting transfers between devices, shards(): shared.append(lax.ppermute(moved[i], AXES, across()))  8.56 us
    ppermute x5, starting transfers between devices, shards(): mine = jnp.maximum(mine, lax.ppermute(parts[1 + i], AXES, moves(back)))  7.33 us
    ppermute x1, starting transfers between devices, shards(): lax.ppermute(mine, AXES, across())  5.55 us
    ppermute x2, starting transfers between devices, shards(): moved.append(lax.ppermute(moved[source], AXES, moves(hops)))  4.25 us
    ppermute x2, waiting for transfers between devices, shards(): moved.append(lax.ppermute(moved[source], AXES, moves(hops)))  3.28 us
  transfers between devices with their start and end apart: 18, of which 10 were waited for; matrix products, arithmetic and copies ran while one was open for 0% of the time, Pallas kernels for 13%

profile of v1, /device:TPU:1, one launch (start us, length us, event | category | flops | bytes accessed | tf_op | source)
XLA Modules:
  0.0 95.6 jit_solution(1039873577469774567)
XLA Ops:
  0.0 2.1 %shard_map.73 = bf16[384,512]{1,0:T(8,128)(2,1)} custom-call(f32[384,512]{1,0:T(8,128)} %x_ref.1), custom_call_target="tpu_custom_call" | custom-call | tf_op jit(solution)/shard_map/pallas_call | solution.py:246
  2.2 1.5 %collective-permute-start = (bf16[384,512]{1,0:T(8,128)(2,1)}, bf16[384,512]{1,0:T(8,128)(2,1)S(1)}, u32[]{:S(2)}, u32[]{:S(2)}) collective-permute-start(bf16[384,512]{1,0:T(8,128)(2,1)} %shard_map.73), channel_id=1, source_target_pairs={{0,1},{1,0},{2,3},{3,2},{4,5},{5,4},{6,7},{7,6},{8,9},{9,8},{10,11... | collective-permute-start | bytes 1179656 | tf_op jit(solution)/shard_map/ppermute | solution.py:249
  3.7 1.6 %collective-permute-done = bf16[384,512]{1,0:T(8,128)(2,1)S(1)} collective-permute-done((bf16[384,512]{1,0:T(8,128)(2,1)}, bf16[384,512]{1,0:T(8,128)(2,1)S(1)}, u32[]{:S(2)}, u32[]{:S(2)}) %collective-permute-start) | collective-permute-done | bytes 393248 | tf_op jit(solution)/shard_map/ppermute | solution.py:249
  5.2 1.0 %pad_maximum_fusion.refs_2_ = bf16[768,512]{1,0:T(8,128)(2,1)S(1)} fusion(bf16[384,512]{1,0:T(8,128)(2,1)S(1)} %collective-permute-done, bf16[384,512]{1,0:T(8,128)(2,1)} %shard_map.73), kind=kLoop, calls=%fused_computation | loop fusion | flops 1572864 | bytes 1572864 | tf_op jit(solution)/shard_map/concatenate | solution.py:250
  6.3 3.9 %collective-permute-start.3 = (bf16[768,512]{1,0:T(8,128)(2,1)S(1)}, bf16[768,512]{1,0:T(8,128)(2,1)S(1)}, u32[]{:S(2)}, u32[]{:S(2)}) collective-permute-start(bf16[768,512]{1,0:T(8,128)(2,1)S(1)} %pad_maximum_fusion.refs_2_), channel_id=1, source_target_pairs={{22,0},{3,1},{16,2},{5,3},{18,4},{7,5},{20,6},{1,7},{30,8},{11,9},... | collective-permute-start | bytes 2359304 | tf_op jit(solution)/shard_map/ppermute | solution.py:256
  10.2 2.7 %collective-permute-start.1 = (bf16[768,512]{1,0:T(8,128)(2,1)S(1)}, bf16[768,512]{1,0:T(8,128)(2,1)S(1)}, u32[]{:S(2)}, u32[]{:S(2)}) collective-permute-start(bf16[768,512]{1,0:T(8,128)(2,1)S(1)} %pad_maximum_fusion.refs_2_), channel_id=1, source_target_pairs={{120,0},{33,1},{122,2},{35,3},{124,4},{37,5},{126,6},{39,7},{112,8... | collective-permute-start | bytes 2359304 | tf_op jit(solution)/shard_map/ppermute | solution.py:256
  12.9 2.7 %collective-permute-start.5 = (bf16[768,512]{1,0:T(8,128)(2,1)S(1)}, bf16[768,512]{1,0:T(8,128)(2,1)S(1)}, u32[]{:S(2)}, u32[]{:S(2)}) collective-permute-start(bf16[768,512]{1,0:T(8,128)(2,1)S(1)} %pad_maximum_fusion.refs_2_), channel_id=1, source_target_pairs={{6,0},{49,1},{0,2},{51,3},{2,4},{53,5},{4,6},{55,7},{14,8},{57,9},... | collective-permute-start | bytes 2359304 | tf_op jit(solution)/shard_map/ppermute | solution.py:256
  15.6 3.5 %collective-permute-done.3.refs_5_ = bf16[768,512]{1,0:T(8,128)(2,1)S(1)} collective-permute-done((bf16[768,512]{1,0:T(8,128)(2,1)S(1)}, bf16[768,512]{1,0:T(8,128)(2,1)S(1)}, u32[]{:S(2)}, u32[]{:S(2)}) %collective-permute-start.3) | collective-permute-done | bytes 786464 | tf_op jit(solution)/shard_map/ppermute | solution.py:256
  19.1 1.3 %collective-permute-start.9 = (bf16[768,512]{1,0:T(8,128)(2,1)S(1)}, bf16[768,512]{1,0:T(8,128)(2,1)}, u32[]{:S(2)}, u32[]{:S(2)}) collective-permute-start(bf16[768,512]{1,0:T(8,128)(2,1)S(1)} %collective-permute-done.3.refs_5_), channel_id=1, source_target_pairs={{16,0},{97,1},{18,2},{99,3},{20,4},{101,5},{22,6},{103,7},{24,8},{... | collective-permute-start | bytes 2359304 | tf_op jit(solution)/shard_map/ppermute | solution.py:259
  20.4 9.9 %collective-permute-done.1.refs_3_ = bf16[768,512]{1,0:T(8,128)(2,1)S(1)} collective-permute-done((bf16[768,512]{1,0:T(8,128)(2,1)S(1)}, bf16[768,512]{1,0:T(8,128)(2,1)S(1)}, u32[]{:S(2)}, u32[]{:S(2)}) %collective-permute-start.1) | collective-permute-done | bytes 786464 | tf_op jit(solution)/shard_map/ppermute | solution.py:256
  30.3 3.0 %collective-permute-start.7 = (bf16[768,512]{1,0:T(8,128)(2,1)S(1)}, bf16[768,512]{1,0:T(8,128)(2,1)}, u32[]{:S(2)}, u32[]{:S(2)}) collective-permute-start(bf16[768,512]{1,0:T(8,128)(2,1)S(1)} %collective-permute-done.1.refs_3_), channel_id=1, source_target_pairs={{6,0},{35,1},{0,2},{37,3},{2,4},{39,5},{4,6},{33,7},{14,8},{43,9},... | collective-permute-start | bytes 2359304 | tf_op jit(solution)/shard_map/ppermute | solution.py:259
  34.1 5.4 %collective-permute-start.10 = (bf16[768,512]{1,0:T(8,128)(2,1)}, bf16[768,512]{1,0:T(8,128)(2,1)}, u32[]{:S(2)}, u32[]{:S(2)}) collective-permute-start(bf16[768,512]{1,0:T(8,128)(2,1)} %collective-permute-done.9.refs_11_), channel_id=1, source_target_pairs={{0,1},{1,0},{2,3},{3,2},{4,5},{5,4},{6,7},{7,6},{8,9},{9,8},{10,11... | collective-permute-start | bytes 2359304 | tf_op jit(solution)/shard_map/ppermute | solution.py:261
  39.4 3.0 %collective-permute-done.7.refs_9_ = bf16[768,512]{1,0:T(8,128)(2,1)} collective-permute-done((bf16[768,512]{1,0:T(8,128)(2,1)S(1)}, bf16[768,512]{1,0:T(8,128)(2,1)}, u32[]{:S(2)}, u32[]{:S(2)}) %collective-permute-start.7) | collective-permute-done | bytes 786464 | tf_op jit(solution)/shard_map/ppermute | solution.py:259
  42.4 2.7 %collective-permute-start.8 = (bf16[768,512]{1,0:T(8,128)(2,1)}, bf16[768,512]{1,0:T(8,128)(2,1)}, u32[]{:S(2)}, u32[]{:S(2)}) collective-permute-start(bf16[768,512]{1,0:T(8,128)(2,1)} %collective-permute-done.7.refs_9_), channel_id=1, source_target_pairs={{0,1},{1,0},{2,3},{3,2},{4,5},{5,4},{6,7},{7,6},{8,9},{9,8},{10,11... | collective-permute-start | bytes 2359304 | tf_op jit(solution)/shard_map/ppermute | solution.py:261
  45.9 12.2 %shard_map.74.refs_13_ = f32[22,768]{1,0:T(8,128)S(1)} custom-call(s32[13]{0:T(128)S(1)} %pad_add_fusion.refs_0_.meta, s32[30]{0:T(128)S(1)} %copy-done.3, bf16[768,512]{1,0:T(8,128)(2,1)S(1)} %pad_maximum_fusion.refs_2_, bf16[768,512]{1,0:T(8,128)(2,1)S(1)} %collective-permute-done.1.refs_3_, bf16[768,512]{1,0:T(8,128)(2,1)} %collective-permute-done.2.refs_4_, ...), custom_call_target="tpu_custom_call" | custom-call | flops 4529848320 | bytes 5505024 | tf_op jit(solution)/shard_map/pallas_call | solution.py:276
  58.1 15.7 %shard_map.75.mine_ref = f32[22,768]{1,0:T(8,128)S(1)} custom-call(s32[13]{0:T(128)S(1)} %pad_add_fusion.refs_0_.meta, s32[40]{0:T(128)S(1)} %copy-done.2, bf16[768,512]{1,0:T(8,128)(2,1)S(1)} %pad_maximum_fusion.refs_2_, bf16[768,512]{1,0:T(8,128)(2,1)S(1)} %collective-permute-done.1.refs_3_, bf16[768,512]{1,0:T(8,128)(2,1)} %collective-permute-done.2.refs_4_, ...), custom_call_target="tpu_custom_call" | custom-call | flops 5284823040 | bytes 8650752 | tf_op jit(solution)/shard_map/pallas_call | solution.py:276
  74.0 1.3 %collective-permute-done.11.other_ref = f32[22,768]{1,0:T(8,128)S(1)} collective-permute-done((f32[22,768]{1,0:T(8,128)S(1)}, f32[22,768]{1,0:T(8,128)S(1)}, u32[]{:S(2)}, u32[]{:S(2)}) %collective-permute-start.11) | collective-permute-done | bytes 67616 | tf_op jit(solution)/shard_map/ppermute | solution.py:323
  75.8 1.6 %shard_map.76 = (f32[2,768]{1,0:T(2,128)}, f32[2,768]{1,0:T(2,128)}, f32[2,768]{1,0:T(2,128)}, f32[2,768]{1,0:T(2,128)}, f32[2,768]{1,0:T(2,128)}, /*index=5*/f32[2,768]{1,0:T(2,128)}) custom-call(s32[13]{0:T(128)} %copy-done.1, f32[22,768]{1,0:T(8,128)} %copy-done, f32[22,768]{1,0:T(8,128)} %copy-done.4), custom_call_target="tpu_custom_call" | custom-call | tf_op jit(solution)/shard_map/pallas_call | solution.py:318
  77.4 1.6 %collective-permute-start.12 = (f32[2,768]{1,0:T(2,128)}, f32[2,768]{1,0:T(2,128)S(1)}, u32[]{:S(2)}, u32[]{:S(2)}) collective-permute-start(f32[2,768]{1,0:T(2,128)} %get-tuple-element.12), channel_id=1, source_target_pairs={{48,0},{97,1},{50,2},{99,3},{52,4},{101,5},{54,6},{103,7},{56,8},{... | collective-permute-start | bytes 18440 | tf_op jit(solution)/shard_map/ppermute | solution.py:327
  79.9 1.9 %collective-permute-start.15 = (f32[2,768]{1,0:T(2,128)}, f32[2,768]{1,0:T(2,128)S(1)}, u32[]{:S(2)}, u32[]{:S(2)}) collective-permute-start(f32[2,768]{1,0:T(2,128)} %get-tuple-element.15), channel_id=1, source_target_pairs={{50,0},{71,1},{52,2},{65,3},{54,4},{67,5},{48,6},{69,7},{58,8},{79... | collective-permute-start | bytes 18440 | tf_op jit(solution)/shard_map/ppermute | solution.py:327
  81.8 3.0 %collective-permute-start.16 = (f32[2,768]{1,0:T(2,128)}, f32[2,768]{1,0:T(2,128)S(1)}, u32[]{:S(2)}, u32[]{:S(2)}) collective-permute-start(f32[2,768]{1,0:T(2,128)} %get-tuple-element.16), channel_id=1, source_target_pairs={{10,0},{39,1},{12,2},{33,3},{14,4},{35,5},{8,6},{37,7},{2,8},{47,9... | collective-permute-start | bytes 18440 | tf_op jit(solution)/shard_map/ppermute | solution.py:327
  85.0 1.1 %collective-permute-done.15 = f32[2,768]{1,0:T(2,128)S(1)} collective-permute-done((f32[2,768]{1,0:T(2,128)}, f32[2,768]{1,0:T(2,128)S(1)}, u32[]{:S(2)}, u32[]{:S(2)}) %collective-permute-start.15) | collective-permute-done | bytes 6176 | tf_op jit(solution)/shard_map/ppermute | solution.py:327
  87.3 5.5 %collective-permute-start.17 = (f32[2,768]{1,0:T(2,128)S(1)}, f32[2,768]{1,0:T(2,128)S(1)}, u32[]{:S(2)}, u32[]{:S(2)}) collective-permute-start(f32[2,768]{1,0:T(2,128)S(1)} %maximum_maximum_fusion.mine_ref), channel_id=1, source_target_pairs={{0,1},{1,0},{2,3},{3,2},{4,5},{5,4},{6,7},{7,6},{8,9},{9,8},{10,11... | collective-permute-start | bytes 18440 | tf_op jit(solution)/shard_map/ppermute | solution.py:333
  94.2 1.3 %shard_map.77 = f32[2,384]{1,0:T(2,128)} custom-call(s32[13]{0:T(128)} %copy-done.1, f32[2,768]{1,0:T(2,128)} %copy-done.5, f32[2,768]{1,0:T(2,128)} %copy-done.6), custom_call_target="tpu_custom_call" | custom-call | tf_op jit(solution)/shard_map/pallas_call | solution.py:328
  (41 shorter events, 5.3 us)
Async XLA Ops:
  2.1 43.6 %copy-start.7 = (s32[11]{0:T(128)S(1)}, s32[11]{0:T(128)}, u32[]{:S(2)}) copy-start(s32[11]{0:T(128)} %constant.129.clone) | copy-start | bytes 136
  2.1 43.6 %copy-start.8 = (s32[11]{0:T(128)S(1)}, s32[11]{0:T(128)}, u32[]{:S(2)}) copy-start(s32[11]{0:T(128)} %constant.128.clone) | copy-start | bytes 136
  2.2 43.6 %copy-start.9 = (s32[11]{0:T(128)S(1)}, s32[11]{0:T(128)}, u32[]{:S(2)}) copy-start(s32[11]{0:T(128)} %constant.127.clone) | copy-start | bytes 136
  2.2 43.8 %copy-start.3 = (s32[30]{0:T(128)S(1)}, s32[30]{0:T(128)}, u32[]{:S(2)}) copy-start(s32[30]{0:T(128)} %constant.130.clone.refs_1_) | copy-start | bytes 364
  2.2 3.1 %collective-permute-start = (bf16[384,512]{1,0:T(8,128)(2,1)}, bf16[384,512]{1,0:T(8,128)(2,1)S(1)}, u32[]{:S(2)}, u32[]{:S(2)}) collective-permute-start(bf16[384,512]{1,0:T(8,128)(2,1)} %shard_map.73), channel_id=1, source_target_pairs={{0,1},{1,0},{2,3},{3,2},{4,5},{5,4},{6,7},{7,6},{8,9},{9,8},{10,11... | collective-permute-start | bytes 1179656 | tf_op jit(solution)/shard_map/ppermute | solution.py:249
  6.3 12.8 %collective-permute-start.3 = (bf16[768,512]{1,0:T(8,128)(2,1)S(1)}, bf16[768,512]{1,0:T(8,128)(2,1)S(1)}, u32[]{:S(2)}, u32[]{:S(2)}) collective-permute-start(bf16[768,512]{1,0:T(8,128)(2,1)S(1)} %pad_maximum_fusion.refs_2_), channel_id=1, source_target_pairs={{22,0},{3,1},{16,2},{5,3},{18,4},{7,5},{20,6},{1,7},{30,8},{11,9},... | collective-permute-start | bytes 2359304 | tf_op jit(solution)/shard_map/ppermute | solution.py:256
  10.2 20.1 %collective-permute-start.1 = (bf16[768,512]{1,0:T(8,128)(2,1)S(1)}, bf16[768,512]{1,0:T(8,128)(2,1)S(1)}, u32[]{:S(2)}, u32[]{:S(2)}) collective-permute-start(bf16[768,512]{1,0:T(8,128)(2,1)S(1)} %pad_maximum_fusion.refs_2_), channel_id=1, source_target_pairs={{120,0},{33,1},{122,2},{35,3},{124,4},{37,5},{126,6},{39,7},{112,8... | collective-permute-start | bytes 2359304 | tf_op jit(solution)/shard_map/ppermute | solution.py:256
  12.9 20.3 %collective-permute-start.5 = (bf16[768,512]{1,0:T(8,128)(2,1)S(1)}, bf16[768,512]{1,0:T(8,128)(2,1)S(1)}, u32[]{:S(2)}, u32[]{:S(2)}) collective-permute-start(bf16[768,512]{1,0:T(8,128)(2,1)S(1)} %pad_maximum_fusion.refs_2_), channel_id=1, source_target_pairs={{6,0},{49,1},{0,2},{51,3},{2,4},{53,5},{4,6},{55,7},{14,8},{57,9},... | collective-permute-start | bytes 2359304 | tf_op jit(solution)/shard_map/ppermute | solution.py:256
  19.1 14.9 %collective-permute-start.9 = (bf16[768,512]{1,0:T(8,128)(2,1)S(1)}, bf16[768,512]{1,0:T(8,128)(2,1)}, u32[]{:S(2)}, u32[]{:S(2)}) collective-permute-start(bf16[768,512]{1,0:T(8,128)(2,1)S(1)} %collective-permute-done.3.refs_5_), channel_id=1, source_target_pairs={{16,0},{97,1},{18,2},{99,3},{20,4},{101,5},{22,6},{103,7},{24,8},{... | collective-permute-start | bytes 2359304 | tf_op jit(solution)/shard_map/ppermute | solution.py:259
  30.3 12.1 %collective-permute-start.7 = (bf16[768,512]{1,0:T(8,128)(2,1)S(1)}, bf16[768,512]{1,0:T(8,128)(2,1)}, u32[]{:S(2)}, u32[]{:S(2)}) collective-permute-start(bf16[768,512]{1,0:T(8,128)(2,1)S(1)} %collective-permute-done.1.refs_3_), channel_id=1, source_target_pairs={{6,0},{35,1},{0,2},{37,3},{2,4},{39,5},{4,6},{33,7},{14,8},{43,9},... | collective-permute-start | bytes 2359304 | tf_op jit(solution)/shard_map/ppermute | solution.py:259
  33.2 12.6 %collective-permute-start.6 = (bf16[768,512]{1,0:T(8,128)(2,1)S(1)}, bf16[768,512]{1,0:T(8,128)(2,1)}, u32[]{:S(2)}, u32[]{:S(2)}) collective-permute-start(bf16[768,512]{1,0:T(8,128)(2,1)S(1)} %collective-permute-done.5.refs_7_), channel_id=1, source_target_pairs={{0,1},{1,0},{2,3},{3,2},{4,5},{5,4},{6,7},{7,6},{8,9},{9,8},{10,11... | collective-permute-start | bytes 2359304 | tf_op jit(solution)/shard_map/ppermute | solution.py:261
  33.2 12.7 %collective-permute-start.4 = (bf16[768,512]{1,0:T(8,128)(2,1)S(1)}, bf16[768,512]{1,0:T(8,128)(2,1)}, u32[]{:S(2)}, u32[]{:S(2)}) collective-permute-start(bf16[768,512]{1,0:T(8,128)(2,1)S(1)} %collective-permute-done.3.refs_5_), channel_id=1, source_target_pairs={{0,1},{1,0},{2,3},{3,2},{4,5},{5,4},{6,7},{7,6},{8,9},{9,8},{10,11... | collective-permute-start | bytes 2359304 | tf_op jit(solution)/shard_map/ppermute | solution.py:261
  33.7 12.2 %collective-permute-start.2 = (bf16[768,512]{1,0:T(8,128)(2,1)S(1)}, bf16[768,512]{1,0:T(8,128)(2,1)}, u32[]{:S(2)}, u32[]{:S(2)}) collective-permute-start(bf16[768,512]{1,0:T(8,128)(2,1)S(1)} %collective-permute-done.1.refs_3_), channel_id=1, source_target_pairs={{0,1},{1,0},{2,3},{3,2},{4,5},{5,4},{6,7},{7,6},{8,9},{9,8},{10,11... | collective-permute-start | bytes 2359304 | tf_op jit(solution)/shard_map/ppermute | solution.py:261
  34.1 24.0 %collective-permute-start.10 = (bf16[768,512]{1,0:T(8,128)(2,1)}, bf16[768,512]{1,0:T(8,128)(2,1)}, u32[]{:S(2)}, u32[]{:S(2)}) collective-permute-start(bf16[768,512]{1,0:T(8,128)(2,1)} %collective-permute-done.9.refs_11_), channel_id=1, source_target_pairs={{0,1},{1,0},{2,3},{3,2},{4,5},{5,4},{6,7},{7,6},{8,9},{9,8},{10,11... | collective-permute-start | bytes 2359304 | tf_op jit(solution)/shard_map/ppermute | solution.py:261
  42.4 15.7 %collective-permute-start.8 = (bf16[768,512]{1,0:T(8,128)(2,1)}, bf16[768,512]{1,0:T(8,128)(2,1)}, u32[]{:S(2)}, u32[]{:S(2)}) collective-permute-start(bf16[768,512]{1,0:T(8,128)(2,1)} %collective-permute-done.7.refs_9_), channel_id=1, source_target_pairs={{0,1},{1,0},{2,3},{3,2},{4,5},{5,4},{6,7},{7,6},{8,9},{9,8},{10,11... | collective-permute-start | bytes 2359304 | tf_op jit(solution)/shard_map/ppermute | solution.py:261
  45.9 12.2 %copy-start.1 = (s32[13]{0:T(128)}, s32[13]{0:T(128)S(1)}, u32[]{:S(2)}) copy-start(s32[13]{0:T(128)S(1)} %pad_add_fusion.refs_0_.meta) | copy-start | bytes 160
  45.9 12.2 %copy-start.2 = (s32[40]{0:T(128)S(1)}, s32[40]{0:T(128)}, u32[]{:S(2)}) copy-start(s32[40]{0:T(128)} %constant.131.clone.refs_1_) | copy-start | bytes 484
  73.9 1.3 %collective-permute-start.11 = (f32[22,768]{1,0:T(8,128)S(1)}, f32[22,768]{1,0:T(8,128)S(1)}, u32[]{:S(2)}, u32[]{:S(2)}) collective-permute-start(f32[22,768]{1,0:T(8,128)S(1)} %shard_map.75.mine_ref), channel_id=1, source_target_pairs={{0,1},{1,0},{2,3},{3,2},{4,5},{5,4},{6,7},{7,6},{8,9},{9,8},{10,11... | collective-permute-start | bytes 202760 | tf_op jit(solution)/shard_map/ppermute | solution.py:323
  77.4 7.3 %collective-permute-start.12 = (f32[2,768]{1,0:T(2,128)}, f32[2,768]{1,0:T(2,128)S(1)}, u32[]{:S(2)}, u32[]{:S(2)}) collective-permute-start(f32[2,768]{1,0:T(2,128)} %get-tuple-element.12), channel_id=1, source_target_pairs={{48,0},{97,1},{50,2},{99,3},{52,4},{101,5},{54,6},{103,7},{56,8},{... | collective-permute-start | bytes 18440 | tf_op jit(solution)/shard_map/ppermute | solution.py:327
  79.0 5.7 %collective-permute-start.13 = (f32[2,768]{1,0:T(2,128)}, f32[2,768]{1,0:T(2,128)S(1)}, u32[]{:S(2)}, u32[]{:S(2)}) collective-permute-start(f32[2,768]{1,0:T(2,128)} %get-tuple-element.13), channel_id=1, source_target_pairs={{26,0},{7,1},{28,2},{1,3},{30,4},{3,5},{24,6},{5,7},{18,8},{15,9},... | collective-permute-start | bytes 18440 | tf_op jit(solution)/shard_map/ppermute | solution.py:327
  79.0 6.0 %collective-permute-start.14 = (f32[2,768]{1,0:T(2,128)}, f32[2,768]{1,0:T(2,128)S(1)}, u32[]{:S(2)}, u32[]{:S(2)}) collective-permute-start(f32[2,768]{1,0:T(2,128)} %get-tuple-element.14), channel_id=1, source_target_pairs={{2,0},{121,1},{4,2},{123,3},{6,4},{125,5},{0,6},{127,7},{10,8},{11... | collective-permute-start | bytes 18440 | tf_op jit(solution)/shard_map/ppermute | solution.py:327
  79.9 6.3 %collective-permute-start.15 = (f32[2,768]{1,0:T(2,128)}, f32[2,768]{1,0:T(2,128)S(1)}, u32[]{:S(2)}, u32[]{:S(2)}) collective-permute-start(f32[2,768]{1,0:T(2,128)} %get-tuple-element.15), channel_id=1, source_target_pairs={{50,0},{71,1},{52,2},{65,3},{54,4},{67,5},{48,6},{69,7},{58,8},{79... | collective-permute-start | bytes 18440 | tf_op jit(solution)/shard_map/ppermute | solution.py:327
  81.8 4.8 %collective-permute-start.16 = (f32[2,768]{1,0:T(2,128)}, f32[2,768]{1,0:T(2,128)S(1)}, u32[]{:S(2)}, u32[]{:S(2)}) collective-permute-start(f32[2,768]{1,0:T(2,128)} %get-tuple-element.16), channel_id=1, source_target_pairs={{10,0},{39,1},{12,2},{33,3},{14,4},{35,5},{8,6},{37,7},{2,8},{47,9... | collective-permute-start | bytes 18440 | tf_op jit(solution)/shard_map/ppermute | solution.py:327
  87.3 6.4 %collective-permute-start.17 = (f32[2,768]{1,0:T(2,128)S(1)}, f32[2,768]{1,0:T(2,128)S(1)}, u32[]{:S(2)}, u32[]{:S(2)}) collective-permute-start(f32[2,768]{1,0:T(2,128)S(1)} %maximum_maximum_fusion.mine_ref), channel_id=1, source_target_pairs={{0,1},{1,0},{2,3},{3,2},{4,5},{5,4},{6,7},{7,6},{8,9},{9,8},{10,11... | collective-permute-start | bytes 18440 | tf_op jit(solution)/shard_map/ppermute | solution.py:333
  (4 other events, 9.0 us)

commit v2 on v0

v2 whole, which is shorter than its diff:
```python
import functools
import itertools
import math

import jax
import jax.numpy as jnp
from jax import lax
from jax.experimental import pallas as pl
from jax.experimental.pallas import tpu as pltpu
from jax.sharding import PartitionSpec as P

AXES = ("row", "col")
SIDE = 4
HELD = (
    ((0, 0, 0), (0, 1, 0), (3, 0, 1), (0, 2, 0), (2, 0, 1), (1, 3, 3)),
    ((0, 0, 0), (1, 3, 0), (0, 0, 3), (2, 2, 0), (0, 0, 2), (1, 2, 1)),
)
SOURCE = (None, 0, 0, 1, 2, 3)
MOVED = 5
SHARED = (1, 2, 3)
FIRST = ((1, 0), (2, 0), (2, 1))
SECOND = ((1, 6), (2, 6), (2, 7))
THIRD = ((3, 0), (3, 6), (4, 0), (4, 1), (4, 2), (4, 6), (4, 7), (4, 3), (3, 8), (4, 8))
LAST = ((5, 0), (5, 1), (5, 2), (5, 4))
LOW = -3.0


def minus(a, b):
    return tuple((p - q) % SIDE for p, q in zip(a, b))


def coords(device):
    row, col = divmod(device, 16)
    y, x_lo = divmod(row, 2)
    return (col // 8 * 2 + x_lo, y, col // 2 % SIDE, col % 2)


def device_at(x, y, z, core):
    x, y, z = x % SIDE, y % SIDE, z % SIDE
    return (y * 2 + x % 2) * 16 + x // 2 * 8 + z * 2 + core


def moves(hops):
    out = []
    for target in range(128):
        x, y, z, core = coords(target)
        dx, dy, dz = hops[core]
        out.append((device_at(x + dx, y + dy, z + dz, core), target))
    return out


def across():
    return [(device, device ^ 1) for device in range(128)]


def offset_of(name, core):
    return HELD[core][name] if name <= MOVED else HELD[1 - core][name - MOVED]


def check_cover():
    seen = {(0, 0, 0)}
    for a, b in FIRST + SECOND + THIRD + LAST:
        for core in (0, 1):
            diff = minus(offset_of(a, core), offset_of(b, core))
            seen |= {diff, minus((0, 0, 0), diff)}
    assert seen == set(itertools.product(range(SIDE), repeat=3))


def may_touch(a, b):
    steps = {(0, 0, 1), (2, 0, 1), (3, 0, 1), (1, 1, 1)}
    steps |= {minus((0, 0, 0), step) for step in steps}
    return any(minus(offset_of(a, core), offset_of(b, core)) in steps for core in (0, 1))


def normalize_kernel(own_ref, other_ref, o_ref):
    rows, length = own_ref.shape
    for at, ref in ((0, own_ref), (rows, other_ref)):
        x = ref[...]
        average = jnp.sum(x, axis=1, keepdims=True) * (1.0 / length)
        centered = x - average
        power = jnp.sum(centered * centered, axis=1, keepdims=True) * (1.0 / length)
        spread_inv = lax.rsqrt(power + 1e-05) * (1.0 / math.sqrt(length))
        o_ref[at : at + rows] = (centered * spread_inv).astype(jnp.bfloat16)


def here():
    row, col = lax.axis_index("row"), lax.axis_index("col")
    x = (col >> 3) * 2 + (row & 1)
    return x, row >> 1, (col >> 1) & 3, col & 1


def order_of(name, place):
    x, y, z, core = place
    zero, one = offset_of(name, 0), offset_of(name, 1)
    sx, sy, sz = (
        (p + (a if a == b else jnp.where(core == 0, a, b))) & 3
        for p, a, b in zip((x, y, z), zero, one)
    )
    order = ((sy * 2 + (sx & 1)) * 2 + (sx >> 1)) * SIDE + sz
    return order, core if name <= MOVED else 1 - core


def positions(shape, dim, first, order, flip, size):
    at = lax.broadcasted_iota(jnp.int32, shape, dim) + (first + flip * (size // 2))
    return order * size + jnp.where(at >= size, at - size, at)


def phase_kernel(names, pairs, diag, n_prev, n_out, *refs):
    exclude_ref = refs[0]
    blocks = dict(zip(names, refs[1 : 1 + len(names)]))
    rest = refs[1 + len(names) :]
    prev, rest = rest[:n_prev], rest[n_prev:]
    outs, (row_acc, col_acc) = rest[:-2], rest[-2:]
    exclude = exclude_ref[0]
    place = here()
    size = blocks[names[0]].shape[0]
    width = 256
    row_names = sorted({a for a, _ in pairs} | ({0} if diag else set()))
    col_names = sorted({b for _, b in pairs})

    row_acc[...] = jnp.full(row_acc.shape, LOW, jnp.float32)
    col_acc[...] = jnp.full(col_acc.shape, LOW, jnp.float32)

    def product(a, b, part):
        return lax.dot_general(
            blocks[a][...],
            blocks[b][part * width : (part + 1) * width],
            (((1,), (1,)), ((), ())),
            preferred_element_type=jnp.float32,
        )

    def row_max(values):
        best = values[:, :128]
        for at in range(128, width, 128):
            best = jnp.maximum(best, values[:, at : at + 128])
        return best

    def col_max(values):
        return jnp.max(values.reshape(size // 8, 8, width), axis=0)

    def apart(a, b, part):
        order_a, flip_a = order_of(a, place)
        order_b, flip_b = order_of(b, place)
        shape = (size, width)
        return positions(shape, 1, part * width, order_b, flip_b, size) - positions(
            shape, 0, 0, order_a, flip_a, size
        )

    def visit(a, b, masked):
        later = (order_of(b, place)[0] > order_of(a, place)[0]).astype(jnp.int32)
        row_at = 2 * row_names.index(a) + later
        col_at = 2 * col_names.index(b) + 1 - later
        for part in range(size // width):
            values = product(a, b, part)
            if masked:
                values = jnp.where(jnp.abs(apart(a, b, part)) > exclude, values, LOW)
            row_acc[row_at] = jnp.maximum(row_acc[row_at], row_max(values))
            at = pl.ds(part * width, width)
            col_acc[col_at, :, at] = jnp.maximum(col_acc[col_at, :, at], col_max(values))

    if diag:
        at = 2 * row_names.index(0)
        for part in range(size // width):
            values = product(0, 0, part)
            offset = apart(0, 0, part)
            earlier = jnp.where(offset < -exclude, values, LOW)
            later = jnp.where(offset > exclude, values, LOW)
            row_acc[at] = jnp.maximum(row_acc[at], row_max(earlier))
            row_acc[at + 1] = jnp.maximum(row_acc[at + 1], row_max(later))
    for a, b in pairs:
        if may_touch(a, b):
            near = jnp.abs(order_of(a, place)[0] - order_of(b, place)[0]) == 1
            pl.when(near)(functools.partial(visit, a, b, True))
            pl.when(jnp.logical_not(near))(functools.partial(visit, a, b, False))
        else:
            visit(a, b, False)

    lanes = lax.broadcasted_iota(jnp.int32, (size, 128), 1)
    gathered = jnp.full((size, 128), LOW, jnp.float32)
    for at in range(2 * len(row_names)):
        gathered = jnp.where(
            lanes == at, jnp.max(row_acc[at], axis=1, keepdims=True), gathered
        )
    turned = gathered.T
    folded = jnp.max(col_acc[...], axis=1)

    def result(name):
        parts = []
        if name in row_names:
            at = 2 * row_names.index(name)
            parts.append(turned[at : at + 2])
        if name in col_names:
            at = 2 * col_names.index(name)
            parts.append(folded[at : at + 2])
        if n_prev and (name <= MOVED or not isinstance(n_out, tuple)):
            parts.append(prev[0][2 * name : 2 * name + 2])
        elif n_prev and name > MOVED:
            parts.append(prev[1][2 * (name - MOVED - 1) : 2 * (name - MOVED)])
        if n_out == "each" and name in SHARED:
            at = 2 * SHARED.index(name)
            parts.append(prev[1][at : at + 2])
        return functools.reduce(jnp.maximum, parts) if parts else jnp.full((2, size), LOW)

    if n_out == "each":
        for name in range(MOVED + 1):
            outs[name][...] = result(name)
    else:
        for name in range(MOVED + 1):
            outs[0][2 * name : 2 * name + 2] = result(name)
        for i, name in enumerate(SHARED):
            outs[1][2 * i : 2 * i + 2] = result(MOVED + name)


SMEM = pl.BlockSpec(memory_space=pltpu.SMEM)
VMEM = pl.BlockSpec(memory_space=pltpu.VMEM)


def shards(segments, exclusion):
    check_cover()
    rows, length = segments.shape
    size = 2 * rows
    float32 = jnp.float32

    def phase(pairs, blocks, prev, diag=False, each=False):
        names = sorted({name for pair in pairs for name in pair} | ({0} if diag else set()))
        rows_of = {a for a, _ in pairs} | ({0} if diag else set())
        cols_of = {b for _, b in pairs}
        if each:
            out_shape = [jax.ShapeDtypeStruct((2, size), float32)] * (MOVED + 1)
        else:
            out_shape = [
                jax.ShapeDtypeStruct((2 * MOVED + 2, size), float32),
                jax.ShapeDtypeStruct((2 * len(SHARED), size), float32),
            ]
        count = len(pairs) + diag
        return pl.pallas_call(
            functools.partial(
                phase_kernel, names, pairs, diag, len(prev), "each" if each else (2,)
            ),
            out_shape=out_shape,
            in_specs=[SMEM] + [VMEM] * (len(names) + len(prev)),
            out_specs=[VMEM] * len(out_shape),
            scratch_shapes=[
                pltpu.VMEM((2 * len(rows_of), size, 128), float32),
                pltpu.VMEM((2 * max(len(cols_of), 1), 8, size), float32),
            ],
            compiler_params=pltpu.CompilerParams(vmem_limit_bytes=40 * 2**20),
            cost_estimate=pl.CostEstimate(
                flops=2 * count * size * size * length,
                bytes_accessed=len(names) * 2 * size * length,
                transcendentals=0,
            ),
        )(exclusion, *[blocks[name] for name in names], *prev)

    block = pl.pallas_call(
        normalize_kernel, out_shape=jax.ShapeDtypeStruct((size, length), jnp.bfloat16)
    )(segments, lax.ppermute(segments, AXES, across()))

    blocks = {0: block}

    def move(i):
        hops = tuple(minus(HELD[c][i], HELD[c][SOURCE[i]]) for c in (0, 1))
        blocks[i] = lax.ppermute(blocks[SOURCE[i]], AXES, moves(hops))

    def share(i):
        blocks[MOVED + i] = lax.ppermute(blocks[i], AXES, across())

    def after(i, done):
        blocks[i], done = lax.optimization_barrier((blocks[i], done))
        return done

    move(1)
    move(2)
    best = phase((), blocks, (), diag=True)
    best = after(1, best)
    best = after(2, best)
    move(3)
    move(4)
    share(1)
    share(2)
    best = phase(FIRST, blocks, best)
    best = phase(SECOND, blocks, best)
    best = after(3, best)
    best = after(4, best)
    move(5)
    share(3)
    best = phase(THIRD, blocks, best)
    best = after(5, best)
    parts = phase(LAST, blocks, (best[0], lax.ppermute(best[1], AXES, across())), each=True)

    mine = parts[0]
    for i in range(1, MOVED + 1):
        back = tuple(minus((0, 0, 0), HELD[c][i]) for c in (0, 1))
        mine = jnp.maximum(mine, lax.ppermute(parts[i], AXES, moves(back)))
    other = lax.ppermute(mine, AXES, across())
    return 1.0 - jnp.maximum(mine[:, :rows], other[:, rows:])


def solution(mesh):
    return jax.shard_map(
        shards,
        mesh=mesh,
        in_specs=(P(AXES, None), P()),
        out_specs=P(None, AXES),
        check_vma=False,
    )
```

time: 379 us -> 76.3 us (0.20)
  waiting for transfers between devices: 134 us -> 23.8 us
  blocking collectives: 95.5 us -> 0 us
  matrix products: 91.4 us -> 0 us
  other arithmetic: 32.5 us -> 0.59 us
  Pallas kernels: 0 us -> 22.1 us
  starting transfers between devices: 8.72 us -> 26.3 us
  between operations: 14.5 us -> 0.69 us
    all_gather x2 -> x0, waiting for transfers between devices: 126 us -> none  [the longest x1 90.9 us: shards(): lax.all_gather(segments, 'col', axis=0, tiled=True)]
    all_gather x4 -> x0, blocking collectives: 95.5 us -> none  [the longest x1 34 us: shards(): lax.all_gather(spread_inv, 'col', axis=0, tiled=True)]
    dot_general x16 -> x0, matrix products: 91.4 us -> none  [tile_minima(): lax.dot_general(row_data, col_data, (((1,), (1,)), ((), ())), preferred_e...]
    ppermute x0 -> x16, starting transfers between devices: none -> 26.3 us  [the longest x5 10.9 us: shards(): mine = jnp.maximum(mine, lax.ppermute(parts[i], AXES, moves(back)))]
    ppermute x0 -> x16, waiting for transfers between devices: none -> 23.8 us  [the longest x5 15.1 us: move(): blocks[i] = lax.ppermute(blocks[SOURCE[i]], AXES, moves(hops))]
    pallas_call x0 -> x6, Pallas kernels: none -> 22.1 us  [the longest x5 19.4 us: phase(): pl.pallas_call(functools.partial(phase_kernel, names, pairs, diag, len(pr...]
    dynamic_update_slice x15 -> x0, other arithmetic: 18.3 us -> none  [shards(): lax.dynamic_update_slice_in_dim(visit_row_min, jnp.minimum(previous, part...]
    convert_element_type x2 -> x0, other arithmetic: 9.65 us -> none  [normalize(): ((samples - average[:, None]) * spread_inv[:, None]).astype(jnp.bfloat16)]
  transfers between devices with their start and end apart: 4 -> 16, of which waited for: 3 -> 9; matrix products, arithmetic and copies ran while one was open for 7% -> 0% of each run, Pallas kernels for 0% -> 21%
where the time goes in v2:
time: 76.3 us; the launch traced here: 75.5 us
  starting transfers between devices  26.3 us (34%)
  waiting for transfers between devices  23.8 us (31%)
  Pallas kernels  22.1 us (29%)
  local copies, waits for them, and re-layouts  2.02 us (3%)
    pallas_call x5, Pallas kernels, phase(): pl.pallas_call(functools.partial(phase_kernel, names, pairs, diag, len(pr...  19.4 us
    ppermute x5, waiting for transfers between devices, move(): blocks[i] = lax.ppermute(blocks[SOURCE[i]], AXES, moves(hops))  15.1 us
    ppermute x5, starting transfers between devices, shards(): mine = jnp.maximum(mine, lax.ppermute(parts[i], AXES, moves(back)))  10.9 us
    ppermute x5, starting transfers between devices, move(): blocks[i] = lax.ppermute(blocks[SOURCE[i]], AXES, moves(hops))  10.6 us
    ppermute x5, waiting for transfers between devices, shards(): mine = jnp.maximum(mine, lax.ppermute(parts[i], AXES, moves(back)))  4.52 us
    pallas_call x1, Pallas kernels, shards(): pl.pallas_call(normalize_kernel, out_shape=jax.ShapeDtypeStruct((size, le...  2.73 us
    ppermute x1, starting transfers between devices, shards(): lax.ppermute(best[1], AXES, across())  2.26 us
    ppermute x1, waiting for transfers between devices, shards(): lax.ppermute(segments, AXES, across())  2.12 us
  transfers between devices with their start and end apart: 16, of which 9 were waited for; matrix products, arithmetic and copies ran while one was open for 0% of the time, Pallas kernels for 21%

profile of v2, /device:TPU:1, one launch (start us, length us, event | category | flops | bytes accessed | tf_op | source)
XLA Modules:
  0.0 75.5 jit_solution(9686625008647765983)
XLA Ops:
  0.0 1.4 %collective-permute-start = (f32[384,512]{1,0:T(8,128)}, f32[384,512]{1,0:T(8,128)S(1)}, u32[]{:S(2)}, u32[]{:S(2)}) collective-permute-start(f32[384,512]{1,0:T(8,128)} %own_ref.1), channel_id=1, source_target_pairs={{0,1},{1,0},{2,3},{3,2},{4,5},{5,4},{6,7},{7,6},{8,9},{9,8},{10,11... | collective-permute-start | bytes 2359304 | tf_op jit(solution)/shard_map/ppermute | solution.py:257
  1.4 2.1 %collective-permute-done.other_ref = f32[384,512]{1,0:T(8,128)S(1)} collective-permute-done((f32[384,512]{1,0:T(8,128)}, f32[384,512]{1,0:T(8,128)S(1)}, u32[]{:S(2)}, u32[]{:S(2)}) %collective-permute-start) | collective-permute-done | bytes 786464 | tf_op jit(solution)/shard_map/ppermute | solution.py:257
  3.5 0.9 %copy-done.2 = f32[384,512]{1,0:T(8,128)} copy-done((f32[384,512]{1,0:T(8,128)}, f32[384,512]{1,0:T(8,128)S(1)}, u32[]{:S(2)}) %copy-start.2) | copy-done | bytes 786456
  4.4 2.7 %shard_map.28.refs_1_ = bf16[768,512]{1,0:T(8,128)(2,1)} custom-call(f32[384,512]{1,0:T(8,128)} %own_ref.1, f32[384,512]{1,0:T(8,128)} %copy-done.2), custom_call_target="tpu_custom_call" | custom-call | tf_op jit(solution)/shard_map/pallas_call | solution.py:255
  7.2 3.6 %collective-permute-start.1 = (bf16[768,512]{1,0:T(8,128)(2,1)}, bf16[768,512]{1,0:T(8,128)(2,1)S(1)}, u32[]{:S(2)}, u32[]{:S(2)}) collective-permute-start(bf16[768,512]{1,0:T(8,128)(2,1)} %shard_map.28.refs_1_), channel_id=1, source_target_pairs={{32,0},{113,1},{34,2},{115,3},{36,4},{117,5},{38,6},{119,7},{40,8}... | collective-permute-start | bytes 2359304 | tf_op jit(solution)/shard_map/ppermute | solution.py:263
  10.7 1.6 %collective-permute-start.2 = (bf16[768,512]{1,0:T(8,128)(2,1)}, bf16[768,512]{1,0:T(8,128)(2,1)S(1)}, u32[]{:S(2)}, u32[]{:S(2)}) collective-permute-start(bf16[768,512]{1,0:T(8,128)(2,1)} %shard_map.28.refs_1_), channel_id=1, source_target_pairs={{26,0},{7,1},{28,2},{1,3},{30,4},{3,5},{24,6},{5,7},{18,8},{15,9},... | collective-permute-start | bytes 2359304 | tf_op jit(solution)/shard_map/ppermute | solution.py:263
  13.0 1.1 %copy-done = bf16[768,512]{1,0:T(8,128)(2,1)S(1)} copy-done((bf16[768,512]{1,0:T(8,128)(2,1)S(1)}, bf16[768,512]{1,0:T(8,128)(2,1)}, u32[]{:S(2)}) %copy-start) | copy-done | bytes 786456
  14.2 1.3 %shard_map.29 = (f32[12,768]{1,0:T(8,128)S(1)}, f32[6,768]{1,0:T(8,128)S(1)}) custom-call(s32[1]{0:T(128)S(6)} %copy.3.refs_0_, bf16[768,512]{1,0:T(8,128)(2,1)S(1)} %copy-done), custom_call_target="tpu_custom_call" | custom-call | flops 603979776 | bytes 786432 | tf_op jit(solution)/shard_map/pallas_call | solution.py:236
  15.5 5.3 %collective-permute-done.1.refs_2_.refs_1_ = bf16[768,512]{1,0:T(8,128)(2,1)S(1)} collective-permute-done((bf16[768,512]{1,0:T(8,128)(2,1)}, bf16[768,512]{1,0:T(8,128)(2,1)S(1)}, u32[]{:S(2)}, u32[]{:S(2)}) %collective-permute-start.1) | collective-permute-done | bytes 786464 | tf_op jit(solution)/shard_map/ppermute | solution.py:263
  20.8 3.6 %collective-permute-done.2.refs_3_.refs_2_ = bf16[768,512]{1,0:T(8,128)(2,1)S(1)} collective-permute-done((bf16[768,512]{1,0:T(8,128)(2,1)}, bf16[768,512]{1,0:T(8,128)(2,1)S(1)}, u32[]{:S(2)}, u32[]{:S(2)}) %collective-permute-start.2) | collective-permute-done | bytes 786464 | tf_op jit(solution)/shard_map/ppermute | solution.py:263
  24.4 1.0 %collective-permute-start.6 = (bf16[768,512]{1,0:T(8,128)(2,1)S(1)}, bf16[768,512]{1,0:T(8,128)(2,1)S(1)}, u32[]{:S(2)}, u32[]{:S(2)}) collective-permute-start(bf16[768,512]{1,0:T(8,128)(2,1)S(1)} %collective-permute-done.2.refs_3_.refs_2_), channel_id=1, source_target_pairs={{0,1},{1,0},{2,3},{3,2},{4,5},{5,4},{6,7},{7,6},{8,9},{9,8},{10,11... | collective-permute-start | bytes 2359304 | tf_op jit(solution)/shard_map/ppermute | solution.py:266
  26.6 3.0 %shard_map.30 = (f32[12,768]{1,0:T(8,128)S(1)}, f32[6,768]{1,0:T(8,128)S(1)}) custom-call(s32[1]{0:T(128)S(6)} %copy.3.refs_0_, bf16[768,512]{1,0:T(8,128)(2,1)S(1)} %copy-done.1, bf16[768,512]{1,0:T(8,128)(2,1)S(1)} %collective-permute-done.1.refs_2_.refs_1_, bf16[768,512]{1,0:T(8,128)(2,1)S(1)} %collective-permute-done.2.refs_3_.refs_2_, ...), custom_call_target="tpu_custom_call" | custom-call | flops 1811939328 | bytes 2359296 | tf_op jit(solution)/shard_map/pallas_call | solution.py:236
  29.6 2.8 %shard_map.31 = (f32[12,768]{1,0:T(8,128)S(1)}, f32[6,768]{1,0:T(8,128)S(1)}) custom-call(s32[1]{0:T(128)S(6)} %copy.3.refs_0_, bf16[768,512]{1,0:T(8,128)(2,1)S(1)} %collective-permute-done.1.refs_2_.refs_1_, bf16[768,512]{1,0:T(8,128)(2,1)S(1)} %collective-permute-done.2.refs_3_.refs_2_, bf16[768,512]{1,0:T(8,128)(2,1)S(1)} %collective-permute-done.5.refs_3_.refs_6_, ...), custom_call_target="tpu_custom_call" | custom-call | flops 1811939328 | bytes 3145728 | tf_op jit(solution)/shard_map/pallas_call | solution.py:236
  32.4 5.9 %collective-permute-done.4.refs_4_ = bf16[768,512]{1,0:T(8,128)(2,1)S(1)} collective-permute-done((bf16[768,512]{1,0:T(8,128)(2,1)S(1)}, bf16[768,512]{1,0:T(8,128)(2,1)S(1)}, u32[]{:S(2)}, u32[]{:S(2)}) %collective-permute-start.4) | collective-permute-done | bytes 786464 | tf_op jit(solution)/shard_map/ppermute | solution.py:263
  38.4 4.2 %collective-permute-start.7 = (bf16[768,512]{1,0:T(8,128)(2,1)S(1)}, bf16[768,512]{1,0:T(8,128)(2,1)S(1)}, u32[]{:S(2)}, u32[]{:S(2)}) collective-permute-start(bf16[768,512]{1,0:T(8,128)(2,1)S(1)} %collective-permute-done.4.refs_4_), channel_id=1, source_target_pairs={{54,0},{27,1},{48,2},{29,3},{50,4},{31,5},{52,6},{25,7},{62,8},{19... | collective-permute-start | bytes 2359304 | tf_op jit(solution)/shard_map/ppermute | solution.py:263
  42.6 8.8 %shard_map.32 = (f32[12,768]{1,0:T(8,128)S(1)}, f32[6,768]{1,0:T(8,128)S(1)}) custom-call(s32[1]{0:T(128)S(6)} %copy.3.refs_0_, bf16[768,512]{1,0:T(8,128)(2,1)S(1)} %copy-done.1, bf16[768,512]{1,0:T(8,128)(2,1)S(1)} %collective-permute-done.1.refs_2_.refs_1_, bf16[768,512]{1,0:T(8,128)(2,1)S(1)} %collective-permute-done.2.refs_3_.refs_2_, ...), custom_call_target="tpu_custom_call" | custom-call | flops 6039797760 | bytes 6291456 | tf_op jit(solution)/shard_map/pallas_call | solution.py:236
  51.6 2.3 %collective-permute-start.9 = (f32[6,768]{1,0:T(8,128)S(1)}, f32[6,768]{1,0:T(8,128)S(1)}, u32[]{:S(2)}, u32[]{:S(2)}) collective-permute-start(f32[6,768]{1,0:T(8,128)S(1)} %get-tuple-element.56), channel_id=1, source_target_pairs={{0,1},{1,0},{2,3},{3,2},{4,5},{5,4},{6,7},{7,6},{8,9},{9,8},{10,11... | collective-permute-start | bytes 55304 | tf_op jit(solution)/shard_map/ppermute | solution.py:289
  54.7 3.4 %shard_map.33 = (f32[2,768]{1,0:T(2,128)S(1)}, f32[2,768]{1,0:T(2,128)S(1)}, f32[2,768]{1,0:T(2,128)S(1)}, f32[2,768]{1,0:T(2,128)S(1)}, f32[2,768]{1,0:T(2,128)S(1)}, /*index=5*/f32[2,768]{1,0:T(2,128)S(1)}) custom-call(s32[1]{0:T(128)S(6)} %copy.3.refs_0_, bf16[768,512]{1,0:T(8,128)(2,1)S(1)} %copy-done.1, ...), custom_call_target="tpu_custom_call" | custom-call | flops 2415919104 | bytes 3932160 | tf_op jit(solution)/shard_map/pallas_call | solution.py:236
  58.2 2.9 %collective-permute-start.10 = (f32[2,768]{1,0:T(2,128)S(1)}, f32[2,768]{1,0:T(2,128)S(1)}, u32[]{:S(2)}, u32[]{:S(2)}) collective-permute-start(f32[2,768]{1,0:T(2,128)S(1)} %get-tuple-element.58), channel_id=1, source_target_pairs={{96,0},{57,1},{98,2},{59,3},{100,4},{61,5},{102,6},{63,7},{104,8},... | collective-permute-start | bytes 18440 | tf_op jit(solution)/shard_map/ppermute | solution.py:294
  61.1 2.1 %collective-permute-start.11 = (f32[2,768]{1,0:T(2,128)S(1)}, f32[2,768]{1,0:T(2,128)S(1)}, u32[]{:S(2)}, u32[]{:S(2)}) collective-permute-start(f32[2,768]{1,0:T(2,128)S(1)} %get-tuple-element.59), channel_id=1, source_target_pairs={{22,0},{3,1},{16,2},{5,3},{18,4},{7,5},{20,6},{1,7},{30,8},{11,9},... | collective-permute-start | bytes 18440 | tf_op jit(solution)/shard_map/ppermute | solution.py:294
  63.2 2.3 %collective-permute-start.12 = (f32[2,768]{1,0:T(2,128)S(1)}, f32[2,768]{1,0:T(2,128)S(1)}, u32[]{:S(2)}, u32[]{:S(2)}) collective-permute-start(f32[2,768]{1,0:T(2,128)S(1)} %get-tuple-element.60), channel_id=1, source_target_pairs={{64,0},{73,1},{66,2},{75,3},{68,4},{77,5},{70,6},{79,7},{72,8},{65... | collective-permute-start | bytes 18440 | tf_op jit(solution)/shard_map/ppermute | solution.py:294
  65.4 3.7 %collective-permute-start.14 = (f32[2,768]{1,0:T(2,128)S(1)}, f32[2,768]{1,0:T(2,128)S(1)}, u32[]{:S(2)}, u32[]{:S(2)}) collective-permute-start(f32[2,768]{1,0:T(2,128)S(1)} %get-tuple-element.62), channel_id=1, source_target_pairs={{58,0},{95,1},{60,2},{89,3},{62,4},{91,5},{56,6},{93,7},{50,8},{87... | collective-permute-start | bytes 18440 | tf_op jit(solution)/shard_map/ppermute | solution.py:294
  69.6 4.1 %collective-permute-done.14 = f32[2,768]{1,0:T(2,128)S(1)} collective-permute-done((f32[2,768]{1,0:T(2,128)S(1)}, f32[2,768]{1,0:T(2,128)S(1)}, u32[]{:S(2)}, u32[]{:S(2)}) %collective-permute-start.14) | collective-permute-done | bytes 6176 | tf_op jit(solution)/shard_map/ppermute | solution.py:294
  73.7 1.2 %collective-permute-done.15 = f32[2,768]{1,0:T(2,128)S(1)} collective-permute-done((f32[2,768]{1,0:T(2,128)S(1)}, f32[2,768]{1,0:T(2,128)S(1)}, u32[]{:S(2)}, u32[]{:S(2)}) %collective-permute-start.15) | collective-permute-done | bytes 6176 | tf_op jit(solution)/shard_map/ppermute | solution.py:295
  (22 shorter events, 3.4 us)
Async XLA Ops:
  0.0 3.5 %collective-permute-start = (f32[384,512]{1,0:T(8,128)}, f32[384,512]{1,0:T(8,128)S(1)}, u32[]{:S(2)}, u32[]{:S(2)}) collective-permute-start(f32[384,512]{1,0:T(8,128)} %own_ref.1), channel_id=1, source_target_pairs={{0,1},{1,0},{2,3},{3,2},{4,5},{5,4},{6,7},{7,6},{8,9},{9,8},{10,11... | collective-permute-start | bytes 2359304 | tf_op jit(solution)/shard_map/ppermute | solution.py:257
  3.5 0.9 %copy-start.2 = (f32[384,512]{1,0:T(8,128)}, f32[384,512]{1,0:T(8,128)S(1)}, u32[]{:S(2)}) copy-start(f32[384,512]{1,0:T(8,128)S(1)} %collective-permute-done.other_ref) | copy-start | bytes 2359300
  7.2 13.6 %collective-permute-start.1 = (bf16[768,512]{1,0:T(8,128)(2,1)}, bf16[768,512]{1,0:T(8,128)(2,1)S(1)}, u32[]{:S(2)}, u32[]{:S(2)}) collective-permute-start(bf16[768,512]{1,0:T(8,128)(2,1)} %shard_map.28.refs_1_), channel_id=1, source_target_pairs={{32,0},{113,1},{34,2},{115,3},{36,4},{117,5},{38,6},{119,7},{40,8}... | collective-permute-start | bytes 2359304 | tf_op jit(solution)/shard_map/ppermute | solution.py:263
  10.7 13.7 %collective-permute-start.2 = (bf16[768,512]{1,0:T(8,128)(2,1)}, bf16[768,512]{1,0:T(8,128)(2,1)S(1)}, u32[]{:S(2)}, u32[]{:S(2)}) collective-permute-start(bf16[768,512]{1,0:T(8,128)(2,1)} %shard_map.28.refs_1_), channel_id=1, source_target_pairs={{26,0},{7,1},{28,2},{1,3},{30,4},{3,5},{24,6},{5,7},{18,8},{15,9},... | collective-permute-start | bytes 2359304 | tf_op jit(solution)/shard_map/ppermute | solution.py:263
  13.0 1.1 %copy-start = (bf16[768,512]{1,0:T(8,128)(2,1)S(1)}, bf16[768,512]{1,0:T(8,128)(2,1)}, u32[]{:S(2)}) copy-start(bf16[768,512]{1,0:T(8,128)(2,1)} %shard_map.28.refs_1_) | copy-start | bytes 2359300
  14.2 12.4 %copy-start.1 = (bf16[768,512]{1,0:T(8,128)(2,1)S(1)}, bf16[768,512]{1,0:T(8,128)(2,1)}, u32[]{:S(2)}) copy-start(bf16[768,512]{1,0:T(8,128)(2,1)} %shard_map.28.refs_1_) | copy-start | bytes 2359300
  24.4 5.2 %collective-permute-start.6 = (bf16[768,512]{1,0:T(8,128)(2,1)S(1)}, bf16[768,512]{1,0:T(8,128)(2,1)S(1)}, u32[]{:S(2)}, u32[]{:S(2)}) collective-permute-start(bf16[768,512]{1,0:T(8,128)(2,1)S(1)} %collective-permute-done.2.refs_3_.refs_2_), channel_id=1, source_target_pairs={{0,1},{1,0},{2,3},{3,2},{4,5},{5,4},{6,7},{7,6},{8,9},{9,8},{10,11... | collective-permute-start | bytes 2359304 | tf_op jit(solution)/shard_map/ppermute | solution.py:266
  25.4 4.2 %collective-permute-start.5 = (bf16[768,512]{1,0:T(8,128)(2,1)S(1)}, bf16[768,512]{1,0:T(8,128)(2,1)S(1)}, u32[]{:S(2)}, u32[]{:S(2)}) collective-permute-start(bf16[768,512]{1,0:T(8,128)(2,1)S(1)} %collective-permute-done.1.refs_2_.refs_1_), channel_id=1, source_target_pairs={{0,1},{1,0},{2,3},{3,2},{4,5},{5,4},{6,7},{7,6},{8,9},{9,8},{10,11... | collective-permute-start | bytes 2359304 | tf_op jit(solution)/shard_map/ppermute | solution.py:266
  25.4 12.9 %collective-permute-start.4 = (bf16[768,512]{1,0:T(8,128)(2,1)S(1)}, bf16[768,512]{1,0:T(8,128)(2,1)S(1)}, u32[]{:S(2)}, u32[]{:S(2)}) collective-permute-start(bf16[768,512]{1,0:T(8,128)(2,1)S(1)} %collective-permute-done.1.refs_2_.refs_1_), channel_id=1, source_target_pairs={{32,0},{113,1},{34,2},{115,3},{36,4},{117,5},{38,6},{119,7},{40,8}... | collective-permute-start | bytes 2359304 | tf_op jit(solution)/shard_map/ppermute | solution.py:263
  26.2 16.4 %collective-permute-start.3 = (bf16[768,512]{1,0:T(8,128)(2,1)S(1)}, bf16[768,512]{1,0:T(8,128)(2,1)S(1)}, u32[]{:S(2)}, u32[]{:S(2)}) collective-permute-start(bf16[768,512]{1,0:T(8,128)(2,1)S(1)} %collective-permute-done.2.refs_3_.refs_2_), channel_id=1, source_target_pairs={{24,0},{7,1},{26,2},{1,3},{28,4},{3,5},{30,6},{5,7},{16,8},{15,9},... | collective-permute-start | bytes 2359304 | tf_op jit(solution)/shard_map/ppermute | solution.py:263
  38.4 4.2 %collective-permute-start.8 = (bf16[768,512]{1,0:T(8,128)(2,1)S(1)}, bf16[768,512]{1,0:T(8,128)(2,1)S(1)}, u32[]{:S(2)}, u32[]{:S(2)}) collective-permute-start(bf16[768,512]{1,0:T(8,128)(2,1)S(1)} %collective-permute-done.4.refs_4_), channel_id=1, source_target_pairs={{0,1},{1,0},{2,3},{3,2},{4,5},{5,4},{6,7},{7,6},{8,9},{9,8},{10,11... | collective-permute-start | bytes 2359304 | tf_op jit(solution)/shard_map/ppermute | solution.py:266
  38.4 13.2 %collective-permute-start.7 = (bf16[768,512]{1,0:T(8,128)(2,1)S(1)}, bf16[768,512]{1,0:T(8,128)(2,1)S(1)}, u32[]{:S(2)}, u32[]{:S(2)}) collective-permute-start(bf16[768,512]{1,0:T(8,128)(2,1)S(1)} %collective-permute-done.4.refs_4_), channel_id=1, source_target_pairs={{54,0},{27,1},{48,2},{29,3},{50,4},{31,5},{52,6},{25,7},{62,8},{19... | collective-permute-start | bytes 2359304 | tf_op jit(solution)/shard_map/ppermute | solution.py:263
  51.6 3.1 %collective-permute-start.9 = (f32[6,768]{1,0:T(8,128)S(1)}, f32[6,768]{1,0:T(8,128)S(1)}, u32[]{:S(2)}, u32[]{:S(2)}) collective-permute-start(f32[6,768]{1,0:T(8,128)S(1)} %get-tuple-element.56), channel_id=1, source_target_pairs={{0,1},{1,0},{2,3},{3,2},{4,5},{5,4},{6,7},{7,6},{8,9},{9,8},{10,11... | collective-permute-start | bytes 55304 | tf_op jit(solution)/shard_map/ppermute | solution.py:289
  58.2 10.9 %collective-permute-start.10 = (f32[2,768]{1,0:T(2,128)S(1)}, f32[2,768]{1,0:T(2,128)S(1)}, u32[]{:S(2)}, u32[]{:S(2)}) collective-permute-start(f32[2,768]{1,0:T(2,128)S(1)} %get-tuple-element.58), channel_id=1, source_target_pairs={{96,0},{57,1},{98,2},{59,3},{100,4},{61,5},{102,6},{63,7},{104,8},... | collective-permute-start | bytes 18440 | tf_op jit(solution)/shard_map/ppermute | solution.py:294
  61.1 8.0 %collective-permute-start.11 = (f32[2,768]{1,0:T(2,128)S(1)}, f32[2,768]{1,0:T(2,128)S(1)}, u32[]{:S(2)}, u32[]{:S(2)}) collective-permute-start(f32[2,768]{1,0:T(2,128)S(1)} %get-tuple-element.59), channel_id=1, source_target_pairs={{22,0},{3,1},{16,2},{5,3},{18,4},{7,5},{20,6},{1,7},{30,8},{11,9},... | collective-permute-start | bytes 18440 | tf_op jit(solution)/shard_map/ppermute | solution.py:294
  63.2 6.4 %collective-permute-start.12 = (f32[2,768]{1,0:T(2,128)S(1)}, f32[2,768]{1,0:T(2,128)S(1)}, u32[]{:S(2)}, u32[]{:S(2)}) collective-permute-start(f32[2,768]{1,0:T(2,128)S(1)} %get-tuple-element.60), channel_id=1, source_target_pairs={{64,0},{73,1},{66,2},{75,3},{68,4},{77,5},{70,6},{79,7},{72,8},{65... | collective-permute-start | bytes 18440 | tf_op jit(solution)/shard_map/ppermute | solution.py:294
  65.4 4.1 %collective-permute-start.13 = (f32[2,768]{1,0:T(2,128)S(1)}, f32[2,768]{1,0:T(2,128)S(1)}, u32[]{:S(2)}, u32[]{:S(2)}) collective-permute-start(f32[2,768]{1,0:T(2,128)S(1)} %get-tuple-element.61), channel_id=1, source_target_pairs={{14,0},{5,1},{8,2},{7,3},{10,4},{1,5},{12,6},{3,7},{6,8},{13,9},{0... | collective-permute-start | bytes 18440 | tf_op jit(solution)/shard_map/ppermute | solution.py:294
  65.4 8.2 %collective-permute-start.14 = (f32[2,768]{1,0:T(2,128)S(1)}, f32[2,768]{1,0:T(2,128)S(1)}, u32[]{:S(2)}, u32[]{:S(2)}) collective-permute-start(f32[2,768]{1,0:T(2,128)S(1)} %get-tuple-element.62), channel_id=1, source_target_pairs={{58,0},{95,1},{60,2},{89,3},{62,4},{91,5},{56,6},{93,7},{50,8},{87... | collective-permute-start | bytes 18440 | tf_op jit(solution)/shard_map/ppermute | solution.py:294
  73.7 1.2 %collective-permute-start.15 = (f32[2,768]{1,0:T(2,128)S(1)}, f32[2,768]{1,0:T(2,128)S(1)}, u32[]{:S(2)}, u32[]{:S(2)}) collective-permute-start(f32[2,768]{1,0:T(2,128)S(1)} %maximum_maximum_fusion), channel_id=1, source_target_pairs={{0,1},{1,0},{2,3},{3,2},{4,5},{5,4},{6,7},{7,6},{8,9},{9,8},{10,11... | collective-permute-start | bytes 18440 | tf_op jit(solution)/shard_map/ppermute | solution.py:295

commit v3 on v2

--- a/solution.py
+++ b/solution.py
@@ -12,16 +12,17 @@
 AXES = ("row", "col")
 SIDE = 4
 HELD = (
-    ((0, 0, 0), (0, 1, 0), (3, 0, 1), (0, 2, 0), (2, 0, 1), (1, 3, 3)),
-    ((0, 0, 0), (1, 3, 0), (0, 0, 3), (2, 2, 0), (0, 0, 2), (1, 2, 1)),
+    ((0, 0, 0), (0, 1, 1), (0, 0, 3), (3, 1, 1), (0, 0, 2), (3, 1, 2)),
+    ((0, 0, 0), (3, 3, 0), (1, 0, 0), (3, 2, 0), (2, 0, 0), (2, 2, 0)),
 )
 SOURCE = (None, 0, 0, 1, 2, 3)
 MOVED = 5
-SHARED = (1, 2, 3)
+SHARED = (1, 2, 3, 4)
 FIRST = ((1, 0), (2, 0), (2, 1))
 SECOND = ((1, 6), (2, 6), (2, 7))
-THIRD = ((3, 0), (3, 6), (4, 0), (4, 1), (4, 2), (4, 6), (4, 7), (4, 3), (3, 8), (4, 8))
-LAST = ((5, 0), (5, 1), (5, 2), (5, 4))
+THIRD = ((3, 0), (3, 1), (3, 2), (3, 6), (3, 7), (4, 0), (4, 7))
+FOURTH = ((3, 8), (4, 8), (4, 9))
+LAST = ((5, 1), (5, 4), (5, 6), (5, 7), (5, 9))
 LOW = -3.0
 
 
@@ -59,7 +60,7 @@
 
 def check_cover():
     seen = {(0, 0, 0)}
-    for a, b in FIRST + SECOND + THIRD + LAST:
+    for a, b in FIRST + SECOND + THIRD + FOURTH + LAST:
         for core in (0, 1):
             diff = minus(offset_of(a, core), offset_of(b, core))
             seen |= {diff, minus((0, 0, 0), diff)}
@@ -72,15 +73,23 @@
     return any(minus(offset_of(a, core), offset_of(b, core)) in steps for core in (0, 1))
 
 
-def normalize_kernel(own_ref, other_ref, o_ref):
-    rows, length = own_ref.shape
-    for at, ref in ((0, own_ref), (rows, other_ref)):
-        x = ref[...]
-        average = jnp.sum(x, axis=1, keepdims=True) * (1.0 / length)
-        centered = x - average
-        power = jnp.sum(centered * centered, axis=1, keepdims=True) * (1.0 / length)
-        spread_inv = lax.rsqrt(power + 1e-05) * (1.0 / math.sqrt(length))
-        o_ref[at : at + rows] = (centered * spread_inv).astype(jnp.bfloat16)
+def normalize(x):
+    length = x.shape[1]
+    average = jnp.sum(x, axis=1, keepdims=True) * (1.0 / length)
+    centered = x - average
+    power = jnp.sum(centered * centered, axis=1, keepdims=True) * (1.0 / length)
+    spread_inv = lax.rsqrt(power + 1e-05) * (1.0 / math.sqrt(length))
+    return (centered * spread_inv).astype(jnp.bfloat16)
+
+
+def own_kernel(x_ref, o_ref):
+    o_ref[...] = normalize(x_ref[...])
+
+
+def both_kernel(own_ref, other_ref, o_ref):
+    rows = own_ref.shape[0]
+    o_ref[:rows] = own_ref[...]
+    o_ref[rows:] = normalize(other_ref[...])
 
 
 def here():
@@ -105,7 +114,7 @@
     return order * size + jnp.where(at >= size, at - size, at)
 
 
-def phase_kernel(names, pairs, diag, n_prev, n_out, *refs):
+def phase_kernel(names, pairs, diag, n_prev, each, *refs):
     exclude_ref = refs[0]
     blocks = dict(zip(names, refs[1 : 1 + len(names)]))
     rest = refs[1 + len(names) :]
@@ -192,23 +201,26 @@
         if name in col_names:
             at = 2 * col_names.index(name)
             parts.append(folded[at : at + 2])
-        if n_prev and (name <= MOVED or not isinstance(n_out, tuple)):
+        if n_prev and name <= MOVED:
             parts.append(prev[0][2 * name : 2 * name + 2])
-        elif n_prev and name > MOVED:
-            parts.append(prev[1][2 * (name - MOVED - 1) : 2 * (name - MOVED)])
-        if n_out == "each" and name in SHARED:
-            at = 2 * SHARED.index(name)
+        elif n_prev:
+            at = 2 * SHARED.index(name - MOVED)
             parts.append(prev[1][at : at + 2])
         return functools.reduce(jnp.maximum, parts) if parts else jnp.full((2, size), LOW)
 
-    if n_out == "each":
-        for name in range(MOVED + 1):
+    for name in range(MOVED + 1):
+        if each:
             outs[name][...] = result(name)
-    else:
-        for name in range(MOVED + 1):
+        else:
             outs[0][2 * name : 2 * name + 2] = result(name)
-        for i, name in enumerate(SHARED):
-            outs[1][2 * i : 2 * i + 2] = result(MOVED + name)
+    for i, name in enumerate(SHARED):
+        outs[-1][2 * i : 2 * i + 2] = result(MOVED + name)
+
+
+def merge_kernel(*refs):
+    mine, other, outs = refs[: len(SHARED)], refs[len(SHARED)], refs[len(SHARED) + 1 :]
+    for i in range(len(SHARED)):
+        outs[i][...] = jnp.maximum(mine[i][...], other[2 * i : 2 * i + 2])
 
 
 SMEM = pl.BlockSpec(memory_space=pltpu.SMEM)
@@ -225,17 +237,14 @@
         names = sorted({name for pair in pairs for name in pair} | ({0} if diag else set()))
         rows_of = {a for a, _ in pairs} | ({0} if diag else set())
         cols_of = {b for _, b in pairs}
-        if each:
-            out_shape = [jax.ShapeDtypeStruct((2, size), float32)] * (MOVED + 1)
-        else:
-            out_shape = [
-                jax.ShapeDtypeStruct((2 * MOVED + 2, size), float32),
-                jax.ShapeDtypeStruct((2 * len(SHARED), size), float32),
-            ]
+        part = jax.ShapeDtypeStruct((2, size), float32)
+        own_part = jax.ShapeDtypeStruct((2 * MOVED + 2, size), float32)
+        out_shape = [part] * (MOVED + 1) if each else [own_part]
+        out_shape.append(jax.ShapeDtypeStruct((2 * len(SHARED), size), float32))
         count = len(pairs) + diag
         return pl.pallas_call(
             functools.partial(
-                phase_kernel, names, pairs, diag, len(prev), "each" if each else (2,)
+                phase_kernel, names, pairs, diag, len(prev), each
             ),
             out_shape=out_shape,
             in_specs=[SMEM] + [VMEM] * (len(names) + len(prev)),
@@ -244,17 +253,29 @@
                 pltpu.VMEM((2 * len(rows_of), size, 128), float32),
                 pltpu.VMEM((2 * max(len(cols_of), 1), 8, size), float32),
             ],
-            compiler_params=pltpu.CompilerParams(vmem_limit_bytes=40 * 2**20),
+            compiler_params=pltpu.CompilerParams(vmem_limit_bytes=20 * 2**20),
             cost_estimate=pl.CostEstimate(
-                flops=2 * count * size * size * length,
-                bytes_accessed=len(names) * 2 * size * length,
+                flops=8 * 2 * count * size * size * length,
+                bytes_accessed=2 * size * len(names),
                 transcendentals=0,
             ),
         )(exclusion, *[blocks[name] for name in names], *prev)
 
+    other = lax.ppermute(segments, AXES, across())
+    own = pl.pallas_call(
+        own_kernel,
+        out_shape=jax.ShapeDtypeStruct((rows, length), jnp.bfloat16),
+        in_specs=[VMEM],
+        out_specs=VMEM,
+        compiler_params=pltpu.CompilerParams(vmem_limit_bytes=8 * 2**20),
+    )(segments)
     block = pl.pallas_call(
-        normalize_kernel, out_shape=jax.ShapeDtypeStruct((size, length), jnp.bfloat16)
-    )(segments, lax.ppermute(segments, AXES, across()))
+        both_kernel,
+        out_shape=jax.ShapeDtypeStruct((size, length), jnp.bfloat16),
+        in_specs=[VMEM, VMEM],
+        out_specs=VMEM,
+        compiler_params=pltpu.CompilerParams(vmem_limit_bytes=8 * 2**20),
+    )(own, other)
 
     blocks = {0: block}
 
@@ -271,27 +292,36 @@
 
     move(1)
     move(2)
-    best = phase((), blocks, (), diag=True)
-    best = after(1, best)
-    best = after(2, best)
     move(3)
     move(4)
     share(1)
     share(2)
-    best = phase(FIRST, blocks, best)
+    best = phase(FIRST, blocks, (), diag=True)
     best = phase(SECOND, blocks, best)
     best = after(3, best)
-    best = after(4, best)
     move(5)
     share(3)
+    share(4)
     best = phase(THIRD, blocks, best)
+    best = phase(FOURTH, blocks, best)
     best = after(5, best)
-    parts = phase(LAST, blocks, (best[0], lax.ppermute(best[1], AXES, across())), each=True)
-
-    mine = parts[0]
-    for i in range(1, MOVED + 1):
+    *parts, lent = phase(LAST, blocks, best, each=True)
+
+    def give(i, part):
         back = tuple(minus((0, 0, 0), HELD[c][i]) for c in (0, 1))
-        mine = jnp.maximum(mine, lax.ppermute(parts[i], AXES, moves(back)))
+        return lax.ppermute(part, AXES, moves(back))
+
+    lent = lax.ppermute(lent, AXES, across())
+    mine = jnp.maximum(parts[0], give(5, parts[5]))
+    merged = pl.pallas_call(
+        merge_kernel,
+        out_shape=[jax.ShapeDtypeStruct((2, size), float32)] * len(SHARED),
+        in_specs=[VMEM] * (len(SHARED) + 1),
+        out_specs=[VMEM] * len(SHARED),
+        compiler_params=pltpu.CompilerParams(vmem_limit_bytes=4 * 2**20),
+    )(*[parts[i] for i in SHARED], lent)
+    for i in (4, 3, 2, 1):
+        mine = jnp.maximum(mine, give(i, merged[i - 1]))
     other = lax.ppermute(mine, AXES, across())
     return 1.0 - jnp.maximum(mine[:, :rows], other[:, rows:])
 

time: 76.3 us -> 68.9 us (0.903)
  waiting for transfers between devices: 23.8 us -> 13.8 us
  starting transfers between devices: 26.3 us -> 31.8 us
  Pallas kernels: 22.1 us -> 20.7 us
  local copies, waits for them, and re-layouts: 2.02 us -> 1.13 us
    ppermute x3 -> x4, starting transfers between devices: 1.02 us -> 7.8 us  [share(): blocks[MOVED + i] = lax.ppermute(blocks[i], AXES, across())]
    ppermute x7, waiting for transfers between devices: 7.49 us -> 1.49 us  [the longest x5 0.76 us: give(): return lax.ppermute(part, AXES, moves(back))]
    ppermute x5, starting transfers between devices: 10.6 us -> 6.68 us  [move(): blocks[i] = lax.ppermute(blocks[SOURCE[i]], AXES, moves(hops))]
    ppermute x1, starting transfers between devices: 0.09 us -> 3.95 us  [shards(): other = lax.ppermute(mine, AXES, across())]
    ppermute x5, waiting for transfers between devices: 15.1 us -> 11.5 us  [move(): blocks[i] = lax.ppermute(blocks[SOURCE[i]], AXES, moves(hops))]
    pallas_call x1 -> x3, Pallas kernels: 2.73 us -> 0.53 us  [the longest x1 0.26 us: shards(): pl.pallas_call(both_kernel, out_shape=jax.ShapeDtypeStruct((size, length)...]
    ppermute x7, starting transfers between devices: 14.6 us -> 13.4 us  [the longest x5 11.9 us: give(): return lax.ppermute(part, AXES, moves(back))]
    unnamed x6 -> x2, local copies, waits for them, and re-layouts: 2.02 us -> 1.13 us
  transfers between devices with their start and end apart: 16 -> 17, of which waited for: 9 -> 5; matrix products, arithmetic and copies ran while one was open for 0% -> 0% of each run, Pallas kernels for 21% -> 23%
where the time goes in v3:
time: 68.9 us; the launch traced here: 68.8 us
  starting transfers between devices  31.8 us (46%)
  Pallas kernels  20.7 us (30%)
  waiting for transfers between devices  13.8 us (20%)
  local copies, waits for them, and re-layouts  1.13 us (2%)
  between operations  0.72 us (1%)
    pallas_call x5, Pallas kernels, phase(): pl.pallas_call(functools.partial(phase_kernel, names, pairs, diag, len(pr...  20.1 us
    ppermute x5, starting transfers between devices, give(): return lax.ppermute(part, AXES, moves(back))  11.9 us
    ppermute x5, waiting for transfers between devices, move(): blocks[i] = lax.ppermute(blocks[SOURCE[i]], AXES, moves(hops))  11.5 us
    ppermute x4, starting transfers between devices, share(): blocks[MOVED + i] = lax.ppermute(blocks[i], AXES, across())  7.8 us
    ppermute x5, starting transfers between devices, move(): blocks[i] = lax.ppermute(blocks[SOURCE[i]], AXES, moves(hops))  6.68 us
    ppermute x1, starting transfers between devices, shards(): other = lax.ppermute(mine, AXES, across())  3.95 us
    ppermute x1, starting transfers between devices, shards(): other = lax.ppermute(segments, AXES, across())  1.42 us
  transfers between devices with their start and end apart: 17, of which 5 were waited for; matrix products, arithmetic and copies ran while one was open for 0% of the time, Pallas kernels for 23%

profile of v3, /device:TPU:1, one launch (start us, length us, event | category | flops | bytes accessed | tf_op | source)
XLA Modules:
  0.0 68.8 jit_solution(2251670946772519903)
XLA Ops:
  0.0 1.4 %collective-permute-start = (f32[384,512]{1,0:T(8,128)}, f32[384,512]{1,0:T(8,128)S(1)}, u32[]{:S(2)}, u32[]{:S(2)}) collective-permute-start(f32[384,512]{1,0:T(8,128)} %x_ref.1), channel_id=1, source_target_pairs={{0,1},{1,0},{2,3},{3,2},{4,5},{5,4},{6,7},{7,6},{8,9},{9,8},{10,11... | collective-permute-start | bytes 2359304 | tf_op jit(solution)/shard_map/ppermute | solution.py:264
  1.4 1.1 %copy-done = f32[384,512]{1,0:T(8,128)S(1)} copy-done((f32[384,512]{1,0:T(8,128)S(1)}, f32[384,512]{1,0:T(8,128)}, u32[]{:S(2)}) %copy-start) | copy-done | bytes 786456
  2.8 0.7 %collective-permute-done.other_ref = f32[384,512]{1,0:T(8,128)S(1)} collective-permute-done((f32[384,512]{1,0:T(8,128)}, f32[384,512]{1,0:T(8,128)S(1)}, u32[]{:S(2)}, u32[]{:S(2)}) %collective-permute-start) | collective-permute-done | bytes 786464 | tf_op jit(solution)/shard_map/ppermute | solution.py:264
  3.8 2.4 %collective-permute-start.1 = (bf16[768,512]{1,0:T(8,128)(2,1)S(1)}, bf16[768,512]{1,0:T(8,128)(2,1)S(1)}, u32[]{:S(2)}, u32[]{:S(2)}) collective-permute-start(bf16[768,512]{1,0:T(8,128)(2,1)S(1)} %shard_map.29.refs_1_), channel_id=1, source_target_pairs={{34,0},{121,1},{36,2},{123,3},{38,4},{125,5},{32,6},{127,7},{42,8}... | collective-permute-start | bytes 2359304 | tf_op jit(solution)/shard_map/ppermute | solution.py:284
  6.2 1.5 %collective-permute-start.2 = (bf16[768,512]{1,0:T(8,128)(2,1)S(1)}, bf16[768,512]{1,0:T(8,128)(2,1)S(1)}, u32[]{:S(2)}, u32[]{:S(2)}) collective-permute-start(bf16[768,512]{1,0:T(8,128)(2,1)S(1)} %shard_map.29.refs_1_), channel_id=1, source_target_pairs={{6,0},{17,1},{0,2},{19,3},{2,4},{21,5},{4,6},{23,7},{14,8},{25,9},... | collective-permute-start | bytes 2359304 | tf_op jit(solution)/shard_map/ppermute | solution.py:284
  8.3 10.0 %collective-permute-done.1.refs_2_.refs_1_ = bf16[768,512]{1,0:T(8,128)(2,1)S(1)} collective-permute-done((bf16[768,512]{1,0:T(8,128)(2,1)S(1)}, bf16[768,512]{1,0:T(8,128)(2,1)S(1)}, u32[]{:S(2)}, u32[]{:S(2)}) %collective-permute-start.1) | collective-permute-done | bytes 786464 | tf_op jit(solution)/shard_map/ppermute | solution.py:284
  18.3 2.1 %collective-permute-start.5 = (bf16[768,512]{1,0:T(8,128)(2,1)S(1)}, bf16[768,512]{1,0:T(8,128)(2,1)S(1)}, u32[]{:S(2)}, u32[]{:S(2)}) collective-permute-start(bf16[768,512]{1,0:T(8,128)(2,1)S(1)} %collective-permute-done.1.refs_2_.refs_1_), channel_id=1, source_target_pairs={{0,1},{1,0},{2,3},{3,2},{4,5},{5,4},{6,7},{7,6},{8,9},{9,8},{10,11... | collective-permute-start | bytes 2359304 | tf_op jit(solution)/shard_map/ppermute | solution.py:287
  20.3 3.7 %collective-permute-start.6 = (bf16[768,512]{1,0:T(8,128)(2,1)S(1)}, bf16[768,512]{1,0:T(8,128)(2,1)S(1)}, u32[]{:S(2)}, u32[]{:S(2)}) collective-permute-start(bf16[768,512]{1,0:T(8,128)(2,1)S(1)} %collective-permute-done.2.refs_3_.refs_2_), channel_id=1, source_target_pairs={{0,1},{1,0},{2,3},{3,2},{4,5},{5,4},{6,7},{7,6},{8,9},{9,8},{10,11... | collective-permute-start | bytes 2359304 | tf_op jit(solution)/shard_map/ppermute | solution.py:287
  24.0 2.5 %collective-permute-start.3 = (bf16[768,512]{1,0:T(8,128)(2,1)S(1)}, bf16[768,512]{1,0:T(8,128)(2,1)S(1)}, u32[]{:S(2)}, u32[]{:S(2)}) collective-permute-start(bf16[768,512]{1,0:T(8,128)(2,1)S(1)} %collective-permute-done.2.refs_3_.refs_2_), channel_id=1, source_target_pairs={{6,0},{17,1},{0,2},{19,3},{2,4},{21,5},{4,6},{23,7},{14,8},{25,9},... | collective-permute-start | bytes 2359304 | tf_op jit(solution)/shard_map/ppermute | solution.py:284
  26.5 4.0 %shard_map.30 = (f32[12,768]{1,0:T(8,128)S(1)}, f32[8,768]{1,0:T(8,128)S(1)}) custom-call(s32[1]{0:T(128)S(6)} %copy.3.refs_0_, bf16[768,512]{1,0:T(8,128)(2,1)S(1)} %shard_map.29.refs_1_, bf16[768,512]{1,0:T(8,128)(2,1)S(1)} %collective-permute-done.1.refs_2_.refs_1_, bf16[768,512]{1,0:T(8,128)(2,1)S(1)} %collective-permute-done.2.refs_3_.refs_2_), custom_call_target="tpu_custom_call" | custom-call | flops 19327352832 | bytes 4608 | tf_op jit(solution)/shard_map/pallas_call | solution.py:245
  30.5 2.8 %shard_map.31 = (f32[12,768]{1,0:T(8,128)S(1)}, f32[8,768]{1,0:T(8,128)S(1)}) custom-call(s32[1]{0:T(128)S(6)} %copy.3.refs_0_, bf16[768,512]{1,0:T(8,128)(2,1)S(1)} %collective-permute-done.1.refs_2_.refs_1_, bf16[768,512]{1,0:T(8,128)(2,1)S(1)} %collective-permute-done.2.refs_3_.refs_2_, ...), custom_call_target="tpu_custom_call" | custom-call | flops 14495514624 | bytes 6144 | tf_op jit(solution)/shard_map/pallas_call | solution.py:245
  33.9 1.5 %collective-permute-done.3.refs_5_.refs_2_ = bf16[768,512]{1,0:T(8,128)(2,1)S(1)} collective-permute-done((bf16[768,512]{1,0:T(8,128)(2,1)S(1)}, bf16[768,512]{1,0:T(8,128)(2,1)S(1)}, u32[]{:S(2)}, u32[]{:S(2)}) %collective-permute-start.3) | collective-permute-done | bytes 786464 | tf_op jit(solution)/shard_map/ppermute | solution.py:284
  35.4 1.8 %collective-permute-start.9 = (bf16[768,512]{1,0:T(8,128)(2,1)S(1)}, bf16[768,512]{1,0:T(8,128)(2,1)S(1)}, u32[]{:S(2)}, u32[]{:S(2)}) collective-permute-start(bf16[768,512]{1,0:T(8,128)(2,1)S(1)} %collective-permute-done.3.refs_5_.refs_2_), channel_id=1, source_target_pairs={{0,1},{1,0},{2,3},{3,2},{4,5},{5,4},{6,7},{7,6},{8,9},{9,8},{10,11... | collective-permute-start | bytes 2359304 | tf_op jit(solution)/shard_map/ppermute | solution.py:287
  37.2 6.0 %shard_map.32 = (f32[12,768]{1,0:T(8,128)S(1)}, f32[8,768]{1,0:T(8,128)S(1)}) custom-call(s32[1]{0:T(128)S(6)} %copy.3.refs_0_, bf16[768,512]{1,0:T(8,128)(2,1)S(1)} %shard_map.29.refs_1_, bf16[768,512]{1,0:T(8,128)(2,1)S(1)} %collective-permute-done.1.refs_2_.refs_1_, bf16[768,512]{1,0:T(8,128)(2,1)S(1)} %collective-permute-done.2.refs_3_.refs_2_, ...), custom_call_target="tpu_custom_call" | custom-call | flops 33822867456 | bytes 10752 | tf_op jit(solution)/shard_map/pallas_call | solution.py:245
  43.3 3.0 %shard_map.33 = (f32[12,768]{1,0:T(8,128)S(1)}, f32[8,768]{1,0:T(8,128)S(1)}) custom-call(s32[1]{0:T(128)S(6)} %copy.3.refs_0_, bf16[768,512]{1,0:T(8,128)(2,1)S(1)} %collective-permute-done.4.refs_4_.refs_1_, bf16[768,512]{1,0:T(8,128)(2,1)S(1)} %collective-permute-done.3.refs_5_.refs_2_, bf16[768,512]{1,0:T(8,128)(2,1)S(1)} %collective-permute-done.8.refs_3_, ...), custom_call_target="tpu_custom_call" | custom-call | flops 14495514624 | bytes 6144 | tf_op jit(solution)/shard_map/pallas_call | solution.py:245
  46.3 4.4 %shard_map.34 = (f32[2,768]{1,0:T(2,128)S(1)}, f32[2,768]{1,0:T(2,128)S(1)}, f32[2,768]{1,0:T(2,128)S(1)}, f32[2,768]{1,0:T(2,128)S(1)}, f32[2,768]{1,0:T(2,128)...) custom-call(s32[1]{0:T(128)S(6)} %copy.3.refs_0_, bf16[768,512]{1,0:T(8,128)(2,1)S(1)} %collective-permute-done.1.refs_2_.refs_1_, ...), custom_call_target="tpu_custom_call" | custom-call | flops 24159191040 | bytes 9216 | tf_op jit(solution)/shard_map/pallas_call | solution.py:245
  50.7 3.2 %collective-permute-start.10 = (f32[2,768]{1,0:T(2,128)S(1)}, f32[2,768]{1,0:T(2,128)S(1)}, u32[]{:S(2)}, u32[]{:S(2)}) collective-permute-start(f32[2,768]{1,0:T(2,128)S(1)} %get-tuple-element.45), channel_id=1, source_target_pairs={{116,0},{73,1},{118,2},{75,3},{112,4},{77,5},{114,6},{79,7},{124,8... | collective-permute-start | bytes 18440 | tf_op jit(solution)/shard_map/ppermute | solution.py:312
  53.9 1.4 %collective-permute-start.12 = (f32[2,768]{1,0:T(2,128)S(1)}, f32[2,768]{1,0:T(2,128)S(1)}, u32[]{:S(2)}, u32[]{:S(2)}) collective-permute-start(f32[2,768]{1,0:T(2,128)S(1)} %get-tuple-element.51), channel_id=1, source_target_pairs={{4,0},{9,1},{6,2},{11,3},{0,4},{13,5},{2,6},{15,7},{12,8},{1,9},{1... | collective-permute-start | bytes 18440 | tf_op jit(solution)/shard_map/ppermute | solution.py:312
  55.3 3.3 %collective-permute-start.13 = (f32[2,768]{1,0:T(2,128)S(1)}, f32[2,768]{1,0:T(2,128)S(1)}, u32[]{:S(2)}, u32[]{:S(2)}) collective-permute-start(f32[2,768]{1,0:T(2,128)S(1)} %get-tuple-element.52), channel_id=1, source_target_pairs={{118,0},{81,1},{112,2},{83,3},{114,4},{85,5},{116,6},{87,7},{126,8... | collective-permute-start | bytes 18440 | tf_op jit(solution)/shard_map/ppermute | solution.py:312
  58.6 4.0 %collective-permute-start.15 = (f32[2,768]{1,0:T(2,128)S(1)}, f32[2,768]{1,0:T(2,128)S(1)}, u32[]{:S(2)}, u32[]{:S(2)}) collective-permute-start(f32[2,768]{1,0:T(2,128)S(1)} %get-tuple-element.54), channel_id=1, source_target_pairs={{102,0},{49,1},{96,2},{51,3},{98,4},{53,5},{100,6},{55,7},{110,8},... | collective-permute-start | bytes 18440 | tf_op jit(solution)/shard_map/ppermute | solution.py:312
  62.6 0.8 %collective-permute-done.15 = f32[2,768]{1,0:T(2,128)S(1)} collective-permute-done((f32[2,768]{1,0:T(2,128)S(1)}, f32[2,768]{1,0:T(2,128)S(1)}, u32[]{:S(2)}, u32[]{:S(2)}) %collective-permute-start.15) | collective-permute-done | bytes 6176 | tf_op jit(solution)/shard_map/ppermute | solution.py:312
  63.4 3.9 %collective-permute-start.16 = (f32[2,768]{1,0:T(2,128)S(1)}, f32[2,768]{1,0:T(2,128)S(1)}, u32[]{:S(2)}, u32[]{:S(2)}) collective-permute-start(f32[2,768]{1,0:T(2,128)S(1)} %maximum_maximum_fusion), channel_id=1, source_target_pairs={{0,1},{1,0},{2,3},{3,2},{4,5},{5,4},{6,7},{7,6},{8,9},{9,8},{10,11... | collective-permute-start | bytes 18440 | tf_op jit(solution)/shard_map/ppermute | solution.py:325
  67.4 0.8 %collective-permute-done.16 = f32[2,768]{1,0:T(2,128)S(1)} collective-permute-done((f32[2,768]{1,0:T(2,128)S(1)}, f32[2,768]{1,0:T(2,128)S(1)}, u32[]{:S(2)}, u32[]{:S(2)}) %collective-permute-start.16) | collective-permute-done | bytes 6176 | tf_op jit(solution)/shard_map/ppermute | solution.py:325
  68.2 0.6 fusion
  (22 shorter events, 1.3 us)
Async XLA Ops:
  0.0 3.5 %collective-permute-start = (f32[384,512]{1,0:T(8,128)}, f32[384,512]{1,0:T(8,128)S(1)}, u32[]{:S(2)}, u32[]{:S(2)}) collective-permute-start(f32[384,512]{1,0:T(8,128)} %x_ref.1), channel_id=1, source_target_pairs={{0,1},{1,0},{2,3},{3,2},{4,5},{5,4},{6,7},{7,6},{8,9},{9,8},{10,11... | collective-permute-start | bytes 2359304 | tf_op jit(solution)/shard_map/ppermute | solution.py:264
  1.4 1.1 %copy-start = (f32[384,512]{1,0:T(8,128)S(1)}, f32[384,512]{1,0:T(8,128)}, u32[]{:S(2)}) copy-start(f32[384,512]{1,0:T(8,128)} %x_ref.1) | copy-start | bytes 2359300
  3.8 14.5 %collective-permute-start.1 = (bf16[768,512]{1,0:T(8,128)(2,1)S(1)}, bf16[768,512]{1,0:T(8,128)(2,1)S(1)}, u32[]{:S(2)}, u32[]{:S(2)}) collective-permute-start(bf16[768,512]{1,0:T(8,128)(2,1)S(1)} %shard_map.29.refs_1_), channel_id=1, source_target_pairs={{34,0},{121,1},{36,2},{123,3},{38,4},{125,5},{32,6},{127,7},{42,8}... | collective-permute-start | bytes 2359304 | tf_op jit(solution)/shard_map/ppermute | solution.py:284
  6.2 14.2 %collective-permute-start.2 = (bf16[768,512]{1,0:T(8,128)(2,1)S(1)}, bf16[768,512]{1,0:T(8,128)(2,1)S(1)}, u32[]{:S(2)}, u32[]{:S(2)}) collective-permute-start(bf16[768,512]{1,0:T(8,128)(2,1)S(1)} %shard_map.29.refs_1_), channel_id=1, source_target_pairs={{6,0},{17,1},{0,2},{19,3},{2,4},{21,5},{4,6},{23,7},{14,8},{25,9},... | collective-permute-start | bytes 2359304 | tf_op jit(solution)/shard_map/ppermute | solution.py:284
  18.3 12.2 %collective-permute-start.5 = (bf16[768,512]{1,0:T(8,128)(2,1)S(1)}, bf16[768,512]{1,0:T(8,128)(2,1)S(1)}, u32[]{:S(2)}, u32[]{:S(2)}) collective-permute-start(bf16[768,512]{1,0:T(8,128)(2,1)S(1)} %collective-permute-done.1.refs_2_.refs_1_), channel_id=1, source_target_pairs={{0,1},{1,0},{2,3},{3,2},{4,5},{5,4},{6,7},{7,6},{8,9},{9,8},{10,11... | collective-permute-start | bytes 2359304 | tf_op jit(solution)/shard_map/ppermute | solution.py:287
  20.3 12.9 %collective-permute-start.4 = (bf16[768,512]{1,0:T(8,128)(2,1)S(1)}, bf16[768,512]{1,0:T(8,128)(2,1)S(1)}, u32[]{:S(2)}, u32[]{:S(2)}) collective-permute-start(bf16[768,512]{1,0:T(8,128)(2,1)S(1)} %collective-permute-done.1.refs_2_.refs_1_), channel_id=1, source_target_pairs={{24,0},{97,1},{26,2},{99,3},{28,4},{101,5},{30,6},{103,7},{16,8},{... | collective-permute-start | bytes 2359304 | tf_op jit(solution)/shard_map/ppermute | solution.py:284
  20.3 10.1 %collective-permute-start.6 = (bf16[768,512]{1,0:T(8,128)(2,1)S(1)}, bf16[768,512]{1,0:T(8,128)(2,1)S(1)}, u32[]{:S(2)}, u32[]{:S(2)}) collective-permute-start(bf16[768,512]{1,0:T(8,128)(2,1)S(1)} %collective-permute-done.2.refs_3_.refs_2_), channel_id=1, source_target_pairs={{0,1},{1,0},{2,3},{3,2},{4,5},{5,4},{6,7},{7,6},{8,9},{9,8},{10,11... | collective-permute-start | bytes 2359304 | tf_op jit(solution)/shard_map/ppermute | solution.py:287
  24.0 11.4 %collective-permute-start.3 = (bf16[768,512]{1,0:T(8,128)(2,1)S(1)}, bf16[768,512]{1,0:T(8,128)(2,1)S(1)}, u32[]{:S(2)}, u32[]{:S(2)}) collective-permute-start(bf16[768,512]{1,0:T(8,128)(2,1)S(1)} %collective-permute-done.2.refs_3_.refs_2_), channel_id=1, source_target_pairs={{6,0},{17,1},{0,2},{19,3},{2,4},{21,5},{4,6},{23,7},{14,8},{25,9},... | collective-permute-start | bytes 2359304 | tf_op jit(solution)/shard_map/ppermute | solution.py:284
  33.3 10.0 %collective-permute-start.8 = (bf16[768,512]{1,0:T(8,128)(2,1)S(1)}, bf16[768,512]{1,0:T(8,128)(2,1)S(1)}, u32[]{:S(2)}, u32[]{:S(2)}) collective-permute-start(bf16[768,512]{1,0:T(8,128)(2,1)S(1)} %collective-permute-done.4.refs_4_.refs_1_), channel_id=1, source_target_pairs={{0,1},{1,0},{2,3},{3,2},{4,5},{5,4},{6,7},{7,6},{8,9},{9,8},{10,11... | collective-permute-start | bytes 2359304 | tf_op jit(solution)/shard_map/ppermute | solution.py:287
  33.5 12.7 %collective-permute-start.7 = (bf16[768,512]{1,0:T(8,128)(2,1)S(1)}, bf16[768,512]{1,0:T(8,128)(2,1)S(1)}, u32[]{:S(2)}, u32[]{:S(2)}) collective-permute-start(bf16[768,512]{1,0:T(8,128)(2,1)S(1)} %collective-permute-done.4.refs_4_.refs_1_), channel_id=1, source_target_pairs={{2,0},{25,1},{4,2},{27,3},{6,4},{29,5},{0,6},{31,7},{10,8},{17,9},... | collective-permute-start | bytes 2359304 | tf_op jit(solution)/shard_map/ppermute | solution.py:284
  35.4 7.8 %collective-permute-start.9 = (bf16[768,512]{1,0:T(8,128)(2,1)S(1)}, bf16[768,512]{1,0:T(8,128)(2,1)S(1)}, u32[]{:S(2)}, u32[]{:S(2)}) collective-permute-start(bf16[768,512]{1,0:T(8,128)(2,1)S(1)} %collective-permute-done.3.refs_5_.refs_2_), channel_id=1, source_target_pairs={{0,1},{1,0},{2,3},{3,2},{4,5},{5,4},{6,7},{7,6},{8,9},{9,8},{10,11... | collective-permute-start | bytes 2359304 | tf_op jit(solution)/shard_map/ppermute | solution.py:287
  50.6 3.3 %collective-permute-start.11 = (f32[8,768]{1,0:T(8,128)S(1)}, f32[8,768]{1,0:T(8,128)S(1)}, u32[]{:S(2)}, u32[]{:S(2)}) collective-permute-start(f32[8,768]{1,0:T(8,128)S(1)} %get-tuple-element.50), channel_id=1, source_target_pairs={{0,1},{1,0},{2,3},{3,2},{4,5},{5,4},{6,7},{7,6},{8,9},{9,8},{10,11... | collective-permute-start | bytes 73736 | tf_op jit(solution)/shard_map/ppermute | solution.py:314
  50.7 11.9 %collective-permute-start.10 = (f32[2,768]{1,0:T(2,128)S(1)}, f32[2,768]{1,0:T(2,128)S(1)}, u32[]{:S(2)}, u32[]{:S(2)}) collective-permute-start(f32[2,768]{1,0:T(2,128)S(1)} %get-tuple-element.45), channel_id=1, source_target_pairs={{116,0},{73,1},{118,2},{75,3},{112,4},{77,5},{114,6},{79,7},{124,8... | collective-permute-start | bytes 18440 | tf_op jit(solution)/shard_map/ppermute | solution.py:312
  53.9 8.7 %collective-permute-start.12 = (f32[2,768]{1,0:T(2,128)S(1)}, f32[2,768]{1,0:T(2,128)S(1)}, u32[]{:S(2)}, u32[]{:S(2)}) collective-permute-start(f32[2,768]{1,0:T(2,128)S(1)} %get-tuple-element.51), channel_id=1, source_target_pairs={{4,0},{9,1},{6,2},{11,3},{0,4},{13,5},{2,6},{15,7},{12,8},{1,9},{1... | collective-permute-start | bytes 18440 | tf_op jit(solution)/shard_map/ppermute | solution.py:312
  55.3 7.3 %collective-permute-start.13 = (f32[2,768]{1,0:T(2,128)S(1)}, f32[2,768]{1,0:T(2,128)S(1)}, u32[]{:S(2)}, u32[]{:S(2)}) collective-permute-start(f32[2,768]{1,0:T(2,128)S(1)} %get-tuple-element.52), channel_id=1, source_target_pairs={{118,0},{81,1},{112,2},{83,3},{114,4},{85,5},{116,6},{87,7},{126,8... | collective-permute-start | bytes 18440 | tf_op jit(solution)/shard_map/ppermute | solution.py:312
  58.6 4.0 %collective-permute-start.14 = (f32[2,768]{1,0:T(2,128)S(1)}, f32[2,768]{1,0:T(2,128)S(1)}, u32[]{:S(2)}, u32[]{:S(2)}) collective-permute-start(f32[2,768]{1,0:T(2,128)S(1)} %get-tuple-element.53), channel_id=1, source_target_pairs={{2,0},{25,1},{4,2},{27,3},{6,4},{29,5},{0,6},{31,7},{10,8},{17,9},... | collective-permute-start | bytes 18440 | tf_op jit(solution)/shard_map/ppermute | solution.py:312
  58.6 4.8 %collective-permute-start.15 = (f32[2,768]{1,0:T(2,128)S(1)}, f32[2,768]{1,0:T(2,128)S(1)}, u32[]{:S(2)}, u32[]{:S(2)}) collective-permute-start(f32[2,768]{1,0:T(2,128)S(1)} %get-tuple-element.54), channel_id=1, source_target_pairs={{102,0},{49,1},{96,2},{51,3},{98,4},{53,5},{100,6},{55,7},{110,8},... | collective-permute-start | bytes 18440 | tf_op jit(solution)/shard_map/ppermute | solution.py:312
  63.4 4.8 %collective-permute-start.16 = (f32[2,768]{1,0:T(2,128)S(1)}, f32[2,768]{1,0:T(2,128)S(1)}, u32[]{:S(2)}, u32[]{:S(2)}) collective-permute-start(f32[2,768]{1,0:T(2,128)S(1)} %maximum_maximum_fusion), channel_id=1, source_target_pairs={{0,1},{1,0},{2,3},{3,2},{4,5},{5,4},{6,7},{7,6},{8,9},{9,8},{10,11... | collective-permute-start | bytes 18440 | tf_op jit(solution)/shard_map/ppermute | solution.py:325

commit v4 on v3

--- a/solution.py
+++ b/solution.py
@@ -17,6 +17,7 @@
 )
 SOURCE = (None, 0, 0, 1, 2, 3)
 MOVED = 5
+HALVED = (1, 3, 5)
 SHARED = (1, 2, 3, 4)
 FIRST = ((1, 0), (2, 0), (2, 1))
 SECOND = ((1, 6), (2, 6), (2, 7))
@@ -86,10 +87,12 @@
     o_ref[...] = normalize(x_ref[...])
 
 
-def both_kernel(own_ref, other_ref, o_ref):
+def both_kernel(own_ref, other_ref, half_ref, o_ref):
     rows = own_ref.shape[0]
+    half = normalize(other_ref[...])
+    half_ref[...] = half
     o_ref[:rows] = own_ref[...]
-    o_ref[rows:] = normalize(other_ref[...])
+    o_ref[rows:] = half
 
 
 def here():
@@ -114,15 +117,25 @@
     return order * size + jnp.where(at >= size, at - size, at)
 
 
-def phase_kernel(names, pairs, diag, n_prev, each, *refs):
+def phase_kernel(names, counts, pairs, diag, n_prev, each, *refs):
     exclude_ref = refs[0]
-    blocks = dict(zip(names, refs[1 : 1 + len(names)]))
-    rest = refs[1 + len(names) :]
+    rest = refs[1:]
+    pieces = {}
+    for name, count in zip(names, counts):
+        pieces[name], rest = rest[:count], rest[count:]
     prev, rest = rest[:n_prev], rest[n_prev:]
-    outs, (row_acc, col_acc) = rest[:-2], rest[-2:]
+    outs, (whole, row_acc, col_acc) = rest[:-3], rest[-3:]
     exclude = exclude_ref[0]
     place = here()
-    size = blocks[names[0]].shape[0]
+    size = whole.shape[1]
+    blocks = {}
+    for name, parts in pieces.items():
+        if len(parts) == 1:
+            blocks[name] = parts[0]
+        else:
+            blocks[name] = whole.at[sum(len(pieces[other]) > 1 for other in names if other < name)]
+            for i, part in enumerate(parts):
+                blocks[name][i * part.shape[0] : (i + 1) * part.shape[0]] = part[...]
     width = 256
     row_names = sorted({a for a, _ in pairs} | ({0} if diag else set()))
     col_names = sorted({b for _, b in pairs})
@@ -233,7 +246,7 @@
     size = 2 * rows
     float32 = jnp.float32
 
-    def phase(pairs, blocks, prev, diag=False, each=False):
+    def phase(pairs, blocks, prev, weight, diag=False, each=False):
         names = sorted({name for pair in pairs for name in pair} | ({0} if diag else set()))
         rows_of = {a for a, _ in pairs} | ({0} if diag else set())
         cols_of = {b for _, b in pairs}
@@ -242,24 +255,26 @@
         out_shape = [part] * (MOVED + 1) if each else [own_part]
         out_shape.append(jax.ShapeDtypeStruct((2 * len(SHARED), size), float32))
         count = len(pairs) + diag
+        counts = [len(blocks[name]) for name in names]
         return pl.pallas_call(
             functools.partial(
-                phase_kernel, names, pairs, diag, len(prev), each
+                phase_kernel, names, counts, pairs, diag, len(prev), each
             ),
             out_shape=out_shape,
-            in_specs=[SMEM] + [VMEM] * (len(names) + len(prev)),
+            in_specs=[SMEM] + [VMEM] * (sum(counts) + len(prev)),
             out_specs=[VMEM] * len(out_shape),
             scratch_shapes=[
+                pltpu.VMEM((max(1, sum(n > 1 for n in counts)), size, length), jnp.bfloat16),
                 pltpu.VMEM((2 * len(rows_of), size, 128), float32),
                 pltpu.VMEM((2 * max(len(cols_of), 1), 8, size), float32),
             ],
             compiler_params=pltpu.CompilerParams(vmem_limit_bytes=20 * 2**20),
             cost_estimate=pl.CostEstimate(
-                flops=8 * 2 * count * size * size * length,
+                flops=weight * 2 * count * size * size * length,
                 bytes_accessed=2 * size * len(names),
                 transcendentals=0,
             ),
-        )(exclusion, *[blocks[name] for name in names], *prev)
+        )(exclusion, *[part for name in names for part in blocks[name]], *prev)
 
     other = lax.ppermute(segments, AXES, across())
     own = pl.pallas_call(
@@ -269,43 +284,52 @@
         out_specs=VMEM,
         compiler_params=pltpu.CompilerParams(vmem_limit_bytes=8 * 2**20),
     )(segments)
-    block = pl.pallas_call(
+    half, block = pl.pallas_call(
         both_kernel,
-        out_shape=jax.ShapeDtypeStruct((size, length), jnp.bfloat16),
+        out_shape=[
+            jax.ShapeDtypeStruct((rows, length), jnp.bfloat16),
+            jax.ShapeDtypeStruct((size, length), jnp.bfloat16),
+        ],
         in_specs=[VMEM, VMEM],
-        out_specs=VMEM,
+        out_specs=[VMEM, VMEM],
         compiler_params=pltpu.CompilerParams(vmem_limit_bytes=8 * 2**20),
     )(own, other)
 
-    blocks = {0: block}
+    blocks = {0: [block]}
+    sources = {0: [own, half]}
 
     def move(i):
         hops = tuple(minus(HELD[c][i], HELD[c][SOURCE[i]]) for c in (0, 1))
-        blocks[i] = lax.ppermute(blocks[SOURCE[i]], AXES, moves(hops))
+        parts = sources.get(SOURCE[i], blocks[SOURCE[i]]) if i in HALVED else blocks[SOURCE[i]]
+        blocks[i] = [lax.ppermute(part, AXES, moves(hops)) for part in parts]
 
     def share(i):
-        blocks[MOVED + i] = lax.ppermute(blocks[i], AXES, across())
+        blocks[MOVED + i] = [lax.ppermute(part, AXES, across()) for part in blocks[i]]
 
     def after(i, done):
-        blocks[i], done = lax.optimization_barrier((blocks[i], done))
+        first, *rest = blocks[i]
+        first, done = lax.optimization_barrier((first, done))
+        blocks[i] = [first, *rest]
         return done
 
     move(1)
     move(2)
+    best = phase((), blocks, (), 8, diag=True)
+    best = after(1, best)
     move(3)
     move(4)
     share(1)
     share(2)
-    best = phase(FIRST, blocks, (), diag=True)
-    best = phase(SECOND, blocks, best)
+    best = phase(FIRST, blocks, best, 8)
+    best = phase(SECOND, blocks, best, 0)
     best = after(3, best)
     move(5)
     share(3)
     share(4)
-    best = phase(THIRD, blocks, best)
-    best = phase(FOURTH, blocks, best)
+    best = phase(THIRD, blocks, best, 8)
+    best = phase(FOURTH, blocks, best, 8)
     best = after(5, best)
-    *parts, lent = phase(LAST, blocks, best, each=True)
+    *parts, lent = phase(LAST, blocks, best, 1, each=True)
 
     def give(i, part):
         back = tuple(minus((0, 0, 0), HELD[c][i]) for c in (0, 1))

time: 68.9 us -> 68.4 us (level)
  waiting for transfers between devices: 13.8 us -> 6.08 us
  starting transfers between devices: 31.8 us -> 38.2 us
  Pallas kernels: 20.7 us -> 21.5 us
    ppermute x9 -> x14, waiting for transfers between devices: 11.5 us -> 4.48 us  [the longest x8 4.46 us: move(): blocks[i] = [lax.ppermute(part, AXES, moves(hops)) for part in parts]]
    ppermute x9 -> x14, starting transfers between devices: 14.5 us -> 21.4 us  [the longest x6 11.4 us: share(): lax.ppermute(part, AXES, across())]
    pallas_call x6 -> x7, Pallas kernels: 20.4 us -> 21.3 us  [the longest x6 21 us: phase(): pl.pallas_call(functools.partial(phase_kernel, names, counts, pairs, diag...]
    ppermute x1, waiting for transfers between devices: 0.72 us -> 0.01 us  [shards(): other = lax.ppermute(segments, AXES, across())]
    ppermute x5, starting transfers between devices: 11.9 us -> 11.2 us  [give(): return lax.ppermute(part, AXES, moves(back))]
  transfers between devices with their start and end apart: 17 -> 22, of which waited for: 5 -> 5; matrix products, arithmetic and copies ran while one was open for 0% -> 0% of each run, Pallas kernels for 23% -> 25%
where the time goes in v4:
time: 68.4 us; the launch traced here: 68.3 us
  starting transfers between devices  38.2 us (56%)
  Pallas kernels  21.5 us (31%)
  waiting for transfers between devices  6.08 us (9%)
  local copies, waits for them, and re-layouts  1.13 us (2%)
  between operations  0.77 us (1%)
    pallas_call x6, Pallas kernels, phase(): pl.pallas_call(functools.partial(phase_kernel, names, counts, pairs, diag...  21 us
    ppermute x6, starting transfers between devices, share(): lax.ppermute(part, AXES, across())  11.4 us
    ppermute x5, starting transfers between devices, give(): return lax.ppermute(part, AXES, moves(back))  11.2 us
    ppermute x8, starting transfers between devices, move(): blocks[i] = [lax.ppermute(part, AXES, moves(hops)) for part in parts]  9.98 us
    ppermute x8, waiting for transfers between devices, move(): blocks[i] = [lax.ppermute(part, AXES, moves(hops)) for part in parts]  4.46 us
    ppermute x1, starting transfers between devices, shards(): other = lax.ppermute(mine, AXES, across())  4.15 us
    ppermute x1, starting transfers between devices, shards(): other = lax.ppermute(segments, AXES, across())  1.42 us
  transfers between devices with their start and end apart: 22, of which 5 were waited for; matrix products, arithmetic and copies ran while one was open for 0% of the time, Pallas kernels for 25%

profile of v4, /device:TPU:1, one launch (start us, length us, event | category | flops | bytes accessed | tf_op | source)
XLA Modules:
  0.0 68.3 jit_solution(17016849997593046884)
XLA Ops:
  0.0 1.4 %collective-permute-start.1 = (f32[384,512]{1,0:T(8,128)}, f32[384,512]{1,0:T(8,128)S(1)}, u32[]{:S(2)}, u32[]{:S(2)}) collective-permute-start(f32[384,512]{1,0:T(8,128)} %x_ref.1), channel_id=1, source_target_pairs={{0,1},{1,0},{2,3},{3,2},{4,5},{5,4},{6,7},{7,6},{8,9},{9,8},{10,11... | collective-permute-start | bytes 2359304 | tf_op jit(solution)/shard_map/ppermute | solution.py:279
  1.4 1.1 %copy-done = f32[384,512]{1,0:T(8,128)S(1)} copy-done((f32[384,512]{1,0:T(8,128)S(1)}, f32[384,512]{1,0:T(8,128)}, u32[]{:S(2)}) %copy-start) | copy-done | bytes 786456
  2.8 2.4 %collective-permute-start = (bf16[384,512]{1,0:T(8,128)(2,1)S(1)}, bf16[384,512]{1,0:T(8,128)(2,1)S(1)}, u32[]{:S(2)}, u32[]{:S(2)}) collective-permute-start(bf16[384,512]{1,0:T(8,128)(2,1)S(1)} %shard_map.28.own_ref), channel_id=1, source_target_pairs={{34,0},{121,1},{36,2},{123,3},{38,4},{125,5},{32,6},{127,7},{42,8}... | collective-permute-start | bytes 1179656 | tf_op jit(solution)/shard_map/ppermute | solution.py:304
  6.1 1.5 %collective-permute-start.3 = (bf16[768,512]{1,0:T(8,128)(2,1)S(1)}, bf16[768,512]{1,0:T(8,128)(2,1)S(1)}, u32[]{:S(2)}, u32[]{:S(2)}) collective-permute-start(bf16[768,512]{1,0:T(8,128)(2,1)S(1)} %get-tuple-element.37.refs_1_), channel_id=1, source_target_pairs={{6,0},{17,1},{0,2},{19,3},{2,4},{21,5},{4,6},{23,7},{14,8},{25,9},... | collective-permute-start | bytes 2359304 | tf_op jit(solution)/shard_map/ppermute | solution.py:304
  7.7 1.0 %collective-permute-start.2 = (bf16[384,512]{1,0:T(8,128)(2,1)S(1)}, bf16[384,512]{1,0:T(8,128)(2,1)S(1)}, u32[]{:S(2)}, u32[]{:S(2)}) collective-permute-start(bf16[384,512]{1,0:T(8,128)(2,1)S(1)} %get-tuple-element.41), channel_id=1, source_target_pairs={{34,0},{121,1},{36,2},{123,3},{38,4},{125,5},{32,6},{127,7},{42,8}... | collective-permute-start | bytes 1179656 | tf_op jit(solution)/shard_map/ppermute | solution.py:304
  8.7 1.3 %shard_map.30 = (f32[12,768]{1,0:T(8,128)S(1)}, f32[8,768]{1,0:T(8,128)S(1)}) custom-call(s32[1]{0:T(128)S(6)} %copy.3.refs_0_, bf16[768,512]{1,0:T(8,128)(2,1)S(1)} %get-tuple-element.37.refs_1_), custom_call_target="tpu_custom_call" | custom-call | flops 4831838208 | bytes 1536 | tf_op jit(solution)/shard_map/pallas_call | solution.py:259
  10.0 3.1 %collective-permute-done.refs_2_.refs_1_ = bf16[384,512]{1,0:T(8,128)(2,1)S(1)} collective-permute-done((bf16[384,512]{1,0:T(8,128)(2,1)S(1)}, bf16[384,512]{1,0:T(8,128)(2,1)S(1)}, u32[]{:S(2)}, u32[]{:S(2)}) %collective-permute-start) | collective-permute-done | bytes 393248 | tf_op jit(solution)/shard_map/ppermute | solution.py:304
  13.1 2.2 %collective-permute-start.6 = (bf16[384,512]{1,0:T(8,128)(2,1)S(1)}, bf16[384,512]{1,0:T(8,128)(2,1)S(1)}, u32[]{:S(2)}, u32[]{:S(2)}) collective-permute-start(bf16[384,512]{1,0:T(8,128)(2,1)S(1)} %collective-permute-done.refs_2_.refs_1_), channel_id=1, source_target_pairs={{0,1},{1,0},{2,3},{3,2},{4,5},{5,4},{6,7},{7,6},{8,9},{9,8},{10,11... | collective-permute-start | bytes 1179656 | tf_op jit(solution)/shard_map/ppermute | solution.py:307
  15.3 1.0 %collective-permute-start.5 = (bf16[384,512]{1,0:T(8,128)(2,1)S(1)}, bf16[384,512]{1,0:T(8,128)(2,1)S(1)}, u32[]{:S(2)}, u32[]{:S(2)}) collective-permute-start(bf16[384,512]{1,0:T(8,128)(2,1)S(1)} %collective-permute-done.refs_2_.refs_1_), channel_id=1, source_target_pairs={{24,0},{97,1},{26,2},{99,3},{28,4},{101,5},{30,6},{103,7},{16,8},{... | collective-permute-start | bytes 1179656 | tf_op jit(solution)/shard_map/ppermute | solution.py:304
  16.3 1.4 %collective-permute-done.2.refs_3_.refs_2_ = bf16[384,512]{1,0:T(8,128)(2,1)S(1)} collective-permute-done((bf16[384,512]{1,0:T(8,128)(2,1)S(1)}, bf16[384,512]{1,0:T(8,128)(2,1)S(1)}, u32[]{:S(2)}, u32[]{:S(2)}) %collective-permute-start.2) | collective-permute-done | bytes 393248 | tf_op jit(solution)/shard_map/ppermute | solution.py:304
  17.6 1.6 %collective-permute-start.7 = (bf16[384,512]{1,0:T(8,128)(2,1)S(1)}, bf16[384,512]{1,0:T(8,128)(2,1)S(1)}, u32[]{:S(2)}, u32[]{:S(2)}) collective-permute-start(bf16[384,512]{1,0:T(8,128)(2,1)S(1)} %collective-permute-done.2.refs_3_.refs_2_), channel_id=1, source_target_pairs={{0,1},{1,0},{2,3},{3,2},{4,5},{5,4},{6,7},{7,6},{8,9},{9,8},{10,11... | collective-permute-start | bytes 1179656 | tf_op jit(solution)/shard_map/ppermute | solution.py:307
  20.2 3.5 %collective-permute-start.8 = (bf16[768,512]{1,0:T(8,128)(2,1)S(1)}, bf16[768,512]{1,0:T(8,128)(2,1)S(1)}, u32[]{:S(2)}, u32[]{:S(2)}) collective-permute-start(bf16[768,512]{1,0:T(8,128)(2,1)S(1)} %collective-permute-done.3.refs_4_.refs_3_), channel_id=1, source_target_pairs={{0,1},{1,0},{2,3},{3,2},{4,5},{5,4},{6,7},{7,6},{8,9},{9,8},{10,11... | collective-permute-start | bytes 2359304 | tf_op jit(solution)/shard_map/ppermute | solution.py:307
  23.7 2.5 %collective-permute-start.4 = (bf16[768,512]{1,0:T(8,128)(2,1)S(1)}, bf16[768,512]{1,0:T(8,128)(2,1)S(1)}, u32[]{:S(2)}, u32[]{:S(2)}) collective-permute-start(bf16[768,512]{1,0:T(8,128)(2,1)S(1)} %collective-permute-done.3.refs_4_.refs_3_), channel_id=1, source_target_pairs={{6,0},{17,1},{0,2},{19,3},{2,4},{21,5},{4,6},{23,7},{14,8},{25,9},... | collective-permute-start | bytes 2359304 | tf_op jit(solution)/shard_map/ppermute | solution.py:304
  26.2 3.1 %shard_map.31 = (f32[12,768]{1,0:T(8,128)S(1)}, f32[8,768]{1,0:T(8,128)S(1)}) custom-call(s32[1]{0:T(128)S(6)} %copy.3.refs_0_, bf16[768,512]{1,0:T(8,128)(2,1)S(1)} %get-tuple-element.37.refs_1_, bf16[384,512]{1,0:T(8,128)(2,1)S(1)} %collective-permute-done.refs_2_.refs_1_, bf16[384,512]{1,0:T(8,128)(2,1)S(1)} %collective-permute-done.2.refs_3_.refs_2_, ...), custom_call_target="tpu_custom_call" | custom-call | flops 14495514624 | bytes 4608 | tf_op jit(solution)/shard_map/pallas_call | solution.py:259
  29.4 2.9 %shard_map.32 = (f32[12,768]{1,0:T(8,128)S(1)}, f32[8,768]{1,0:T(8,128)S(1)}) custom-call(s32[1]{0:T(128)S(6)} %copy.3.refs_0_, bf16[384,512]{1,0:T(8,128)(2,1)S(1)} %collective-permute-done.refs_2_.refs_1_, bf16[384,512]{1,0:T(8,128)(2,1)S(1)} %collective-permute-done.2.refs_3_.refs_2_, bf16[768,512]{1,0:T(8,128)(2,1)S(1)} %collective-permute-done.3.refs_4_.refs_3_, ...), custom_call_target="tpu_custom_call" | custom-call | bytes 6144 | tf_op jit(solution)/shard_map/pallas_call | solution.py:259
  32.3 3.2 %collective-permute-start.11 = (bf16[384,512]{1,0:T(8,128)(2,1)S(1)}, bf16[384,512]{1,0:T(8,128)(2,1)S(1)}, u32[]{:S(2)}, u32[]{:S(2)}) collective-permute-start(bf16[384,512]{1,0:T(8,128)(2,1)S(1)} %collective-permute-done.5.refs_5_.refs_1_), channel_id=1, source_target_pairs={{0,1},{1,0},{2,3},{3,2},{4,5},{5,4},{6,7},{7,6},{8,9},{9,8},{10,11... | collective-permute-start | bytes 1179656 | tf_op jit(solution)/shard_map/ppermute | solution.py:307
  36.9 5.9 %shard_map.33 = (f32[12,768]{1,0:T(8,128)S(1)}, f32[8,768]{1,0:T(8,128)S(1)}) custom-call(s32[1]{0:T(128)S(6)} %copy.3.refs_0_, bf16[768,512]{1,0:T(8,128)(2,1)S(1)} %get-tuple-element.37.refs_1_, bf16[384,512]{1,0:T(8,128)(2,1)S(1)} %collective-permute-done.refs_2_.refs_1_, bf16[384,512]{1,0:T(8,128)(2,1)S(1)} %collective-permute-done.2.refs_3_.refs_2_, ...), custom_call_target="tpu_custom_call" | custom-call | flops 33822867456 | bytes 10752 | tf_op jit(solution)/shard_map/pallas_call | solution.py:259
  42.8 3.1 %shard_map.34 = (f32[12,768]{1,0:T(8,128)S(1)}, f32[8,768]{1,0:T(8,128)S(1)}) custom-call(s32[1]{0:T(128)S(6)} %copy.3.refs_0_, bf16[384,512]{1,0:T(8,128)(2,1)S(1)} %collective-permute-done.5.refs_5_.refs_1_, bf16[384,512]{1,0:T(8,128)(2,1)S(1)} %collective-permute-done.10.refs_6_.refs_2_, bf16[768,512]{1,0:T(8,128)(2,1)S(1)} %collective-permute-done.4.refs_7_.refs_3_, ...), custom_call_target="tpu_custom_call" | custom-call | flops 14495514624 | bytes 6144 | tf_op jit(solution)/shard_map/pallas_call | solution.py:259
  46.0 4.7 %shard_map.35 = (f32[2,768]{1,0:T(2,128)S(1)}, f32[2,768]{1,0:T(2,128)S(1)}, f32[2,768]{1,0:T(2,128)S(1)}, f32[2,768]{1,0:T(2,128)S(1)}, f32[2,768]{1,0:T(2,128)...) custom-call(s32[1]{0:T(128)S(6)} %copy.3.refs_0_, bf16[384,512]{1,0:T(8,128)(2,1)S(1)} %collective-permute-done.refs_2_.refs_1_, ...), custom_call_target="tpu_custom_call" | custom-call | flops 3019898880 | bytes 9216 | tf_op jit(solution)/shard_map/pallas_call | solution.py:259
  50.7 2.7 %collective-permute-start.15 = (f32[2,768]{1,0:T(2,128)S(1)}, f32[2,768]{1,0:T(2,128)S(1)}, u32[]{:S(2)}, u32[]{:S(2)}) collective-permute-start(f32[2,768]{1,0:T(2,128)S(1)} %get-tuple-element.59), channel_id=1, source_target_pairs={{116,0},{73,1},{118,2},{75,3},{112,4},{77,5},{114,6},{79,7},{124,8... | collective-permute-start | bytes 18440 | tf_op jit(solution)/shard_map/ppermute | solution.py:336
  53.5 1.2 %collective-permute-start.17 = (f32[2,768]{1,0:T(2,128)S(1)}, f32[2,768]{1,0:T(2,128)S(1)}, u32[]{:S(2)}, u32[]{:S(2)}) collective-permute-start(f32[2,768]{1,0:T(2,128)S(1)} %get-tuple-element.65), channel_id=1, source_target_pairs={{4,0},{9,1},{6,2},{11,3},{0,4},{13,5},{2,6},{15,7},{12,8},{1,9},{1... | collective-permute-start | bytes 18440 | tf_op jit(solution)/shard_map/ppermute | solution.py:336
  54.6 4.0 %collective-permute-start.18 = (f32[2,768]{1,0:T(2,128)S(1)}, f32[2,768]{1,0:T(2,128)S(1)}, u32[]{:S(2)}, u32[]{:S(2)}) collective-permute-start(f32[2,768]{1,0:T(2,128)S(1)} %get-tuple-element.66), channel_id=1, source_target_pairs={{118,0},{81,1},{112,2},{83,3},{114,4},{85,5},{116,6},{87,7},{126,8... | collective-permute-start | bytes 18440 | tf_op jit(solution)/shard_map/ppermute | solution.py:336
  58.6 3.3 %collective-permute-start.20 = (f32[2,768]{1,0:T(2,128)S(1)}, f32[2,768]{1,0:T(2,128)S(1)}, u32[]{:S(2)}, u32[]{:S(2)}) collective-permute-start(f32[2,768]{1,0:T(2,128)S(1)} %get-tuple-element.68), channel_id=1, source_target_pairs={{102,0},{49,1},{96,2},{51,3},{98,4},{53,5},{100,6},{55,7},{110,8},... | collective-permute-start | bytes 18440 | tf_op jit(solution)/shard_map/ppermute | solution.py:336
  62.7 4.2 %collective-permute-start.21 = (f32[2,768]{1,0:T(2,128)S(1)}, f32[2,768]{1,0:T(2,128)S(1)}, u32[]{:S(2)}, u32[]{:S(2)}) collective-permute-start(f32[2,768]{1,0:T(2,128)S(1)} %maximum_maximum_fusion), channel_id=1, source_target_pairs={{0,1},{1,0},{2,3},{3,2},{4,5},{5,4},{6,7},{7,6},{8,9},{9,8},{10,11... | collective-permute-start | bytes 18440 | tf_op jit(solution)/shard_map/ppermute | solution.py:349
  (33 shorter events, 5.3 us)
Async XLA Ops:
  0.0 5.9 %collective-permute-start.1 = (f32[384,512]{1,0:T(8,128)}, f32[384,512]{1,0:T(8,128)S(1)}, u32[]{:S(2)}, u32[]{:S(2)}) collective-permute-start(f32[384,512]{1,0:T(8,128)} %x_ref.1), channel_id=1, source_target_pairs={{0,1},{1,0},{2,3},{3,2},{4,5},{5,4},{6,7},{7,6},{8,9},{9,8},{10,11... | collective-permute-start | bytes 2359304 | tf_op jit(solution)/shard_map/ppermute | solution.py:279
  1.4 1.1 %copy-start = (f32[384,512]{1,0:T(8,128)S(1)}, f32[384,512]{1,0:T(8,128)}, u32[]{:S(2)}) copy-start(f32[384,512]{1,0:T(8,128)} %x_ref.1) | copy-start | bytes 2359300
  2.8 10.2 %collective-permute-start = (bf16[384,512]{1,0:T(8,128)(2,1)S(1)}, bf16[384,512]{1,0:T(8,128)(2,1)S(1)}, u32[]{:S(2)}, u32[]{:S(2)}) collective-permute-start(bf16[384,512]{1,0:T(8,128)(2,1)S(1)} %shard_map.28.own_ref), channel_id=1, source_target_pairs={{34,0},{121,1},{36,2},{123,3},{38,4},{125,5},{32,6},{127,7},{42,8}... | collective-permute-start | bytes 1179656 | tf_op jit(solution)/shard_map/ppermute | solution.py:304
  6.1 14.1 %collective-permute-start.3 = (bf16[768,512]{1,0:T(8,128)(2,1)S(1)}, bf16[768,512]{1,0:T(8,128)(2,1)S(1)}, u32[]{:S(2)}, u32[]{:S(2)}) collective-permute-start(bf16[768,512]{1,0:T(8,128)(2,1)S(1)} %get-tuple-element.37.refs_1_), channel_id=1, source_target_pairs={{6,0},{17,1},{0,2},{19,3},{2,4},{21,5},{4,6},{23,7},{14,8},{25,9},... | collective-permute-start | bytes 2359304 | tf_op jit(solution)/shard_map/ppermute | solution.py:304
  7.7 9.9 %collective-permute-start.2 = (bf16[384,512]{1,0:T(8,128)(2,1)S(1)}, bf16[384,512]{1,0:T(8,128)(2,1)S(1)}, u32[]{:S(2)}, u32[]{:S(2)}) collective-permute-start(bf16[384,512]{1,0:T(8,128)(2,1)S(1)} %get-tuple-element.41), channel_id=1, source_target_pairs={{34,0},{121,1},{36,2},{123,3},{38,4},{125,5},{32,6},{127,7},{42,8}... | collective-permute-start | bytes 1179656 | tf_op jit(solution)/shard_map/ppermute | solution.py:304
  13.1 10.6 %collective-permute-start.6 = (bf16[384,512]{1,0:T(8,128)(2,1)S(1)}, bf16[384,512]{1,0:T(8,128)(2,1)S(1)}, u32[]{:S(2)}, u32[]{:S(2)}) collective-permute-start(bf16[384,512]{1,0:T(8,128)(2,1)S(1)} %collective-permute-done.refs_2_.refs_1_), channel_id=1, source_target_pairs={{0,1},{1,0},{2,3},{3,2},{4,5},{5,4},{6,7},{7,6},{8,9},{9,8},{10,11... | collective-permute-start | bytes 1179656 | tf_op jit(solution)/shard_map/ppermute | solution.py:307
  15.3 17.0 %collective-permute-start.5 = (bf16[384,512]{1,0:T(8,128)(2,1)S(1)}, bf16[384,512]{1,0:T(8,128)(2,1)S(1)}, u32[]{:S(2)}, u32[]{:S(2)}) collective-permute-start(bf16[384,512]{1,0:T(8,128)(2,1)S(1)} %collective-permute-done.refs_2_.refs_1_), channel_id=1, source_target_pairs={{24,0},{97,1},{26,2},{99,3},{28,4},{101,5},{30,6},{103,7},{16,8},{... | collective-permute-start | bytes 1179656 | tf_op jit(solution)/shard_map/ppermute | solution.py:304
  17.6 11.7 %collective-permute-start.7 = (bf16[384,512]{1,0:T(8,128)(2,1)S(1)}, bf16[384,512]{1,0:T(8,128)(2,1)S(1)}, u32[]{:S(2)}, u32[]{:S(2)}) collective-permute-start(bf16[384,512]{1,0:T(8,128)(2,1)S(1)} %collective-permute-done.2.refs_3_.refs_2_), channel_id=1, source_target_pairs={{0,1},{1,0},{2,3},{3,2},{4,5},{5,4},{6,7},{7,6},{8,9},{9,8},{10,11... | collective-permute-start | bytes 1179656 | tf_op jit(solution)/shard_map/ppermute | solution.py:307
  19.2 10.0 %collective-permute-start.10 = (bf16[384,512]{1,0:T(8,128)(2,1)S(1)}, bf16[384,512]{1,0:T(8,128)(2,1)S(1)}, u32[]{:S(2)}, u32[]{:S(2)}) collective-permute-start(bf16[384,512]{1,0:T(8,128)(2,1)S(1)} %collective-permute-done.2.refs_3_.refs_2_), channel_id=1, source_target_pairs={{24,0},{97,1},{26,2},{99,3},{28,4},{101,5},{30,6},{103,7},{16,8},{... | collective-permute-start | bytes 1179656 | tf_op jit(solution)/shard_map/ppermute | solution.py:304
  20.2 9.2 %collective-permute-start.8 = (bf16[768,512]{1,0:T(8,128)(2,1)S(1)}, bf16[768,512]{1,0:T(8,128)(2,1)S(1)}, u32[]{:S(2)}, u32[]{:S(2)}) collective-permute-start(bf16[768,512]{1,0:T(8,128)(2,1)S(1)} %collective-permute-done.3.refs_4_.refs_3_), channel_id=1, source_target_pairs={{0,1},{1,0},{2,3},{3,2},{4,5},{5,4},{6,7},{7,6},{8,9},{9,8},{10,11... | collective-permute-start | bytes 2359304 | tf_op jit(solution)/shard_map/ppermute | solution.py:307
  23.7 12.4 %collective-permute-start.4 = (bf16[768,512]{1,0:T(8,128)(2,1)S(1)}, bf16[768,512]{1,0:T(8,128)(2,1)S(1)}, u32[]{:S(2)}, u32[]{:S(2)}) collective-permute-start(bf16[768,512]{1,0:T(8,128)(2,1)S(1)} %collective-permute-done.3.refs_4_.refs_3_), channel_id=1, source_target_pairs={{6,0},{17,1},{0,2},{19,3},{2,4},{21,5},{4,6},{23,7},{14,8},{25,9},... | collective-permute-start | bytes 2359304 | tf_op jit(solution)/shard_map/ppermute | solution.py:304
  29.2 13.6 %collective-permute-start.12 = (bf16[384,512]{1,0:T(8,128)(2,1)S(1)}, bf16[384,512]{1,0:T(8,128)(2,1)S(1)}, u32[]{:S(2)}, u32[]{:S(2)}) collective-permute-start(bf16[384,512]{1,0:T(8,128)(2,1)S(1)} %collective-permute-done.10.refs_6_.refs_2_), channel_id=1, source_target_pairs={{0,1},{1,0},{2,3},{3,2},{4,5},{5,4},{6,7},{7,6},{8,9},{9,8},{10,11... | collective-permute-start | bytes 1179656 | tf_op jit(solution)/shard_map/ppermute | solution.py:307
  29.3 16.6 %collective-permute-start.14 = (bf16[384,512]{1,0:T(8,128)(2,1)S(1)}, bf16[384,512]{1,0:T(8,128)(2,1)S(1)}, u32[]{:S(2)}, u32[]{:S(2)}) collective-permute-start(bf16[384,512]{1,0:T(8,128)(2,1)S(1)} %collective-permute-done.10.refs_6_.refs_2_), channel_id=1, source_target_pairs={{2,0},{25,1},{4,2},{27,3},{6,4},{29,5},{0,6},{31,7},{10,8},{17,9},... | collective-permute-start | bytes 1179656 | tf_op jit(solution)/shard_map/ppermute | solution.py:304
  32.3 10.5 %collective-permute-start.11 = (bf16[384,512]{1,0:T(8,128)(2,1)S(1)}, bf16[384,512]{1,0:T(8,128)(2,1)S(1)}, u32[]{:S(2)}, u32[]{:S(2)}) collective-permute-start(bf16[384,512]{1,0:T(8,128)(2,1)S(1)} %collective-permute-done.5.refs_5_.refs_1_), channel_id=1, source_target_pairs={{0,1},{1,0},{2,3},{3,2},{4,5},{5,4},{6,7},{7,6},{8,9},{9,8},{10,11... | collective-permute-start | bytes 1179656 | tf_op jit(solution)/shard_map/ppermute | solution.py:307
  35.5 10.4 %collective-permute-start.9 = (bf16[384,512]{1,0:T(8,128)(2,1)S(1)}, bf16[384,512]{1,0:T(8,128)(2,1)S(1)}, u32[]{:S(2)}, u32[]{:S(2)}) collective-permute-start(bf16[384,512]{1,0:T(8,128)(2,1)S(1)} %collective-permute-done.5.refs_5_.refs_1_), channel_id=1, source_target_pairs={{2,0},{25,1},{4,2},{27,3},{6,4},{29,5},{0,6},{31,7},{10,8},{17,9},... | collective-permute-start | bytes 1179656 | tf_op jit(solution)/shard_map/ppermute | solution.py:304
  36.1 6.8 %collective-permute-start.13 = (bf16[768,512]{1,0:T(8,128)(2,1)S(1)}, bf16[768,512]{1,0:T(8,128)(2,1)S(1)}, u32[]{:S(2)}, u32[]{:S(2)}) collective-permute-start(bf16[768,512]{1,0:T(8,128)(2,1)S(1)} %collective-permute-done.4.refs_7_.refs_3_), channel_id=1, source_target_pairs={{0,1},{1,0},{2,3},{3,2},{4,5},{5,4},{6,7},{7,6},{8,9},{9,8},{10,11... | collective-permute-start | bytes 2359304 | tf_op jit(solution)/shard_map/ppermute | solution.py:307
  50.7 2.8 %collective-permute-start.16 = (f32[8,768]{1,0:T(8,128)S(1)}, f32[8,768]{1,0:T(8,128)S(1)}, u32[]{:S(2)}, u32[]{:S(2)}) collective-permute-start(f32[8,768]{1,0:T(8,128)S(1)} %get-tuple-element.64), channel_id=1, source_target_pairs={{0,1},{1,0},{2,3},{3,2},{4,5},{5,4},{6,7},{7,6},{8,9},{9,8},{10,11... | collective-permute-start | bytes 73736 | tf_op jit(solution)/shard_map/ppermute | solution.py:338
  50.7 11.2 %collective-permute-start.15 = (f32[2,768]{1,0:T(2,128)S(1)}, f32[2,768]{1,0:T(2,128)S(1)}, u32[]{:S(2)}, u32[]{:S(2)}) collective-permute-start(f32[2,768]{1,0:T(2,128)S(1)} %get-tuple-element.59), channel_id=1, source_target_pairs={{116,0},{73,1},{118,2},{75,3},{112,4},{77,5},{114,6},{79,7},{124,8... | collective-permute-start | bytes 18440 | tf_op jit(solution)/shard_map/ppermute | solution.py:336
  53.5 8.5 %collective-permute-start.17 = (f32[2,768]{1,0:T(2,128)S(1)}, f32[2,768]{1,0:T(2,128)S(1)}, u32[]{:S(2)}, u32[]{:S(2)}) collective-permute-start(f32[2,768]{1,0:T(2,128)S(1)} %get-tuple-element.65), channel_id=1, source_target_pairs={{4,0},{9,1},{6,2},{11,3},{0,4},{13,5},{2,6},{15,7},{12,8},{1,9},{1... | collective-permute-start | bytes 18440 | tf_op jit(solution)/shard_map/ppermute | solution.py:336
  54.6 7.3 %collective-permute-start.18 = (f32[2,768]{1,0:T(2,128)S(1)}, f32[2,768]{1,0:T(2,128)S(1)}, u32[]{:S(2)}, u32[]{:S(2)}) collective-permute-start(f32[2,768]{1,0:T(2,128)S(1)} %get-tuple-element.66), channel_id=1, source_target_pairs={{118,0},{81,1},{112,2},{83,3},{114,4},{85,5},{116,6},{87,7},{126,8... | collective-permute-start | bytes 18440 | tf_op jit(solution)/shard_map/ppermute | solution.py:336
  58.6 4.0 %collective-permute-start.19 = (f32[2,768]{1,0:T(2,128)S(1)}, f32[2,768]{1,0:T(2,128)S(1)}, u32[]{:S(2)}, u32[]{:S(2)}) collective-permute-start(f32[2,768]{1,0:T(2,128)S(1)} %get-tuple-element.67), channel_id=1, source_target_pairs={{2,0},{25,1},{4,2},{27,3},{6,4},{29,5},{0,6},{31,7},{10,8},{17,9},... | collective-permute-start | bytes 18440 | tf_op jit(solution)/shard_map/ppermute | solution.py:336
  58.6 4.1 %collective-permute-start.20 = (f32[2,768]{1,0:T(2,128)S(1)}, f32[2,768]{1,0:T(2,128)S(1)}, u32[]{:S(2)}, u32[]{:S(2)}) collective-permute-start(f32[2,768]{1,0:T(2,128)S(1)} %get-tuple-element.68), channel_id=1, source_target_pairs={{102,0},{49,1},{96,2},{51,3},{98,4},{53,5},{100,6},{55,7},{110,8},... | collective-permute-start | bytes 18440 | tf_op jit(solution)/shard_map/ppermute | solution.py:336
  62.7 5.0 %collective-permute-start.21 = (f32[2,768]{1,0:T(2,128)S(1)}, f32[2,768]{1,0:T(2,128)S(1)}, u32[]{:S(2)}, u32[]{:S(2)}) collective-permute-start(f32[2,768]{1,0:T(2,128)S(1)} %maximum_maximum_fusion), channel_id=1, source_target_pairs={{0,1},{1,0},{2,3},{3,2},{4,5},{5,4},{6,7},{7,6},{8,9},{9,8},{10,11... | collective-permute-start | bytes 18440 | tf_op jit(solution)/shard_map/ppermute | solution.py:349

commit v5 on v4

--- a/solution.py
+++ b/solution.py
@@ -22,8 +22,7 @@
 FIRST = ((1, 0), (2, 0), (2, 1))
 SECOND = ((1, 6), (2, 6), (2, 7))
 THIRD = ((3, 0), (3, 1), (3, 2), (3, 6), (3, 7), (4, 0), (4, 7))
-FOURTH = ((3, 8), (4, 8), (4, 9))
-LAST = ((5, 1), (5, 4), (5, 6), (5, 7), (5, 9))
+LAST = ((3, 8), (4, 8), (4, 9), (5, 1), (5, 4), (5, 6), (5, 7), (5, 9))
 LOW = -3.0
 
 
@@ -61,7 +60,7 @@
 
 def check_cover():
     seen = {(0, 0, 0)}
-    for a, b in FIRST + SECOND + THIRD + FOURTH + LAST:
+    for a, b in FIRST + SECOND + THIRD + LAST:
         for core in (0, 1):
             diff = minus(offset_of(a, core), offset_of(b, core))
             seen |= {diff, minus((0, 0, 0), diff)}
@@ -327,7 +326,6 @@
     share(3)
     share(4)
     best = phase(THIRD, blocks, best, 8)
-    best = phase(FOURTH, blocks, best, 8)
     best = after(5, best)
     *parts, lent = phase(LAST, blocks, best, 1, each=True)
 
@@ -344,7 +342,7 @@
         out_specs=[VMEM] * len(SHARED),
         compiler_params=pltpu.CompilerParams(vmem_limit_bytes=4 * 2**20),
     )(*[parts[i] for i in SHARED], lent)
-    for i in (4, 3, 2, 1):
+    for i in (4, 3, 1, 2):
         mine = jnp.maximum(mine, give(i, merged[i - 1]))
     other = lax.ppermute(mine, AXES, across())
     return 1.0 - jnp.maximum(mine[:, :rows], other[:, rows:])

time: 68.4 us -> 65 us (0.950)
  starting transfers between devices: 38.2 us -> 32.5 us
  waiting for transfers between devices: 6.08 us -> 8.91 us
    ppermute x1, starting transfers between devices: 4.15 us -> 0.09 us  [shards(): other = lax.ppermute(mine, AXES, across())]
    ppermute x5, waiting for transfers between devices: 0.77 us -> 2.73 us  [give(): return lax.ppermute(part, AXES, moves(back))]
    ppermute x5, starting transfers between devices: 11.2 us -> 9.51 us  [give(): return lax.ppermute(part, AXES, moves(back))]
    pallas_call x6 -> x5, Pallas kernels: 21 us -> 20.4 us  [phase(): pl.pallas_call(functools.partial(phase_kernel, names, counts, pairs, diag...]
  transfers between devices with their start and end apart: 22 -> 22, of which waited for: 5 -> 6; matrix products, arithmetic and copies ran while one was open for 0% -> 0% of each run, Pallas kernels for 25% -> 21%
where the time goes in v5:
time: 65 us; the launch traced here: 64.8 us
  starting transfers between devices  32.5 us (50%)
  Pallas kernels  21 us (32%)
  waiting for transfers between devices  8.91 us (14%)
  local copies, waits for them, and re-layouts  1.13 us (2%)
  between operations  0.75 us (1%)
    pallas_call x5, Pallas kernels, phase(): pl.pallas_call(functools.partial(phase_kernel, names, counts, pairs, diag...  20.4 us
    ppermute x6, starting transfers between devices, share(): lax.ppermute(part, AXES, across())  11.9 us
    ppermute x5, starting transfers between devices, give(): return lax.ppermute(part, AXES, moves(back))  9.51 us
    ppermute x8, starting transfers between devices, move(): blocks[i] = [lax.ppermute(part, AXES, moves(hops)) for part in parts]  9.49 us
    ppermute x8, waiting for transfers between devices, move(): blocks[i] = [lax.ppermute(part, AXES, moves(hops)) for part in parts]  5.01 us
    ppermute x5, waiting for transfers between devices, give(): return lax.ppermute(part, AXES, moves(back))  2.73 us
    ppermute x1, starting transfers between devices, shards(): other = lax.ppermute(segments, AXES, across())  1.42 us
  transfers between devices with their start and end apart: 22, of which 6 were waited for; matrix products, arithmetic and copies ran while one was open for 0% of the time, Pallas kernels for 21%

profile of v5, /device:TPU:1, one launch (start us, length us, event | category | flops | bytes accessed | tf_op | source)
XLA Modules:
  0.0 64.8 jit_solution(17152022649146636840)
XLA Ops:
  0.0 1.4 %collective-permute-start.1 = (f32[384,512]{1,0:T(8,128)}, f32[384,512]{1,0:T(8,128)S(1)}, u32[]{:S(2)}, u32[]{:S(2)}) collective-permute-start(f32[384,512]{1,0:T(8,128)} %x_ref.1), channel_id=1, source_target_pairs={{0,1},{1,0},{2,3},{3,2},{4,5},{5,4},{6,7},{7,6},{8,9},{9,8},{10,11... | collective-permute-start | bytes 2359304 | tf_op jit(solution)/shard_map/ppermute | solution.py:278
  1.4 1.1 %copy-done = f32[384,512]{1,0:T(8,128)S(1)} copy-done((f32[384,512]{1,0:T(8,128)S(1)}, f32[384,512]{1,0:T(8,128)}, u32[]{:S(2)}) %copy-start) | copy-done | bytes 786456
  2.8 2.4 %collective-permute-start = (bf16[384,512]{1,0:T(8,128)(2,1)S(1)}, bf16[384,512]{1,0:T(8,128)(2,1)S(1)}, u32[]{:S(2)}, u32[]{:S(2)}) collective-permute-start(bf16[384,512]{1,0:T(8,128)(2,1)S(1)} %shard_map.28.own_ref), channel_id=1, source_target_pairs={{34,0},{121,1},{36,2},{123,3},{38,4},{125,5},{32,6},{127,7},{42,8}... | collective-permute-start | bytes 1179656 | tf_op jit(solution)/shard_map/ppermute | solution.py:303
  6.1 1.5 %collective-permute-start.4 = (bf16[768,512]{1,0:T(8,128)(2,1)S(1)}, bf16[768,512]{1,0:T(8,128)(2,1)S(1)}, u32[]{:S(2)}, u32[]{:S(2)}) collective-permute-start(bf16[768,512]{1,0:T(8,128)(2,1)S(1)} %get-tuple-element.35.refs_1_), channel_id=1, source_target_pairs={{6,0},{17,1},{0,2},{19,3},{2,4},{21,5},{4,6},{23,7},{14,8},{25,9},... | collective-permute-start | bytes 2359304 | tf_op jit(solution)/shard_map/ppermute | solution.py:303
  7.7 1.0 %collective-permute-start.2 = (bf16[384,512]{1,0:T(8,128)(2,1)S(1)}, bf16[384,512]{1,0:T(8,128)(2,1)S(1)}, u32[]{:S(2)}, u32[]{:S(2)}) collective-permute-start(bf16[384,512]{1,0:T(8,128)(2,1)S(1)} %get-tuple-element.39), channel_id=1, source_target_pairs={{34,0},{121,1},{36,2},{123,3},{38,4},{125,5},{32,6},{127,7},{42,8}... | collective-permute-start | bytes 1179656 | tf_op jit(solution)/shard_map/ppermute | solution.py:303
  8.7 1.3 %shard_map.30 = (f32[12,768]{1,0:T(8,128)S(1)}, f32[8,768]{1,0:T(8,128)S(1)}) custom-call(s32[1]{0:T(128)S(6)} %copy.3.refs_0_, bf16[768,512]{1,0:T(8,128)(2,1)S(1)} %get-tuple-element.35.refs_1_), custom_call_target="tpu_custom_call" | custom-call | flops 4831838208 | bytes 1536 | tf_op jit(solution)/shard_map/pallas_call | solution.py:258
  10.0 3.1 %collective-permute-done.refs_2_.refs_1_ = bf16[384,512]{1,0:T(8,128)(2,1)S(1)} collective-permute-done((bf16[384,512]{1,0:T(8,128)(2,1)S(1)}, bf16[384,512]{1,0:T(8,128)(2,1)S(1)}, u32[]{:S(2)}, u32[]{:S(2)}) %collective-permute-start) | collective-permute-done | bytes 393248 | tf_op jit(solution)/shard_map/ppermute | solution.py:303
  13.1 2.2 %collective-permute-start.5 = (bf16[384,512]{1,0:T(8,128)(2,1)S(1)}, bf16[384,512]{1,0:T(8,128)(2,1)S(1)}, u32[]{:S(2)}, u32[]{:S(2)}) collective-permute-start(bf16[384,512]{1,0:T(8,128)(2,1)S(1)} %collective-permute-done.refs_2_.refs_1_), channel_id=1, source_target_pairs={{0,1},{1,0},{2,3},{3,2},{4,5},{5,4},{6,7},{7,6},{8,9},{9,8},{10,11... | collective-permute-start | bytes 1179656 | tf_op jit(solution)/shard_map/ppermute | solution.py:306
  16.3 1.4 %collective-permute-done.2.refs_3_.refs_2_ = bf16[384,512]{1,0:T(8,128)(2,1)S(1)} collective-permute-done((bf16[384,512]{1,0:T(8,128)(2,1)S(1)}, bf16[384,512]{1,0:T(8,128)(2,1)S(1)}, u32[]{:S(2)}, u32[]{:S(2)}) %collective-permute-start.2) | collective-permute-done | bytes 393248 | tf_op jit(solution)/shard_map/ppermute | solution.py:303
  17.6 1.6 %collective-permute-start.6 = (bf16[384,512]{1,0:T(8,128)(2,1)S(1)}, bf16[384,512]{1,0:T(8,128)(2,1)S(1)}, u32[]{:S(2)}, u32[]{:S(2)}) collective-permute-start(bf16[384,512]{1,0:T(8,128)(2,1)S(1)} %collective-permute-done.2.refs_3_.refs_2_), channel_id=1, source_target_pairs={{0,1},{1,0},{2,3},{3,2},{4,5},{5,4},{6,7},{7,6},{8,9},{9,8},{10,11... | collective-permute-start | bytes 1179656 | tf_op jit(solution)/shard_map/ppermute | solution.py:306
  20.2 3.5 %collective-permute-start.7 = (bf16[768,512]{1,0:T(8,128)(2,1)S(1)}, bf16[768,512]{1,0:T(8,128)(2,1)S(1)}, u32[]{:S(2)}, u32[]{:S(2)}) collective-permute-start(bf16[768,512]{1,0:T(8,128)(2,1)S(1)} %collective-permute-done.4.refs_4_.refs_3_), channel_id=1, source_target_pairs={{0,1},{1,0},{2,3},{3,2},{4,5},{5,4},{6,7},{7,6},{8,9},{9,8},{10,11... | collective-permute-start | bytes 2359304 | tf_op jit(solution)/shard_map/ppermute | solution.py:306
  23.7 2.5 %collective-permute-start.9 = (bf16[768,512]{1,0:T(8,128)(2,1)S(1)}, bf16[768,512]{1,0:T(8,128)(2,1)S(1)}, u32[]{:S(2)}, u32[]{:S(2)}) collective-permute-start(bf16[768,512]{1,0:T(8,128)(2,1)S(1)} %collective-permute-done.4.refs_4_.refs_3_), channel_id=1, source_target_pairs={{6,0},{17,1},{0,2},{19,3},{2,4},{21,5},{4,6},{23,7},{14,8},{25,9},... | collective-permute-start | bytes 2359304 | tf_op jit(solution)/shard_map/ppermute | solution.py:303
  26.2 3.1 %shard_map.31 = (f32[12,768]{1,0:T(8,128)S(1)}, f32[8,768]{1,0:T(8,128)S(1)}) custom-call(s32[1]{0:T(128)S(6)} %copy.3.refs_0_, bf16[768,512]{1,0:T(8,128)(2,1)S(1)} %get-tuple-element.35.refs_1_, bf16[384,512]{1,0:T(8,128)(2,1)S(1)} %collective-permute-done.refs_2_.refs_1_, bf16[384,512]{1,0:T(8,128)(2,1)S(1)} %collective-permute-done.2.refs_3_.refs_2_, ...), custom_call_target="tpu_custom_call" | custom-call | flops 14495514624 | bytes 4608 | tf_op jit(solution)/shard_map/pallas_call | solution.py:258
  29.3 3.3 %collective-permute-start.13 = (bf16[384,512]{1,0:T(8,128)(2,1)S(1)}, bf16[384,512]{1,0:T(8,128)(2,1)S(1)}, u32[]{:S(2)}, u32[]{:S(2)}) collective-permute-start(bf16[384,512]{1,0:T(8,128)(2,1)S(1)} %collective-permute-done.8.refs_6_.refs_4_), channel_id=1, source_target_pairs={{0,1},{1,0},{2,3},{3,2},{4,5},{5,4},{6,7},{7,6},{8,9},{9,8},{10,11... | collective-permute-start | bytes 1179656 | tf_op jit(solution)/shard_map/ppermute | solution.py:306
  32.6 2.9 %shard_map.32 = (f32[12,768]{1,0:T(8,128)S(1)}, f32[8,768]{1,0:T(8,128)S(1)}) custom-call(s32[1]{0:T(128)S(6)} %copy.3.refs_0_, bf16[384,512]{1,0:T(8,128)(2,1)S(1)} %collective-permute-done.refs_2_.refs_1_, bf16[384,512]{1,0:T(8,128)(2,1)S(1)} %collective-permute-done.2.refs_3_.refs_2_, bf16[768,512]{1,0:T(8,128)(2,1)S(1)} %collective-permute-done.4.refs_4_.refs_3_, ...), custom_call_target="tpu_custom_call" | custom-call | bytes 6144 | tf_op jit(solution)/shard_map/pallas_call | solution.py:258
  36.9 5.9 %shard_map.33 = (f32[12,768]{1,0:T(8,128)S(1)}, f32[8,768]{1,0:T(8,128)S(1)}) custom-call(s32[1]{0:T(128)S(6)} %copy.3.refs_0_, bf16[768,512]{1,0:T(8,128)(2,1)S(1)} %get-tuple-element.35.refs_1_, bf16[384,512]{1,0:T(8,128)(2,1)S(1)} %collective-permute-done.refs_2_.refs_1_, bf16[384,512]{1,0:T(8,128)(2,1)S(1)} %collective-permute-done.2.refs_3_.refs_2_, ...), custom_call_target="tpu_custom_call" | custom-call | flops 33822867456 | bytes 10752 | tf_op jit(solution)/shard_map/pallas_call | solution.py:258
  43.4 7.3 %shard_map.34 = (f32[2,768]{1,0:T(2,128)S(1)}, f32[2,768]{1,0:T(2,128)S(1)}, f32[2,768]{1,0:T(2,128)S(1)}, f32[2,768]{1,0:T(2,128)S(1)}, f32[2,768]{1,0:T(2,128)...) custom-call(s32[1]{0:T(128)S(6)} %copy.3.refs_0_, bf16[384,512]{1,0:T(8,128)(2,1)S(1)} %collective-permute-done.refs_2_.refs_1_, ...), custom_call_target="tpu_custom_call" | custom-call | flops 4831838208 | bytes 12288 | tf_op jit(solution)/shard_map/pallas_call | solution.py:258
  50.7 2.2 %collective-permute-start.15 = (f32[2,768]{1,0:T(2,128)S(1)}, f32[2,768]{1,0:T(2,128)S(1)}, u32[]{:S(2)}, u32[]{:S(2)}) collective-permute-start(f32[2,768]{1,0:T(2,128)S(1)} %get-tuple-element.55), channel_id=1, source_target_pairs={{116,0},{73,1},{118,2},{75,3},{112,4},{77,5},{114,6},{79,7},{124,8... | collective-permute-start | bytes 18440 | tf_op jit(solution)/shard_map/ppermute | solution.py:334
  53.0 1.1 %collective-permute-start.17 = (f32[2,768]{1,0:T(2,128)S(1)}, f32[2,768]{1,0:T(2,128)S(1)}, u32[]{:S(2)}, u32[]{:S(2)}) collective-permute-start(f32[2,768]{1,0:T(2,128)S(1)} %get-tuple-element.61), channel_id=1, source_target_pairs={{4,0},{9,1},{6,2},{11,3},{0,4},{13,5},{2,6},{15,7},{12,8},{1,9},{1... | collective-permute-start | bytes 18440 | tf_op jit(solution)/shard_map/ppermute | solution.py:334
  54.1 4.0 %collective-permute-start.18 = (f32[2,768]{1,0:T(2,128)S(1)}, f32[2,768]{1,0:T(2,128)S(1)}, u32[]{:S(2)}, u32[]{:S(2)}) collective-permute-start(f32[2,768]{1,0:T(2,128)S(1)} %get-tuple-element.62), channel_id=1, source_target_pairs={{118,0},{81,1},{112,2},{83,3},{114,4},{85,5},{116,6},{87,7},{126,8... | collective-permute-start | bytes 18440 | tf_op jit(solution)/shard_map/ppermute | solution.py:334
  58.1 1.2 %collective-permute-start.19 = (f32[2,768]{1,0:T(2,128)S(1)}, f32[2,768]{1,0:T(2,128)S(1)}, u32[]{:S(2)}, u32[]{:S(2)}) collective-permute-start(f32[2,768]{1,0:T(2,128)S(1)} %get-tuple-element.63), channel_id=1, source_target_pairs={{102,0},{49,1},{96,2},{51,3},{98,4},{53,5},{100,6},{55,7},{110,8},... | collective-permute-start | bytes 18440 | tf_op jit(solution)/shard_map/ppermute | solution.py:334
  60.3 1.5 %collective-permute-done.19 = f32[2,768]{1,0:T(2,128)S(1)} collective-permute-done((f32[2,768]{1,0:T(2,128)S(1)}, f32[2,768]{1,0:T(2,128)S(1)}, u32[]{:S(2)}, u32[]{:S(2)}) %collective-permute-start.19) | collective-permute-done | bytes 6176 | tf_op jit(solution)/shard_map/ppermute | solution.py:334
  61.8 1.2 %collective-permute-done.20 = f32[2,768]{1,0:T(2,128)S(1)} collective-permute-done((f32[2,768]{1,0:T(2,128)S(1)}, f32[2,768]{1,0:T(2,128)S(1)}, u32[]{:S(2)}, u32[]{:S(2)}) %collective-permute-start.20) | collective-permute-done | bytes 6176 | tf_op jit(solution)/shard_map/ppermute | solution.py:334
  63.1 1.2 %collective-permute-done.21 = f32[2,768]{1,0:T(2,128)S(1)} collective-permute-done((f32[2,768]{1,0:T(2,128)S(1)}, f32[2,768]{1,0:T(2,128)S(1)}, u32[]{:S(2)}, u32[]{:S(2)}) %collective-permute-start.21) | collective-permute-done | bytes 6176 | tf_op jit(solution)/shard_map/ppermute | solution.py:347
  (32 shorter events, 6.3 us)
Async XLA Ops:
  0.0 5.9 %collective-permute-start.1 = (f32[384,512]{1,0:T(8,128)}, f32[384,512]{1,0:T(8,128)S(1)}, u32[]{:S(2)}, u32[]{:S(2)}) collective-permute-start(f32[384,512]{1,0:T(8,128)} %x_ref.1), channel_id=1, source_target_pairs={{0,1},{1,0},{2,3},{3,2},{4,5},{5,4},{6,7},{7,6},{8,9},{9,8},{10,11... | collective-permute-start | bytes 2359304 | tf_op jit(solution)/shard_map/ppermute | solution.py:278
  1.4 1.1 %copy-start = (f32[384,512]{1,0:T(8,128)S(1)}, f32[384,512]{1,0:T(8,128)}, u32[]{:S(2)}) copy-start(f32[384,512]{1,0:T(8,128)} %x_ref.1) | copy-start | bytes 2359300
  2.8 10.2 %collective-permute-start = (bf16[384,512]{1,0:T(8,128)(2,1)S(1)}, bf16[384,512]{1,0:T(8,128)(2,1)S(1)}, u32[]{:S(2)}, u32[]{:S(2)}) collective-permute-start(bf16[384,512]{1,0:T(8,128)(2,1)S(1)} %shard_map.28.own_ref), channel_id=1, source_target_pairs={{34,0},{121,1},{36,2},{123,3},{38,4},{125,5},{32,6},{127,7},{42,8}... | collective-permute-start | bytes 1179656 | tf_op jit(solution)/shard_map/ppermute | solution.py:303
  6.1 14.1 %collective-permute-start.4 = (bf16[768,512]{1,0:T(8,128)(2,1)S(1)}, bf16[768,512]{1,0:T(8,128)(2,1)S(1)}, u32[]{:S(2)}, u32[]{:S(2)}) collective-permute-start(bf16[768,512]{1,0:T(8,128)(2,1)S(1)} %get-tuple-element.35.refs_1_), channel_id=1, source_target_pairs={{6,0},{17,1},{0,2},{19,3},{2,4},{21,5},{4,6},{23,7},{14,8},{25,9},... | collective-permute-start | bytes 2359304 | tf_op jit(solution)/shard_map/ppermute | solution.py:303
  7.7 9.9 %collective-permute-start.2 = (bf16[384,512]{1,0:T(8,128)(2,1)S(1)}, bf16[384,512]{1,0:T(8,128)(2,1)S(1)}, u32[]{:S(2)}, u32[]{:S(2)}) collective-permute-start(bf16[384,512]{1,0:T(8,128)(2,1)S(1)} %get-tuple-element.39), channel_id=1, source_target_pairs={{34,0},{121,1},{36,2},{123,3},{38,4},{125,5},{32,6},{127,7},{42,8}... | collective-permute-start | bytes 1179656 | tf_op jit(solution)/shard_map/ppermute | solution.py:303
  13.1 10.6 %collective-permute-start.5 = (bf16[384,512]{1,0:T(8,128)(2,1)S(1)}, bf16[384,512]{1,0:T(8,128)(2,1)S(1)}, u32[]{:S(2)}, u32[]{:S(2)}) collective-permute-start(bf16[384,512]{1,0:T(8,128)(2,1)S(1)} %collective-permute-done.refs_2_.refs_1_), channel_id=1, source_target_pairs={{0,1},{1,0},{2,3},{3,2},{4,5},{5,4},{6,7},{7,6},{8,9},{9,8},{10,11... | collective-permute-start | bytes 1179656 | tf_op jit(solution)/shard_map/ppermute | solution.py:306
  15.3 20.2 %collective-permute-start.3 = (bf16[384,512]{1,0:T(8,128)(2,1)S(1)}, bf16[384,512]{1,0:T(8,128)(2,1)S(1)}, u32[]{:S(2)}, u32[]{:S(2)}) collective-permute-start(bf16[384,512]{1,0:T(8,128)(2,1)S(1)} %collective-permute-done.refs_2_.refs_1_), channel_id=1, source_target_pairs={{24,0},{97,1},{26,2},{99,3},{28,4},{101,5},{30,6},{103,7},{16,8},{... | collective-permute-start | bytes 1179656 | tf_op jit(solution)/shard_map/ppermute | solution.py:303
  17.6 11.7 %collective-permute-start.6 = (bf16[384,512]{1,0:T(8,128)(2,1)S(1)}, bf16[384,512]{1,0:T(8,128)(2,1)S(1)}, u32[]{:S(2)}, u32[]{:S(2)}) collective-permute-start(bf16[384,512]{1,0:T(8,128)(2,1)S(1)} %collective-permute-done.2.refs_3_.refs_2_), channel_id=1, source_target_pairs={{0,1},{1,0},{2,3},{3,2},{4,5},{5,4},{6,7},{7,6},{8,9},{9,8},{10,11... | collective-permute-start | bytes 1179656 | tf_op jit(solution)/shard_map/ppermute | solution.py:306
  19.2 10.0 %collective-permute-start.8 = (bf16[384,512]{1,0:T(8,128)(2,1)S(1)}, bf16[384,512]{1,0:T(8,128)(2,1)S(1)}, u32[]{:S(2)}, u32[]{:S(2)}) collective-permute-start(bf16[384,512]{1,0:T(8,128)(2,1)S(1)} %collective-permute-done.2.refs_3_.refs_2_), channel_id=1, source_target_pairs={{24,0},{97,1},{26,2},{99,3},{28,4},{101,5},{30,6},{103,7},{16,8},{... | collective-permute-start | bytes 1179656 | tf_op jit(solution)/shard_map/ppermute | solution.py:303
  20.2 12.4 %collective-permute-start.7 = (bf16[768,512]{1,0:T(8,128)(2,1)S(1)}, bf16[768,512]{1,0:T(8,128)(2,1)S(1)}, u32[]{:S(2)}, u32[]{:S(2)}) collective-permute-start(bf16[768,512]{1,0:T(8,128)(2,1)S(1)} %collective-permute-done.4.refs_4_.refs_3_), channel_id=1, source_target_pairs={{0,1},{1,0},{2,3},{3,2},{4,5},{5,4},{6,7},{7,6},{8,9},{9,8},{10,11... | collective-permute-start | bytes 2359304 | tf_op jit(solution)/shard_map/ppermute | solution.py:306
  23.7 12.4 %collective-permute-start.9 = (bf16[768,512]{1,0:T(8,128)(2,1)S(1)}, bf16[768,512]{1,0:T(8,128)(2,1)S(1)}, u32[]{:S(2)}, u32[]{:S(2)}) collective-permute-start(bf16[768,512]{1,0:T(8,128)(2,1)S(1)} %collective-permute-done.4.refs_4_.refs_3_), channel_id=1, source_target_pairs={{6,0},{17,1},{0,2},{19,3},{2,4},{21,5},{4,6},{23,7},{14,8},{25,9},... | collective-permute-start | bytes 2359304 | tf_op jit(solution)/shard_map/ppermute | solution.py:303
  29.2 14.1 %collective-permute-start.11 = (bf16[384,512]{1,0:T(8,128)(2,1)S(1)}, bf16[384,512]{1,0:T(8,128)(2,1)S(1)}, u32[]{:S(2)}, u32[]{:S(2)}) collective-permute-start(bf16[384,512]{1,0:T(8,128)(2,1)S(1)} %collective-permute-done.8.refs_6_.refs_4_), channel_id=1, source_target_pairs={{2,0},{25,1},{4,2},{27,3},{6,4},{29,5},{0,6},{31,7},{10,8},{17,9},... | collective-permute-start | bytes 1179656 | tf_op jit(solution)/shard_map/ppermute | solution.py:303
  29.3 14.0 %collective-permute-start.13 = (bf16[384,512]{1,0:T(8,128)(2,1)S(1)}, bf16[384,512]{1,0:T(8,128)(2,1)S(1)}, u32[]{:S(2)}, u32[]{:S(2)}) collective-permute-start(bf16[384,512]{1,0:T(8,128)(2,1)S(1)} %collective-permute-done.8.refs_6_.refs_4_), channel_id=1, source_target_pairs={{0,1},{1,0},{2,3},{3,2},{4,5},{5,4},{6,7},{7,6},{8,9},{9,8},{10,11... | collective-permute-start | bytes 1179656 | tf_op jit(solution)/shard_map/ppermute | solution.py:306
  35.5 7.9 %collective-permute-start.10 = (bf16[384,512]{1,0:T(8,128)(2,1)S(1)}, bf16[384,512]{1,0:T(8,128)(2,1)S(1)}, u32[]{:S(2)}, u32[]{:S(2)}) collective-permute-start(bf16[384,512]{1,0:T(8,128)(2,1)S(1)} %collective-permute-done.3.refs_5_.refs_3_), channel_id=1, source_target_pairs={{2,0},{25,1},{4,2},{27,3},{6,4},{29,5},{0,6},{31,7},{10,8},{17,9},... | collective-permute-start | bytes 1179656 | tf_op jit(solution)/shard_map/ppermute | solution.py:303
  35.5 7.8 %collective-permute-start.12 = (bf16[384,512]{1,0:T(8,128)(2,1)S(1)}, bf16[384,512]{1,0:T(8,128)(2,1)S(1)}, u32[]{:S(2)}, u32[]{:S(2)}) collective-permute-start(bf16[384,512]{1,0:T(8,128)(2,1)S(1)} %collective-permute-done.3.refs_5_.refs_3_), channel_id=1, source_target_pairs={{0,1},{1,0},{2,3},{3,2},{4,5},{5,4},{6,7},{7,6},{8,9},{9,8},{10,11... | collective-permute-start | bytes 1179656 | tf_op jit(solution)/shard_map/ppermute | solution.py:306
  36.1 7.3 %collective-permute-start.14 = (bf16[768,512]{1,0:T(8,128)(2,1)S(1)}, bf16[768,512]{1,0:T(8,128)(2,1)S(1)}, u32[]{:S(2)}, u32[]{:S(2)}) collective-permute-start(bf16[768,512]{1,0:T(8,128)(2,1)S(1)} %collective-permute-done.9.refs_7_.refs_5_), channel_id=1, source_target_pairs={{0,1},{1,0},{2,3},{3,2},{4,5},{5,4},{6,7},{7,6},{8,9},{9,8},{10,11... | collective-permute-start | bytes 2359304 | tf_op jit(solution)/shard_map/ppermute | solution.py:306
  50.7 2.3 %collective-permute-start.16 = (f32[8,768]{1,0:T(8,128)S(1)}, f32[8,768]{1,0:T(8,128)S(1)}, u32[]{:S(2)}, u32[]{:S(2)}) collective-permute-start(f32[8,768]{1,0:T(8,128)S(1)} %get-tuple-element.60), channel_id=1, source_target_pairs={{0,1},{1,0},{2,3},{3,2},{4,5},{5,4},{6,7},{7,6},{8,9},{9,8},{10,11... | collective-permute-start | bytes 73736 | tf_op jit(solution)/shard_map/ppermute | solution.py:336
  50.7 9.5 %collective-permute-start.15 = (f32[2,768]{1,0:T(2,128)S(1)}, f32[2,768]{1,0:T(2,128)S(1)}, u32[]{:S(2)}, u32[]{:S(2)}) collective-permute-start(f32[2,768]{1,0:T(2,128)S(1)} %get-tuple-element.55), channel_id=1, source_target_pairs={{116,0},{73,1},{118,2},{75,3},{112,4},{77,5},{114,6},{79,7},{124,8... | collective-permute-start | bytes 18440 | tf_op jit(solution)/shard_map/ppermute | solution.py:334
  53.0 7.3 %collective-permute-start.17 = (f32[2,768]{1,0:T(2,128)S(1)}, f32[2,768]{1,0:T(2,128)S(1)}, u32[]{:S(2)}, u32[]{:S(2)}) collective-permute-start(f32[2,768]{1,0:T(2,128)S(1)} %get-tuple-element.61), channel_id=1, source_target_pairs={{4,0},{9,1},{6,2},{11,3},{0,4},{13,5},{2,6},{15,7},{12,8},{1,9},{1... | collective-permute-start | bytes 18440 | tf_op jit(solution)/shard_map/ppermute | solution.py:334
  54.1 6.2 %collective-permute-start.18 = (f32[2,768]{1,0:T(2,128)S(1)}, f32[2,768]{1,0:T(2,128)S(1)}, u32[]{:S(2)}, u32[]{:S(2)}) collective-permute-start(f32[2,768]{1,0:T(2,128)S(1)} %get-tuple-element.62), channel_id=1, source_target_pairs={{118,0},{81,1},{112,2},{83,3},{114,4},{85,5},{116,6},{87,7},{126,8... | collective-permute-start | bytes 18440 | tf_op jit(solution)/shard_map/ppermute | solution.py:334
  58.1 3.7 %collective-permute-start.19 = (f32[2,768]{1,0:T(2,128)S(1)}, f32[2,768]{1,0:T(2,128)S(1)}, u32[]{:S(2)}, u32[]{:S(2)}) collective-permute-start(f32[2,768]{1,0:T(2,128)S(1)} %get-tuple-element.63), channel_id=1, source_target_pairs={{102,0},{49,1},{96,2},{51,3},{98,4},{53,5},{100,6},{55,7},{110,8},... | collective-permute-start | bytes 18440 | tf_op jit(solution)/shard_map/ppermute | solution.py:334
  59.3 3.7 %collective-permute-start.20 = (f32[2,768]{1,0:T(2,128)S(1)}, f32[2,768]{1,0:T(2,128)S(1)}, u32[]{:S(2)}, u32[]{:S(2)}) collective-permute-start(f32[2,768]{1,0:T(2,128)S(1)} %get-tuple-element.64), channel_id=1, source_target_pairs={{2,0},{25,1},{4,2},{27,3},{6,4},{29,5},{0,6},{31,7},{10,8},{17,9},... | collective-permute-start | bytes 18440 | tf_op jit(solution)/shard_map/ppermute | solution.py:334
  63.0 1.2 %collective-permute-start.21 = (f32[2,768]{1,0:T(2,128)S(1)}, f32[2,768]{1,0:T(2,128)S(1)}, u32[]{:S(2)}, u32[]{:S(2)}) collective-permute-start(f32[2,768]{1,0:T(2,128)S(1)} %maximum_maximum_fusion), channel_id=1, source_target_pairs={{0,1},{1,0},{2,3},{3,2},{4,5},{5,4},{6,7},{7,6},{8,9},{9,8},{10,11... | collective-permute-start | bytes 18440 | tf_op jit(solution)/shard_map/ppermute | solution.py:347

commit v6 on v5

--- a/solution.py
+++ b/solution.py
@@ -320,12 +320,11 @@
     share(1)
     share(2)
     best = phase(FIRST, blocks, best, 8)
-    best = phase(SECOND, blocks, best, 0)
     best = after(3, best)
     move(5)
     share(3)
     share(4)
-    best = phase(THIRD, blocks, best, 8)
+    best = phase(SECOND + THIRD, blocks, best, 8)
     best = after(5, best)
     *parts, lent = phase(LAST, blocks, best, 1, each=True)
 

time: 65 us -> 67.7 us (1.042)
  starting transfers between devices: 32.5 us -> 35.7 us
    ppermute x6, starting transfers between devices: 11.9 us -> 15.9 us  [share(): lax.ppermute(part, AXES, across())]
    ppermute x8, starting transfers between devices: 9.49 us -> 8.25 us  [move(): blocks[i] = [lax.ppermute(part, AXES, moves(hops)) for part in parts]]
    pallas_call x5 -> x4, Pallas kernels: 20.4 us -> 20.3 us  [phase(): pl.pallas_call(functools.partial(phase_kernel, names, counts, pairs, diag...]
  transfers between devices with their start and end apart: 22 -> 22, of which waited for: 6 -> 6; matrix products, arithmetic and copies ran while one was open for 0% -> 0% of each run, Pallas kernels for 21% -> 20%
where the time goes in v6:
time: 67.7 us; the launch traced here: 67.5 us
  starting transfers between devices  35.7 us (53%)
  Pallas kernels  20.9 us (31%)
  waiting for transfers between devices  8.47 us (13%)
  local copies, waits for them, and re-layouts  1.13 us (2%)
  between operations  0.74 us (1%)
    pallas_call x4, Pallas kernels, phase(): pl.pallas_call(functools.partial(phase_kernel, names, counts, pairs, diag...  20.3 us
    ppermute x6, starting transfers between devices, share(): lax.ppermute(part, AXES, across())  15.9 us
    ppermute x5, starting transfers between devices, give(): return lax.ppermute(part, AXES, moves(back))  9.63 us
    ppermute x8, starting transfers between devices, move(): blocks[i] = [lax.ppermute(part, AXES, moves(hops)) for part in parts]  8.25 us
    ppermute x8, waiting for transfers between devices, move(): blocks[i] = [lax.ppermute(part, AXES, moves(hops)) for part in parts]  4.56 us
    ppermute x5, waiting for transfers between devices, give(): return lax.ppermute(part, AXES, moves(back))  2.73 us
    ppermute x1, starting transfers between devices, shards(): other = lax.ppermute(segments, AXES, across())  1.42 us
  transfers between devices with their start and end apart: 22, of which 6 were waited for; matrix products, arithmetic and copies ran while one was open for 0% of the time, Pallas kernels for 20%

profile of v6, /device:TPU:1, one launch (start us, length us, event | category | flops | bytes accessed | tf_op | source)
XLA Modules:
  0.0 67.5 jit_solution(1807015969331796988)
XLA Ops:
  0.0 1.4 %collective-permute-start.1 = (f32[384,512]{1,0:T(8,128)}, f32[384,512]{1,0:T(8,128)S(1)}, u32[]{:S(2)}, u32[]{:S(2)}) collective-permute-start(f32[384,512]{1,0:T(8,128)} %x_ref.1), channel_id=1, source_target_pairs={{0,1},{1,0},{2,3},{3,2},{4,5},{5,4},{6,7},{7,6},{8,9},{9,8},{10,11... | collective-permute-start | bytes 2359304 | tf_op jit(solution)/shard_map/ppermute | solution.py:278
  1.4 1.1 %copy-done = f32[384,512]{1,0:T(8,128)S(1)} copy-done((f32[384,512]{1,0:T(8,128)S(1)}, f32[384,512]{1,0:T(8,128)}, u32[]{:S(2)}) %copy-start) | copy-done | bytes 786456
  2.8 2.4 %collective-permute-start = (bf16[384,512]{1,0:T(8,128)(2,1)S(1)}, bf16[384,512]{1,0:T(8,128)(2,1)S(1)}, u32[]{:S(2)}, u32[]{:S(2)}) collective-permute-start(bf16[384,512]{1,0:T(8,128)(2,1)S(1)} %shard_map.28.own_ref), channel_id=1, source_target_pairs={{34,0},{121,1},{36,2},{123,3},{38,4},{125,5},{32,6},{127,7},{42,8}... | collective-permute-start | bytes 1179656 | tf_op jit(solution)/shard_map/ppermute | solution.py:303
  6.1 1.5 %collective-permute-start.4 = (bf16[768,512]{1,0:T(8,128)(2,1)S(1)}, bf16[768,512]{1,0:T(8,128)(2,1)S(1)}, u32[]{:S(2)}, u32[]{:S(2)}) collective-permute-start(bf16[768,512]{1,0:T(8,128)(2,1)S(1)} %get-tuple-element.33.refs_1_), channel_id=1, source_target_pairs={{6,0},{17,1},{0,2},{19,3},{2,4},{21,5},{4,6},{23,7},{14,8},{25,9},... | collective-permute-start | bytes 2359304 | tf_op jit(solution)/shard_map/ppermute | solution.py:303
  7.7 1.0 %collective-permute-start.2 = (bf16[384,512]{1,0:T(8,128)(2,1)S(1)}, bf16[384,512]{1,0:T(8,128)(2,1)S(1)}, u32[]{:S(2)}, u32[]{:S(2)}) collective-permute-start(bf16[384,512]{1,0:T(8,128)(2,1)S(1)} %get-tuple-element.37), channel_id=1, source_target_pairs={{34,0},{121,1},{36,2},{123,3},{38,4},{125,5},{32,6},{127,7},{42,8}... | collective-permute-start | bytes 1179656 | tf_op jit(solution)/shard_map/ppermute | solution.py:303
  8.7 1.3 %shard_map.30 = (f32[12,768]{1,0:T(8,128)S(1)}, f32[8,768]{1,0:T(8,128)S(1)}) custom-call(s32[1]{0:T(128)S(6)} %copy.3.refs_0_, bf16[768,512]{1,0:T(8,128)(2,1)S(1)} %get-tuple-element.33.refs_1_), custom_call_target="tpu_custom_call" | custom-call | flops 4831838208 | bytes 1536 | tf_op jit(solution)/shard_map/pallas_call | solution.py:258
  10.0 3.1 %collective-permute-done.refs_2_.refs_1_ = bf16[384,512]{1,0:T(8,128)(2,1)S(1)} collective-permute-done((bf16[384,512]{1,0:T(8,128)(2,1)S(1)}, bf16[384,512]{1,0:T(8,128)(2,1)S(1)}, u32[]{:S(2)}, u32[]{:S(2)}) %collective-permute-start) | collective-permute-done | bytes 393248 | tf_op jit(solution)/shard_map/ppermute | solution.py:303
  13.1 3.6 %collective-permute-start.8 = (bf16[384,512]{1,0:T(8,128)(2,1)S(1)}, bf16[384,512]{1,0:T(8,128)(2,1)S(1)}, u32[]{:S(2)}, u32[]{:S(2)}) collective-permute-start(bf16[384,512]{1,0:T(8,128)(2,1)S(1)} %collective-permute-done.refs_2_.refs_1_), channel_id=1, source_target_pairs={{0,1},{1,0},{2,3},{3,2},{4,5},{5,4},{6,7},{7,6},{8,9},{9,8},{10,11... | collective-permute-start | bytes 1179656 | tf_op jit(solution)/shard_map/ppermute | solution.py:306
  16.7 1.0 %collective-permute-done.2.refs_3_.refs_2_ = bf16[384,512]{1,0:T(8,128)(2,1)S(1)} collective-permute-done((bf16[384,512]{1,0:T(8,128)(2,1)S(1)}, bf16[384,512]{1,0:T(8,128)(2,1)S(1)}, u32[]{:S(2)}, u32[]{:S(2)}) %collective-permute-start.2) | collective-permute-done | bytes 393248 | tf_op jit(solution)/shard_map/ppermute | solution.py:303
  17.8 2.9 %collective-permute-start.9 = (bf16[384,512]{1,0:T(8,128)(2,1)S(1)}, bf16[384,512]{1,0:T(8,128)(2,1)S(1)}, u32[]{:S(2)}, u32[]{:S(2)}) collective-permute-start(bf16[384,512]{1,0:T(8,128)(2,1)S(1)} %collective-permute-done.2.refs_3_.refs_2_), channel_id=1, source_target_pairs={{0,1},{1,0},{2,3},{3,2},{4,5},{5,4},{6,7},{7,6},{8,9},{9,8},{10,11... | collective-permute-start | bytes 1179656 | tf_op jit(solution)/shard_map/ppermute | solution.py:306
  20.7 1.5 %collective-permute-start.6 = (bf16[768,512]{1,0:T(8,128)(2,1)S(1)}, bf16[768,512]{1,0:T(8,128)(2,1)S(1)}, u32[]{:S(2)}, u32[]{:S(2)}) collective-permute-start(bf16[768,512]{1,0:T(8,128)(2,1)S(1)} %collective-permute-done.4.refs_4_), channel_id=1, source_target_pairs={{6,0},{17,1},{0,2},{19,3},{2,4},{21,5},{4,6},{23,7},{14,8},{25,9},... | collective-permute-start | bytes 2359304 | tf_op jit(solution)/shard_map/ppermute | solution.py:303
  22.2 2.0 %collective-permute-start.10 = (bf16[768,512]{1,0:T(8,128)(2,1)S(1)}, bf16[768,512]{1,0:T(8,128)(2,1)S(1)}, u32[]{:S(2)}, u32[]{:S(2)}) collective-permute-start(bf16[768,512]{1,0:T(8,128)(2,1)S(1)} %collective-permute-done.4.refs_4_), channel_id=1, source_target_pairs={{0,1},{1,0},{2,3},{3,2},{4,5},{5,4},{6,7},{7,6},{8,9},{9,8},{10,11... | collective-permute-start | bytes 2359304 | tf_op jit(solution)/shard_map/ppermute | solution.py:306
  24.2 3.1 %shard_map.31 = (f32[12,768]{1,0:T(8,128)S(1)}, f32[8,768]{1,0:T(8,128)S(1)}) custom-call(s32[1]{0:T(128)S(6)} %copy.3.refs_0_, bf16[768,512]{1,0:T(8,128)(2,1)S(1)} %get-tuple-element.33.refs_1_, bf16[384,512]{1,0:T(8,128)(2,1)S(1)} %collective-permute-done.refs_2_.refs_1_, bf16[384,512]{1,0:T(8,128)(2,1)S(1)} %collective-permute-done.2.refs_3_.refs_2_, ...), custom_call_target="tpu_custom_call" | custom-call | flops 14495514624 | bytes 4608 | tf_op jit(solution)/shard_map/pallas_call | solution.py:258
  28.0 2.3 %collective-permute-start.12 = (bf16[384,512]{1,0:T(8,128)(2,1)S(1)}, bf16[384,512]{1,0:T(8,128)(2,1)S(1)}, u32[]{:S(2)}, u32[]{:S(2)}) collective-permute-start(bf16[384,512]{1,0:T(8,128)(2,1)S(1)} %collective-permute-done.3.refs_5_.refs_3_), channel_id=1, source_target_pairs={{0,1},{1,0},{2,3},{3,2},{4,5},{5,4},{6,7},{7,6},{8,9},{9,8},{10,11... | collective-permute-start | bytes 1179656 | tf_op jit(solution)/shard_map/ppermute | solution.py:306
  30.3 1.1 %collective-permute-start.11 = (bf16[384,512]{1,0:T(8,128)(2,1)S(1)}, bf16[384,512]{1,0:T(8,128)(2,1)S(1)}, u32[]{:S(2)}, u32[]{:S(2)}) collective-permute-start(bf16[384,512]{1,0:T(8,128)(2,1)S(1)} %collective-permute-done.5.refs_6_.refs_4_), channel_id=1, source_target_pairs={{2,0},{25,1},{4,2},{27,3},{6,4},{29,5},{0,6},{31,7},{10,8},{17,9},... | collective-permute-start | bytes 1179656 | tf_op jit(solution)/shard_map/ppermute | solution.py:303
  31.9 5.0 %collective-permute-start.13 = (bf16[384,512]{1,0:T(8,128)(2,1)S(1)}, bf16[384,512]{1,0:T(8,128)(2,1)S(1)}, u32[]{:S(2)}, u32[]{:S(2)}) collective-permute-start(bf16[384,512]{1,0:T(8,128)(2,1)S(1)} %collective-permute-done.5.refs_6_.refs_4_), channel_id=1, source_target_pairs={{0,1},{1,0},{2,3},{3,2},{4,5},{5,4},{6,7},{7,6},{8,9},{9,8},{10,11... | collective-permute-start | bytes 1179656 | tf_op jit(solution)/shard_map/ppermute | solution.py:306
  36.9 8.5 %shard_map.32 = (f32[12,768]{1,0:T(8,128)S(1)}, f32[8,768]{1,0:T(8,128)S(1)}) custom-call(s32[1]{0:T(128)S(6)} %copy.3.refs_0_, bf16[768,512]{1,0:T(8,128)(2,1)S(1)} %get-tuple-element.33.refs_1_, bf16[384,512]{1,0:T(8,128)(2,1)S(1)} %collective-permute-done.refs_2_.refs_1_, bf16[384,512]{1,0:T(8,128)(2,1)S(1)} %collective-permute-done.2.refs_3_.refs_2_, ...), custom_call_target="tpu_custom_call" | custom-call | flops 48318382080 | bytes 10752 | tf_op jit(solution)/shard_map/pallas_call | solution.py:258
  45.4 7.5 %shard_map.33 = (f32[2,768]{1,0:T(2,128)S(1)}, f32[2,768]{1,0:T(2,128)S(1)}, f32[2,768]{1,0:T(2,128)S(1)}, f32[2,768]{1,0:T(2,128)S(1)}, f32[2,768]{1,0:T(2,128)...) custom-call(s32[1]{0:T(128)S(6)} %copy.3.refs_0_, bf16[384,512]{1,0:T(8,128)(2,1)S(1)} %collective-permute-done.refs_2_.refs_1_, ...), custom_call_target="tpu_custom_call" | custom-call | flops 4831838208 | bytes 12288 | tf_op jit(solution)/shard_map/pallas_call | solution.py:258
  53.3 2.8 %collective-permute-start.15 = (f32[2,768]{1,0:T(2,128)S(1)}, f32[2,768]{1,0:T(2,128)S(1)}, u32[]{:S(2)}, u32[]{:S(2)}) collective-permute-start(f32[2,768]{1,0:T(2,128)S(1)} %get-tuple-element.51), channel_id=1, source_target_pairs={{116,0},{73,1},{118,2},{75,3},{112,4},{77,5},{114,6},{79,7},{124,8... | collective-permute-start | bytes 18440 | tf_op jit(solution)/shard_map/ppermute | solution.py:333
  56.2 0.8 %collective-permute-start.17 = (f32[2,768]{1,0:T(2,128)S(1)}, f32[2,768]{1,0:T(2,128)S(1)}, u32[]{:S(2)}, u32[]{:S(2)}) collective-permute-start(f32[2,768]{1,0:T(2,128)S(1)} %get-tuple-element.57), channel_id=1, source_target_pairs={{4,0},{9,1},{6,2},{11,3},{0,4},{13,5},{2,6},{15,7},{12,8},{1,9},{1... | collective-permute-start | bytes 18440 | tf_op jit(solution)/shard_map/ppermute | solution.py:333
  57.0 4.2 %collective-permute-start.18 = (f32[2,768]{1,0:T(2,128)S(1)}, f32[2,768]{1,0:T(2,128)S(1)}, u32[]{:S(2)}, u32[]{:S(2)}) collective-permute-start(f32[2,768]{1,0:T(2,128)S(1)} %get-tuple-element.58), channel_id=1, source_target_pairs={{118,0},{81,1},{112,2},{83,3},{114,4},{85,5},{116,6},{87,7},{126,8... | collective-permute-start | bytes 18440 | tf_op jit(solution)/shard_map/ppermute | solution.py:333
  62.0 1.0 %collective-permute-start.20 = (f32[2,768]{1,0:T(2,128)S(1)}, f32[2,768]{1,0:T(2,128)S(1)}, u32[]{:S(2)}, u32[]{:S(2)}) collective-permute-start(f32[2,768]{1,0:T(2,128)S(1)} %get-tuple-element.60), channel_id=1, source_target_pairs={{2,0},{25,1},{4,2},{27,3},{6,4},{29,5},{0,6},{31,7},{10,8},{17,9},... | collective-permute-start | bytes 18440 | tf_op jit(solution)/shard_map/ppermute | solution.py:333
  63.0 1.9 %collective-permute-done.19 = f32[2,768]{1,0:T(2,128)S(1)} collective-permute-done((f32[2,768]{1,0:T(2,128)S(1)}, f32[2,768]{1,0:T(2,128)S(1)}, u32[]{:S(2)}, u32[]{:S(2)}) %collective-permute-start.19) | collective-permute-done | bytes 6176 | tf_op jit(solution)/shard_map/ppermute | solution.py:333
  65.8 1.2 %collective-permute-done.21 = f32[2,768]{1,0:T(2,128)S(1)} collective-permute-done((f32[2,768]{1,0:T(2,128)S(1)}, f32[2,768]{1,0:T(2,128)S(1)}, u32[]{:S(2)}, u32[]{:S(2)}) %collective-permute-start.21) | collective-permute-done | bytes 6176 | tf_op jit(solution)/shard_map/ppermute | solution.py:346
  (31 shorter events, 4.6 us)
Async XLA Ops:
  0.0 5.9 %collective-permute-start.1 = (f32[384,512]{1,0:T(8,128)}, f32[384,512]{1,0:T(8,128)S(1)}, u32[]{:S(2)}, u32[]{:S(2)}) collective-permute-start(f32[384,512]{1,0:T(8,128)} %x_ref.1), channel_id=1, source_target_pairs={{0,1},{1,0},{2,3},{3,2},{4,5},{5,4},{6,7},{7,6},{8,9},{9,8},{10,11... | collective-permute-start | bytes 2359304 | tf_op jit(solution)/shard_map/ppermute | solution.py:278
  1.4 1.1 %copy-start = (f32[384,512]{1,0:T(8,128)S(1)}, f32[384,512]{1,0:T(8,128)}, u32[]{:S(2)}) copy-start(f32[384,512]{1,0:T(8,128)} %x_ref.1) | copy-start | bytes 2359300
  2.8 10.2 %collective-permute-start = (bf16[384,512]{1,0:T(8,128)(2,1)S(1)}, bf16[384,512]{1,0:T(8,128)(2,1)S(1)}, u32[]{:S(2)}, u32[]{:S(2)}) collective-permute-start(bf16[384,512]{1,0:T(8,128)(2,1)S(1)} %shard_map.28.own_ref), channel_id=1, source_target_pairs={{34,0},{121,1},{36,2},{123,3},{38,4},{125,5},{32,6},{127,7},{42,8}... | collective-permute-start | bytes 1179656 | tf_op jit(solution)/shard_map/ppermute | solution.py:303
  6.1 14.6 %collective-permute-start.4 = (bf16[768,512]{1,0:T(8,128)(2,1)S(1)}, bf16[768,512]{1,0:T(8,128)(2,1)S(1)}, u32[]{:S(2)}, u32[]{:S(2)}) collective-permute-start(bf16[768,512]{1,0:T(8,128)(2,1)S(1)} %get-tuple-element.33.refs_1_), channel_id=1, source_target_pairs={{6,0},{17,1},{0,2},{19,3},{2,4},{21,5},{4,6},{23,7},{14,8},{25,9},... | collective-permute-start | bytes 2359304 | tf_op jit(solution)/shard_map/ppermute | solution.py:303
  7.7 10.0 %collective-permute-start.2 = (bf16[384,512]{1,0:T(8,128)(2,1)S(1)}, bf16[384,512]{1,0:T(8,128)(2,1)S(1)}, u32[]{:S(2)}, u32[]{:S(2)}) collective-permute-start(bf16[384,512]{1,0:T(8,128)(2,1)S(1)} %get-tuple-element.37), channel_id=1, source_target_pairs={{34,0},{121,1},{36,2},{123,3},{38,4},{125,5},{32,6},{127,7},{42,8}... | collective-permute-start | bytes 1179656 | tf_op jit(solution)/shard_map/ppermute | solution.py:303
  13.1 9.1 %collective-permute-start.3 = (bf16[384,512]{1,0:T(8,128)(2,1)S(1)}, bf16[384,512]{1,0:T(8,128)(2,1)S(1)}, u32[]{:S(2)}, u32[]{:S(2)}) collective-permute-start(bf16[384,512]{1,0:T(8,128)(2,1)S(1)} %collective-permute-done.refs_2_.refs_1_), channel_id=1, source_target_pairs={{24,0},{97,1},{26,2},{99,3},{28,4},{101,5},{30,6},{103,7},{16,8},{... | collective-permute-start | bytes 1179656 | tf_op jit(solution)/shard_map/ppermute | solution.py:303
  13.1 14.2 %collective-permute-start.8 = (bf16[384,512]{1,0:T(8,128)(2,1)S(1)}, bf16[384,512]{1,0:T(8,128)(2,1)S(1)}, u32[]{:S(2)}, u32[]{:S(2)}) collective-permute-start(bf16[384,512]{1,0:T(8,128)(2,1)S(1)} %collective-permute-done.refs_2_.refs_1_), channel_id=1, source_target_pairs={{0,1},{1,0},{2,3},{3,2},{4,5},{5,4},{6,7},{7,6},{8,9},{9,8},{10,11... | collective-permute-start | bytes 1179656 | tf_op jit(solution)/shard_map/ppermute | solution.py:306
  17.7 10.3 %collective-permute-start.5 = (bf16[384,512]{1,0:T(8,128)(2,1)S(1)}, bf16[384,512]{1,0:T(8,128)(2,1)S(1)}, u32[]{:S(2)}, u32[]{:S(2)}) collective-permute-start(bf16[384,512]{1,0:T(8,128)(2,1)S(1)} %collective-permute-done.2.refs_3_.refs_2_), channel_id=1, source_target_pairs={{24,0},{97,1},{26,2},{99,3},{28,4},{101,5},{30,6},{103,7},{16,8},{... | collective-permute-start | bytes 1179656 | tf_op jit(solution)/shard_map/ppermute | solution.py:303
  17.8 12.5 %collective-permute-start.9 = (bf16[384,512]{1,0:T(8,128)(2,1)S(1)}, bf16[384,512]{1,0:T(8,128)(2,1)S(1)}, u32[]{:S(2)}, u32[]{:S(2)}) collective-permute-start(bf16[384,512]{1,0:T(8,128)(2,1)S(1)} %collective-permute-done.2.refs_3_.refs_2_), channel_id=1, source_target_pairs={{0,1},{1,0},{2,3},{3,2},{4,5},{5,4},{6,7},{7,6},{8,9},{9,8},{10,11... | collective-permute-start | bytes 1179656 | tf_op jit(solution)/shard_map/ppermute | solution.py:306
  20.7 11.1 %collective-permute-start.6 = (bf16[768,512]{1,0:T(8,128)(2,1)S(1)}, bf16[768,512]{1,0:T(8,128)(2,1)S(1)}, u32[]{:S(2)}, u32[]{:S(2)}) collective-permute-start(bf16[768,512]{1,0:T(8,128)(2,1)S(1)} %collective-permute-done.4.refs_4_), channel_id=1, source_target_pairs={{6,0},{17,1},{0,2},{19,3},{2,4},{21,5},{4,6},{23,7},{14,8},{25,9},... | collective-permute-start | bytes 2359304 | tf_op jit(solution)/shard_map/ppermute | solution.py:303
  22.2 14.7 %collective-permute-start.10 = (bf16[768,512]{1,0:T(8,128)(2,1)S(1)}, bf16[768,512]{1,0:T(8,128)(2,1)S(1)}, u32[]{:S(2)}, u32[]{:S(2)}) collective-permute-start(bf16[768,512]{1,0:T(8,128)(2,1)S(1)} %collective-permute-done.4.refs_4_), channel_id=1, source_target_pairs={{0,1},{1,0},{2,3},{3,2},{4,5},{5,4},{6,7},{7,6},{8,9},{9,8},{10,11... | collective-permute-start | bytes 2359304 | tf_op jit(solution)/shard_map/ppermute | solution.py:306
  27.3 18.0 %collective-permute-start.7 = (bf16[384,512]{1,0:T(8,128)(2,1)S(1)}, bf16[384,512]{1,0:T(8,128)(2,1)S(1)}, u32[]{:S(2)}, u32[]{:S(2)}) collective-permute-start(bf16[384,512]{1,0:T(8,128)(2,1)S(1)} %collective-permute-done.3.refs_5_.refs_3_), channel_id=1, source_target_pairs={{2,0},{25,1},{4,2},{27,3},{6,4},{29,5},{0,6},{31,7},{10,8},{17,9},... | collective-permute-start | bytes 1179656 | tf_op jit(solution)/shard_map/ppermute | solution.py:303
  28.0 17.3 %collective-permute-start.12 = (bf16[384,512]{1,0:T(8,128)(2,1)S(1)}, bf16[384,512]{1,0:T(8,128)(2,1)S(1)}, u32[]{:S(2)}, u32[]{:S(2)}) collective-permute-start(bf16[384,512]{1,0:T(8,128)(2,1)S(1)} %collective-permute-done.3.refs_5_.refs_3_), channel_id=1, source_target_pairs={{0,1},{1,0},{2,3},{3,2},{4,5},{5,4},{6,7},{7,6},{8,9},{9,8},{10,11... | collective-permute-start | bytes 1179656 | tf_op jit(solution)/shard_map/ppermute | solution.py:306
  30.3 15.0 %collective-permute-start.11 = (bf16[384,512]{1,0:T(8,128)(2,1)S(1)}, bf16[384,512]{1,0:T(8,128)(2,1)S(1)}, u32[]{:S(2)}, u32[]{:S(2)}) collective-permute-start(bf16[384,512]{1,0:T(8,128)(2,1)S(1)} %collective-permute-done.5.refs_6_.refs_4_), channel_id=1, source_target_pairs={{2,0},{25,1},{4,2},{27,3},{6,4},{29,5},{0,6},{31,7},{10,8},{17,9},... | collective-permute-start | bytes 1179656 | tf_op jit(solution)/shard_map/ppermute | solution.py:303
  31.9 13.5 %collective-permute-start.13 = (bf16[384,512]{1,0:T(8,128)(2,1)S(1)}, bf16[384,512]{1,0:T(8,128)(2,1)S(1)}, u32[]{:S(2)}, u32[]{:S(2)}) collective-permute-start(bf16[384,512]{1,0:T(8,128)(2,1)S(1)} %collective-permute-done.5.refs_6_.refs_4_), channel_id=1, source_target_pairs={{0,1},{1,0},{2,3},{3,2},{4,5},{5,4},{6,7},{7,6},{8,9},{9,8},{10,11... | collective-permute-start | bytes 1179656 | tf_op jit(solution)/shard_map/ppermute | solution.py:306
  36.9 8.5 %collective-permute-start.14 = (bf16[768,512]{1,0:T(8,128)(2,1)S(1)}, bf16[768,512]{1,0:T(8,128)(2,1)S(1)}, u32[]{:S(2)}, u32[]{:S(2)}) collective-permute-start(bf16[768,512]{1,0:T(8,128)(2,1)S(1)} %collective-permute-done.6.refs_7_.refs_5_), channel_id=1, source_target_pairs={{0,1},{1,0},{2,3},{3,2},{4,5},{5,4},{6,7},{7,6},{8,9},{9,8},{10,11... | collective-permute-start | bytes 2359304 | tf_op jit(solution)/shard_map/ppermute | solution.py:306
  52.9 3.3 %collective-permute-start.16 = (f32[8,768]{1,0:T(8,128)S(1)}, f32[8,768]{1,0:T(8,128)S(1)}, u32[]{:S(2)}, u32[]{:S(2)}) collective-permute-start(f32[8,768]{1,0:T(8,128)S(1)} %get-tuple-element.56), channel_id=1, source_target_pairs={{0,1},{1,0},{2,3},{3,2},{4,5},{5,4},{6,7},{7,6},{8,9},{9,8},{10,11... | collective-permute-start | bytes 73736 | tf_op jit(solution)/shard_map/ppermute | solution.py:335
  53.3 9.6 %collective-permute-start.15 = (f32[2,768]{1,0:T(2,128)S(1)}, f32[2,768]{1,0:T(2,128)S(1)}, u32[]{:S(2)}, u32[]{:S(2)}) collective-permute-start(f32[2,768]{1,0:T(2,128)S(1)} %get-tuple-element.51), channel_id=1, source_target_pairs={{116,0},{73,1},{118,2},{75,3},{112,4},{77,5},{114,6},{79,7},{124,8... | collective-permute-start | bytes 18440 | tf_op jit(solution)/shard_map/ppermute | solution.py:333
  56.2 6.8 %collective-permute-start.17 = (f32[2,768]{1,0:T(2,128)S(1)}, f32[2,768]{1,0:T(2,128)S(1)}, u32[]{:S(2)}, u32[]{:S(2)}) collective-permute-start(f32[2,768]{1,0:T(2,128)S(1)} %get-tuple-element.57), channel_id=1, source_target_pairs={{4,0},{9,1},{6,2},{11,3},{0,4},{13,5},{2,6},{15,7},{12,8},{1,9},{1... | collective-permute-start | bytes 18440 | tf_op jit(solution)/shard_map/ppermute | solution.py:333
  57.0 6.0 %collective-permute-start.18 = (f32[2,768]{1,0:T(2,128)S(1)}, f32[2,768]{1,0:T(2,128)S(1)}, u32[]{:S(2)}, u32[]{:S(2)}) collective-permute-start(f32[2,768]{1,0:T(2,128)S(1)} %get-tuple-element.58), channel_id=1, source_target_pairs={{118,0},{81,1},{112,2},{83,3},{114,4},{85,5},{116,6},{87,7},{126,8... | collective-permute-start | bytes 18440 | tf_op jit(solution)/shard_map/ppermute | solution.py:333
  61.2 3.7 %collective-permute-start.19 = (f32[2,768]{1,0:T(2,128)S(1)}, f32[2,768]{1,0:T(2,128)S(1)}, u32[]{:S(2)}, u32[]{:S(2)}) collective-permute-start(f32[2,768]{1,0:T(2,128)S(1)} %get-tuple-element.59), channel_id=1, source_target_pairs={{102,0},{49,1},{96,2},{51,3},{98,4},{53,5},{100,6},{55,7},{110,8},... | collective-permute-start | bytes 18440 | tf_op jit(solution)/shard_map/ppermute | solution.py:333
  62.0 3.7 %collective-permute-start.20 = (f32[2,768]{1,0:T(2,128)S(1)}, f32[2,768]{1,0:T(2,128)S(1)}, u32[]{:S(2)}, u32[]{:S(2)}) collective-permute-start(f32[2,768]{1,0:T(2,128)S(1)} %get-tuple-element.60), channel_id=1, source_target_pairs={{2,0},{25,1},{4,2},{27,3},{6,4},{29,5},{0,6},{31,7},{10,8},{17,9},... | collective-permute-start | bytes 18440 | tf_op jit(solution)/shard_map/ppermute | solution.py:333
  65.7 1.2 %collective-permute-start.21 = (f32[2,768]{1,0:T(2,128)S(1)}, f32[2,768]{1,0:T(2,128)S(1)}, u32[]{:S(2)}, u32[]{:S(2)}) collective-permute-start(f32[2,768]{1,0:T(2,128)S(1)} %maximum_maximum_fusion), channel_id=1, source_target_pairs={{0,1},{1,0},{2,3},{3,2},{4,5},{5,4},{6,7},{7,6},{8,9},{9,8},{10,11... | collective-permute-start | bytes 18440 | tf_op jit(solution)/shard_map/ppermute | solution.py:346
